TPU v7x, 512 devices: a whole 4x8x8 slice. The times are simulated.
512 devices in a mesh: gx: 8 (over z), gy: 16 (over x, y_lo), gz: 4 (over y_hi, core).
Axes of the slice: x: 4, y: 8 (y_hi: 2, y_lo: 4; y = y_hi * 4 + y_lo), z: 8, core: 2. Of those that a mesh axis runs over, the one named last changes fastest.
Arguments:
- density: float32 [128, 512, 1024], P('gz', 'gy', 'gx'), may hold values from -10 to 10
Outputs:
- potential: float32 [128, 512, 1024], P('gz', 'gy', 'gx')
All inputs are finite; a program needn't handle non-finite values.
Results may differ from a plain program's by a relative error of at most 0.0003.
Values sent between devices are 32-bit elements; how exact they have to be, the bound alone decides.
No kernel may reach another device: no remote copies, remote signals or barrier semaphores. Data moves between devices by JAX's collectives and lax.ppermute only.
A program may use at most 64 MiB of HBM per device.

v0:
```python
import math

import jax
import jax.numpy as jnp
from jax import lax
from jax.sharding import PartitionSpec as P

PATCH = 32
HALO = 8
COARSEN = 4


screen = 6.0
soften = 0.25


def padded_2(x, sides, width):
    for axis, dim in sides:
        peers, length = (lax.axis_size(axis), x.shape[dim])
        up = [(i, (i + 1) % peers) for i in range(peers)]
        down = [(j, i) for i, j in up]
        last = lax.slice_in_dim(x, length - width, length, axis=dim)
        leading = lax.slice_in_dim(x, 0, width, axis=dim)
        before = lax.ppermute(last, axis, up)
        after = lax.ppermute(leading, axis, down)
        x = jnp.concatenate([before, x, after], axis=dim)
    return x


def contract(pattern, former, latter):
    return jnp.einsum(pattern, former, latter, precision=lax.Precision.HIGHEST)


def indices(points):
    return jnp.arange(points, dtype=jnp.int32)


def kernel_value(shift_z, shift_y, shift_x):
    squared = (shift_z * shift_z + shift_y * shift_y + shift_x * shift_x).astype(jnp.float32)
    return jax.scipy.special.erfc(jnp.sqrt(squared) / screen) / (
        4.0 * math.pi * jnp.sqrt(squared + soften)
    )


def window_kernel(length):
    offset = (indices(length) + length // 2) % length - length // 2
    within = (jnp.abs(offset) <= HALO).astype(jnp.float32)
    values = kernel_value(offset[:, None, None], offset[None, :, None], offset[None, None, :])
    return values * within[:, None, None] * within[None, :, None] * within[None, None, :]


def hartley(out_index, in_index, points):
    product = out_index[:, None] * in_index[None, :] % points
    angles = 2.0 * math.pi / points * product.astype(jnp.float32)
    return jnp.cos(angles) + jnp.sin(angles)


def axis_terms(index_list, points):
    signed = (index_list + points // 2) % points - points // 2
    laplace = 2.0 - 2.0 * jnp.cos(2.0 * math.pi / points * index_list.astype(jnp.float32))
    wave = 2.0 * math.pi / (points * COARSEN) * signed.astype(jnp.float32)
    return (laplace, wave * wave, index_list == 0)


def multiplier(index_z, index_y, index_x, points_z, points_y, points_x):
    laplace_z, wave_z, anchor_z = axis_terms(index_z, points_z)
    laplace_y, wave_y, anchor_y = axis_terms(index_y, points_y)
    laplace_x, wave_x, anchor_x = axis_terms(index_x, points_x)
    laplace = laplace_z[:, None, None] + laplace_y[None, :, None] + laplace_x[None, None, :]
    wave_sq = wave_z[:, None, None] + wave_y[None, :, None] + wave_x[None, None, :]
    at_anchor = (
        anchor_z[:, None, None] & anchor_y[None, :, None] & anchor_x[None, None, :]
    ).astype(jnp.float32)
    return (
        (1.0 - at_anchor)
        * jnp.exp(-(screen * screen / 4.0) * wave_sq)
        / (COARSEN * (laplace + at_anchor))
    )


def interp_matrix(points):
    fine_index = indices(COARSEN * points)
    below_index = fine_index // COARSEN
    offset = ((fine_index % COARSEN).astype(jnp.float32) + 0.5) / COARSEN - 0.5
    column = indices(points + 2)[None, :]
    centre = jnp.where(column == (below_index + 1)[:, None], 1.0 - jnp.abs(offset)[:, None], 0.0)
    lower_side = jnp.where(
        (column == below_index[:, None]) & (offset < 0.0)[:, None], -offset[:, None], 0.0
    )
    upper_side = jnp.where(
        (column == (below_index + 2)[:, None]) & (offset > 0.0)[:, None], offset[:, None], 0.0
    )
    return centre + lower_side + upper_side


def short_range(padded, cells_z, cells_y, cells_x):
    length = PATCH + 2 * HALO
    every_index = indices(length)
    square = hartley(every_index, every_index, length)
    narrow = hartley(HALO + indices(PATCH), every_index, length)
    spectral = contract("abc,ma->mbc", window_kernel(length), square)
    spectral = contract("mbc,lb->mlc", spectral, square)
    spectral = contract("mlc,kc->mlk", spectral, square) * (1.0 / length**3)
    count_y, count_x = (cells_y // PATCH, cells_x // PATCH)

    def one_slab(row_index):
        rows = jnp.stack([padded], axis=1)
        levels = jnp.stack(
            [rows[..., band * PATCH : band * PATCH + length] for band in range(count_x)], axis=3
        )
        levels = contract("zqjpi,ki->zqjpk", levels, square)
        levels = contract("zqjpk,lj->zqlpk", levels, square)
        levels = contract("zqlpk,mz->mqlpk", levels, square)
        levels = levels * spectral[:, None, :, None, :]
        levels = contract("mqlpk,zm->zqlpk", levels, narrow)
        levels = contract("zqlpk,jl->zqjpk", levels, narrow)
        levels = contract("zqjpk,ik->zqjpi", levels, narrow)
        return levels.reshape(PATCH, cells_y, cells_x)

    solved = lax.map(one_slab, indices(cells_z // PATCH))
    return solved.reshape(cells_z, cells_y, cells_x)


def body(density):
    cells_z, cells_y, cells_x = density.shape
    block_z, block_y, block_x = (cells_z // COARSEN, cells_y // COARSEN, cells_x // COARSEN)
    charges = density.reshape(block_z, COARSEN, block_y, COARSEN, block_x, COARSEN).sum(
        axis=(1, 3, 5)
    )
    parts_x, parts_y, parts_z = (lax.axis_size("gx"), lax.axis_size("gy"), lax.axis_size("gz"))
    place_x, place_y, place_z = (lax.axis_index("gx"), lax.axis_index("gy"), lax.axis_index("gz"))
    full_x, full_y, full_z = (block_x * parts_x, block_y * parts_y, block_z * parts_z)
    normalise = 1.0 / (full_x * full_y * full_z)
    every_x, every_y, every_z = (indices(full_x), indices(full_y), indices(full_z))
    table_x = hartley(every_x, every_x, full_x)
    table_z = hartley(every_z, every_z, full_z)
    gathered = lax.all_gather(charges, "gy", axis=1, tiled=True)
    spectrum = contract("zyx,ky->zkx", gathered, hartley(every_y, every_y, full_y))
    spectrum = lax.all_to_all(
        lax.all_to_all(spectrum, "gx", split_axis=1, concat_axis=2, tiled=True),
        "gz",
        split_axis=1,
        concat_axis=0,
        tiled=True,
    )
    piece_y = full_y // (parts_x * parts_z)
    freq_y = place_x * (full_y // parts_x) + place_z * piece_y + indices(piece_y)
    spectrum = contract("zkx,mz->mkx", spectrum, table_z)
    spectrum = contract("mkx,jx->mkj", spectrum, table_x)
    spectrum = spectrum * (normalise * multiplier(every_z, freq_y, every_x, full_z, full_y, full_x))
    spectrum = contract("mkx,zm->zkx", spectrum, table_z)
    spectrum = contract("zkj,xj->zkx", spectrum, table_x)
    spectrum = lax.all_to_all(
        lax.all_to_all(spectrum, "gx", split_axis=2, concat_axis=1, tiled=True),
        "gz",
        split_axis=0,
        concat_axis=1,
        tiled=True,
    )
    from_z = every_y // (parts_x * piece_y)
    from_x = every_y // piece_y % parts_x
    within = every_y % piece_y
    sent_y = from_x * (full_y // parts_x) + from_z * piece_y + within
    own_y = place_y * block_y + indices(block_y)
    coarse_field = contract("zkx,yk->zyx", spectrum, hartley(own_y, sent_y, full_y))
    bordered = padded_2(coarse_field, (("gx", 2), ("gy", 1), ("gz", 0)), 1)
    far_field = contract("abc,xc->abx", bordered, interp_matrix(block_x))
    far_field = contract("abx,yb->ayx", far_field, interp_matrix(block_y))
    far_field = contract("ayx,za->zyx", far_field, interp_matrix(block_z))
    padded = padded_2(density, (("gx", 2), ("gy", 1), ("gz", 0)), HALO)
    near_field = short_range(padded, cells_z, cells_y, cells_x)
    return far_field + near_field


def solution(mesh):
    placed = (P("gz", "gy", "gx"),)
    return jax.shard_map(
        body, mesh=mesh, in_specs=placed, out_specs=P("gz", "gy", "gx"), check_vma=False
    )
```

profile of v0, /device:TPU:1, one launch (start us, length us, event | category | flops | bytes accessed | tf_op | source)
XLA Modules:
  0.0 251.3 jit_solution(17138837231144621772)
XLA Ops:
  0.0 19.4 %reshape.455 = f32[8,4,8,4,32,4]{5,4,3,2,1,0:T(8,128)} reshape(f32[32,32,128]{2,1,0:T(8,128)} %param.1) | data formatting | bytes 1048576 | tf_op jit(solution)/shard_map/reshape | solution.py:127
  19.4 7.1 %reduce_sum.9 = f32[8,8,32]{2,1,0:T(8,128)S(1)} reduce(f32[8,4,8,4,32,4]{5,4,3,2,1,0:T(8,128)} %reshape.455, f32[]{:T(128)} %constant.287.clone.1), dimensions={1,3,5}, to_apply=%region_0.0 | reduce | flops 129024 | bytes 532484 | tf_op jit(solution)/shard_map/reduce_sum | solution.py:127
  26.5 41.4 %all_gather.3 = f32[8,128,32]{2,1,0:T(8,128)S(1)} all-gather(f32[8,8,32]{2,1,0:T(8,128)S(1)} %reduce_sum.9), channel_id=1, replica_groups=mesh['gx'=8,'gy'=16,'gz'=4] {'gy'}, dimensions={1}, use_global_device_ids=true | all-gather | bytes 139264 | tf_op jit(solution)/shard_map/all_gather | solution.py:137
  67.9 1.0 convolution_bitcast_fusion.3
  69.1 0.9 reshape.470
  70.0 9.3 %all-to-all-start = ((f32[8,1,4096]{2,1,0:T(1,128)}), f32[8,1,4096]{2,1,0:T(1,128)S(1)}, u32[]{:S(2)}, u32[]{:S(2)}) async-start(f32[8,1,4096]{2,1,0:T(1,128)} %reshape.470), calls=%async_computation | async-start | bytes 262144 | tf_op jit(solution)/shard_map/all_to_all | solution.py:140
  79.4 1.1 fusion.320
  80.5 3.4 %collective-permute-start.6 = (f32[32,32,8]{2,1,0:T(8,128)}, f32[32,32,8]{2,1,0:T(8,128)S(1)}, u32[]{:S(2)}, u32[]{:S(2)}) collective-permute-start(f32[32,32,8]{2,1,0:T(8,128)} %get-tuple-element.31), channel_id=1, source_target_pairs={{0,64},{64,128},{128,192},{192,256},{256,320},{320,384},{384,448},... | collective-permute-start | bytes 98312 | tf_op jit(solution)/shard_map/ppermute | solution.py:24
  83.8 3.7 %collective-permute-start.7 = (f32[32,32,8]{2,1,0:T(8,128)}, f32[32,32,8]{2,1,0:T(8,128)}, u32[]{:S(2)}, u32[]{:S(2)}) collective-permute-start(f32[32,32,8]{2,1,0:T(8,128)} %get-tuple-element.32), channel_id=1, source_target_pairs={{64,0},{128,64},{192,128},{256,192},{320,256},{384,320},{448,384},... | collective-permute-start | bytes 98312 | tf_op jit(solution)/shard_map/ppermute | solution.py:25
  96.0 4.9 %fusion.32 = f32[48,48,48]{2,0,1:T(8,128)S(1)} fusion(f32[48]{0:T(128)S(1)} %compare_convert_fusion, s32[48]{0:T(128)S(1)} %fusion.230, s32[48,48]{0,1:T(8,128)S(1)} %broadcast_add_fusion), kind=kOutput, calls=%fused_computation.50 | convolution fusion | flops 71354880 | bytes 451968 | tf_op jit(solution)/shard_map/abc,ma->mbc/dot_general | solution.py:31
  100.9 1.5 convolution_bitcast_fusion.1
  102.4 1.2 convolution_multiply_fusion
  104.9 1.2 pad_maximum_fusion.7
  106.2 1.9 collective-permute-start.8
  108.1 7.3 %collective-permute-start.9 = (f32[32,8,144]{2,1,0:T(8,128)S(1)}, f32[32,8,144]{2,1,0:T(8,128)S(1)}, u32[]{:S(2)}, u32[]{:S(2)}) collective-permute-start(f32[32,8,144]{2,1,0:T(8,128)S(1)} %get-tuple-element.30), channel_id=1, source_target_pairs={{4,0},{8,4},{12,8},{16,12},{20,16},{24,20},{28,24},{32,28},{36,32}... | collective-permute-start | bytes 442376 | tf_op jit(solution)/shard_map/ppermute | solution.py:25
  117.2 2.2 collective-permute-done.9
  119.4 2.2 pad_maximum_fusion.4
  121.7 14.2 %collective-permute-start.10 = (f32[8,48,144]{2,1,0:T(8,128)}, f32[8,48,144]{2,1,0:T(8,128)}, u32[]{:S(2)}, u32[]{:S(2)}) collective-permute-start(f32[8,48,144]{2,1,0:T(8,128)} %get-tuple-element.26), channel_id=1, source_target_pairs={{0,1},{1,2},{2,3},{3,0},{4,5},{5,6},{6,7},{7,4},{8,9},{9,10},{10,1... | collective-permute-start | bytes 663560 | tf_op jit(solution)/shard_map/ppermute | solution.py:24
  135.8 1.9 collective-permute-start.11
  138.4 1.0 reduce
  140.8 7.5 %all-to-all-start.1 = ((f32[8,16,256]{2,0,1:T(8,128)}), f32[8,16,256]{2,0,1:T(8,128)S(1)}, u32[]{:S(2)}, u32[]{:S(2)}) async-start(f32[8,16,256]{2,0,1:T(8,128)} %reshape.469), calls=%async_computation.1 | async-start | bytes 262144 | tf_op jit(solution)/shard_map/all_to_all | solution.py:139
  148.3 4.1 %collective-permute-done.11 = f32[8,48,144]{2,1,0:T(8,128)} collective-permute-done((f32[8,48,144]{2,1,0:T(8,128)}, f32[8,48,144]{2,1,0:T(8,128)}, u32[]{:S(2)}, u32[]{:S(2)}) %collective-permute-start.11) | collective-permute-done | bytes 221216 | tf_op jit(solution)/shard_map/ppermute | solution.py:25
  152.4 1.9 maximum_bitcast_fusion.2
  154.3 1.0 slice_bitcast_fusion.3
  155.3 5.8 %fusion = f32[48,48,4,48]{3,1,2,0:T(8,128)} fusion(f32[48,1,48,1,48]{4,2,3,0,1:T(8,128)S(1)} %get-tuple-element.16, f32[48,1,48,1,48]{4,2,3,0,1:T(8,128)S(1)} %get-tuple-element.17, f32[48,1,48,1,48]{4,2,3,0,1:T(8,128)S(1)} %get-tuple-element.24, f32[48,1,48,1,48]{4,2,3,0,1:T(8,128)S(1)} %get-tuple-element.15), kind=kOutput, calls=%fused_computation.1 | convolution fusion | flops 256154112 | bytes 3538944 | tf_op jit(solution)/shard_map/while/body/eval_jaxpr/zqjpi,ki->zqjpk/dot_general | solution.py:31
  161.6 1.4 convolution_multiply_fusion.1
  163.4 1.4 fusion.73
  165.0 1.0 reshape.472
  166.0 6.9 %all-to-all-start.2 = ((f32[8,1,4096]{2,1,0:T(1,128)}), f32[8,1,4096]{2,1,0:T(1,128)S(1)}, u32[]{:S(2)}, u32[]{:S(2)}) async-start(f32[8,1,4096]{2,1,0:T(1,128)} %reshape.472), calls=%async_computation.2 | async-start | bytes 262144 | tf_op jit(solution)/shard_map/all_to_all | solution.py:154
  172.9 8.7 %convolution_bitcast_fusion = f32[48,48,4,48]{3,1,2,0:T(8,128)} fusion(f32[48,48,4,48]{3,1,2,0:T(8,128)} %fusion), kind=kOutput, calls=%fused_computation.16 | convolution fusion | flops 254827008 | bytes 3538944 | tf_op jit(solution)/shard_map/while/body/eval_jaxpr/zqjpk,lj->zqlpk/dot_general | solution.py:31
  181.7 0.9 all-to-all-done.2
  182.6 1.0 reduce.1
  184.3 0.9 reshape.474
  185.2 5.4 %all-to-all-start.3 = ((f32[4,1,8192]{2,1,0:T(1,128)}), f32[4,1,8192]{2,1,0:T(1,128)S(1)}, u32[]{:S(2)}, u32[]{:S(2)}) async-start(f32[4,1,8192]{2,1,0:T(1,128)} %reshape.474), calls=%async_computation.3 | async-start | bytes 262144 | tf_op jit(solution)/shard_map/all_to_all | solution.py:153
  190.7 11.5 %fusion.7 = f32[48,48,4,48]{3,0,2,1:T(8,128)} fusion(f32[48,48,4,48]{3,1,2,0:T(8,128)} %convolution_bitcast_fusion), kind=kOutput, calls=%fused_computation.8 | convolution fusion | flops 254827008 | bytes 3538944 | tf_op jit(solution)/shard_map/while/body/eval_jaxpr/zqlpk,mz->mqlpk/dot_general | solution.py:31
  202.2 1.0 reduce.2
  204.7 2.2 collective-permute-start
  206.9 4.3 %collective-permute-start.1 = (f32[8,8,1]{2,1,0:T(8,128)S(1)}, f32[8,8,1]{2,1,0:T(8,128)S(1)}, u32[]{:S(2)}, u32[]{:S(2)}) collective-permute-start(f32[8,8,1]{2,1,0:T(8,128)S(1)} %get-tuple-element.38), channel_id=1, source_target_pairs={{64,0},{128,64},{192,128},{256,192},{320,256},{384,320},{448,384},... | collective-permute-start | bytes 776 | tf_op jit(solution)/shard_map/ppermute | solution.py:25
  211.2 5.1 %fusion.9 = f32[32,48,4,48]{3,0,2,1:T(8,128)S(1)} fusion(f32[48,48,4,48]{3,0,2,1:T(8,128)} %fusion.7, f32[48,48,48]{2,0,1:T(8,128)S(1)} %copy.45, s32[32]{0:T(128)S(1)} %iota_add_fusion), kind=kOutput, calls=%fused_computation.10 | convolution fusion | flops 170327040 | bytes 3391616 | tf_op jit(solution)/shard_map/while/body/eval_jaxpr/mqlpk,zm->zqlpk/dot_general | solution.py:31
  216.4 1.9 collective-permute-start.2
  218.3 7.5 %collective-permute-start.3 = (f32[8,1,34]{2,1,0:T(1,128)S(1)}, f32[8,1,34]{2,1,0:T(1,128)S(1)}, u32[]{:S(2)}, u32[]{:S(2)}) collective-permute-start(f32[8,1,34]{2,1,0:T(1,128)S(1)} %get-tuple-element.36), channel_id=1, source_target_pairs={{4,0},{8,4},{12,8},{16,12},{20,16},{24,20},{28,24},{32,28},{36,32}... | collective-permute-start | bytes 3272 | tf_op jit(solution)/shard_map/ppermute | solution.py:25
  225.8 4.9 %fusion.11 = f32[32,32,4,48]{3,0,2,1:T(8,128)S(1)} fusion(f32[32,48,4,48]{3,0,2,1:T(8,128)S(1)} %fusion.9, s32[32]{0:T(128)S(1)} %iota_add_fusion), kind=kOutput, calls=%fused_computation.12 | convolution fusion | flops 113261568 | bytes 1966208 | tf_op jit(solution)/shard_map/while/body/eval_jaxpr/zqlpk,jl->zqjpk/dot_general | solution.py:31
  230.9 8.6 %collective-permute-start.4 = (f32[1,10,34]{2,1,0:T(8,128)S(1)}, f32[1,10,34]{2,1,0:T(8,128)S(1)}, u32[]{:S(2)}, u32[]{:S(2)}) collective-permute-start(f32[1,10,34]{2,1,0:T(8,128)S(1)} %get-tuple-element.33), channel_id=1, source_target_pairs={{0,1},{1,2},{2,3},{3,0},{4,5},{5,6},{6,7},{7,4},{8,9},{9,10},{10,1... | collective-permute-start | bytes 4088 | tf_op jit(solution)/shard_map/ppermute | solution.py:24
  239.4 1.9 collective-permute-start.5
  241.4 2.0 fusion.14
  243.4 1.4 copy.47
  245.7 2.6 %collective-permute-done.5 = f32[1,10,34]{2,1,0:T(8,128)S(1)} collective-permute-done((f32[1,10,34]{2,1,0:T(8,128)S(1)}, f32[1,10,34]{2,1,0:T(8,128)S(1)}, u32[]{:S(2)}, u32[]{:S(2)}) %collective-permute-start.5) | collective-permute-done | bytes 1392 | tf_op jit(solution)/shard_map/ppermute | solution.py:25
  249.7 1.1 copy.48
  (111 shorter events, 19.4 us)
Async XLA Ops:
  67.9 11.5 %copy-start = (f32[32,32,128]{2,1,0:T(8,128)S(1)}, f32[32,32,128]{2,1,0:T(8,128)}, u32[]{:S(2)}) copy-start(f32[32,32,128]{2,1,0:T(8,128)} %param.1) | copy-start | bytes 1572868
  70.0 67.8 %all-to-all-start = ((f32[8,1,4096]{2,1,0:T(1,128)}), f32[8,1,4096]{2,1,0:T(1,128)S(1)}, u32[]{:S(2)}, u32[]{:S(2)}) async-start(f32[8,1,4096]{2,1,0:T(1,128)} %reshape.470), calls=%async_computation | async-start | bytes 262144 | tf_op jit(solution)/shard_map/all_to_all | solution.py:140
  80.5 24.5 %collective-permute-start.6 = (f32[32,32,8]{2,1,0:T(8,128)}, f32[32,32,8]{2,1,0:T(8,128)S(1)}, u32[]{:S(2)}, u32[]{:S(2)}) collective-permute-start(f32[32,32,8]{2,1,0:T(8,128)} %get-tuple-element.31), channel_id=1, source_target_pairs={{0,64},{64,128},{128,192},{192,256},{256,320},{320,384},{384,448},... | collective-permute-start | bytes 98312 | tf_op jit(solution)/shard_map/ppermute | solution.py:24
  83.8 21.1 %collective-permute-start.7 = (f32[32,32,8]{2,1,0:T(8,128)}, f32[32,32,8]{2,1,0:T(8,128)}, u32[]{:S(2)}, u32[]{:S(2)}) collective-permute-start(f32[32,32,8]{2,1,0:T(8,128)} %get-tuple-element.32), channel_id=1, source_target_pairs={{64,0},{128,64},{192,128},{256,192},{320,256},{384,320},{448,384},... | collective-permute-start | bytes 98312 | tf_op jit(solution)/shard_map/ppermute | solution.py:25
  102.4 1.2 copy-start.13
  102.4 1.9 copy-start.12
  106.2 11.0 %collective-permute-start.8 = (f32[32,8,144]{2,1,0:T(8,128)S(1)}, f32[32,8,144]{2,1,0:T(8,128)S(1)}, u32[]{:S(2)}, u32[]{:S(2)}) collective-permute-start(f32[32,8,144]{2,1,0:T(8,128)S(1)} %get-tuple-element.29), channel_id=1, source_target_pairs={{0,4},{4,8},{8,12},{12,16},{16,20},{20,24},{24,28},{28,32},{32,36}... | collective-permute-start | bytes 442376 | tf_op jit(solution)/shard_map/ppermute | solution.py:24
  108.1 11.3 %collective-permute-start.9 = (f32[32,8,144]{2,1,0:T(8,128)S(1)}, f32[32,8,144]{2,1,0:T(8,128)S(1)}, u32[]{:S(2)}, u32[]{:S(2)}) collective-permute-start(f32[32,8,144]{2,1,0:T(8,128)S(1)} %get-tuple-element.30), channel_id=1, source_target_pairs={{4,0},{8,4},{12,8},{16,12},{20,16},{24,20},{28,24},{32,28},{36,32}... | collective-permute-start | bytes 442376 | tf_op jit(solution)/shard_map/ppermute | solution.py:25
  116.4 21.3 %copy-start.14 = (pred[4]{0:T(512)(128)(4,1)S(1)}, pred[4]{0:T(512)(128)(4,1)}, u32[]{:S(2)}) copy-start(pred[4]{0:T(512)(128)(4,1)} %fusion.229) | copy-start | bytes 16
  116.4 21.3 %copy-start.15 = (pred[32]{0:T(512)(128)(4,1)S(1)}, pred[32]{0:T(512)(128)(4,1)}, u32[]{:S(2)}) copy-start(pred[32]{0:T(512)(128)(4,1)} %iota_compare_fusion.8) | copy-start | bytes 100
  117.2 4.4 %copy-start.1 = (f32[32,8,144]{2,1,0:T(8,128)}, f32[32,8,144]{2,1,0:T(8,128)S(1)}, u32[]{:S(2)}) copy-start(f32[32,8,144]{2,1,0:T(8,128)S(1)} %collective-permute-done.8) | copy-start | bytes 442372
  119.4 2.2 copy-start.2
  121.7 26.6 %collective-permute-start.10 = (f32[8,48,144]{2,1,0:T(8,128)}, f32[8,48,144]{2,1,0:T(8,128)}, u32[]{:S(2)}, u32[]{:S(2)}) collective-permute-start(f32[8,48,144]{2,1,0:T(8,128)} %get-tuple-element.26), channel_id=1, source_target_pairs={{0,1},{1,2},{2,3},{3,0},{4,5},{5,6},{6,7},{7,4},{8,9},{9,10},{10,1... | collective-permute-start | bytes 663560 | tf_op jit(solution)/shard_map/ppermute | solution.py:24
  135.8 16.5 %collective-permute-start.11 = (f32[8,48,144]{2,1,0:T(8,128)}, f32[8,48,144]{2,1,0:T(8,128)}, u32[]{:S(2)}, u32[]{:S(2)}) collective-permute-start(f32[8,48,144]{2,1,0:T(8,128)} %get-tuple-element.28), channel_id=1, source_target_pairs={{1,0},{2,1},{3,2},{0,3},{5,4},{6,5},{7,6},{4,7},{9,8},{10,9},{11,1... | collective-permute-start | bytes 663560 | tf_op jit(solution)/shard_map/ppermute | solution.py:25
  140.8 20.4 %all-to-all-start.1 = ((f32[8,16,256]{2,0,1:T(8,128)}), f32[8,16,256]{2,0,1:T(8,128)S(1)}, u32[]{:S(2)}, u32[]{:S(2)}) async-start(f32[8,16,256]{2,0,1:T(8,128)} %reshape.469), calls=%async_computation.1 | async-start | bytes 262144 | tf_op jit(solution)/shard_map/all_to_all | solution.py:139
  155.3 6.2 %copy-start.8 = (f32[32,4]{0,1:T(4,128)S(1)}, f32[32,4]{0,1:T(4,128)}, u32[]{:S(2)}) copy-start(f32[32,4]{0,1:T(4,128)} %broadcast_add_fusion.1) | copy-start | bytes 1540
  155.3 6.2 %copy-start.9 = (f32[32,4]{0,1:T(4,128)S(1)}, f32[32,4]{0,1:T(4,128)}, u32[]{:S(2)}) copy-start(f32[32,4]{0,1:T(4,128)} %broadcast_add_fusion.2) | copy-start | bytes 1540
  155.3 6.2 %copy-start.24 = (pred[256]{0:T(512)(128)(4,1)S(1)}, pred[256]{0:T(512)(128)(4,1)}, u32[]{:S(2)}) copy-start(pred[256]{0:T(512)(128)(4,1)} %iota_compare_fusion.7) | copy-start | bytes 772
  166.0 16.5 %all-to-all-start.2 = ((f32[8,1,4096]{2,1,0:T(1,128)}), f32[8,1,4096]{2,1,0:T(1,128)S(1)}, u32[]{:S(2)}, u32[]{:S(2)}) async-start(f32[8,1,4096]{2,1,0:T(1,128)} %reshape.472), calls=%async_computation.2 | async-start | bytes 262144 | tf_op jit(solution)/shard_map/all_to_all | solution.py:154
  185.2 16.9 %all-to-all-start.3 = ((f32[4,1,8192]{2,1,0:T(1,128)}), f32[4,1,8192]{2,1,0:T(1,128)S(1)}, u32[]{:S(2)}, u32[]{:S(2)}) async-start(f32[4,1,8192]{2,1,0:T(1,128)} %reshape.474), calls=%async_computation.3 | async-start | bytes 262144 | tf_op jit(solution)/shard_map/all_to_all | solution.py:153
  203.2 0.7 copy-start.10
  203.2 0.7 copy-start.11
  204.7 11.6 %collective-permute-start = (f32[8,8,1]{2,1,0:T(8,128)S(1)}, f32[8,8,1]{2,1,0:T(8,128)S(1)}, u32[]{:S(2)}, u32[]{:S(2)}) collective-permute-start(f32[8,8,1]{2,1,0:T(8,128)S(1)} %get-tuple-element.37), channel_id=1, source_target_pairs={{0,64},{64,128},{128,192},{192,256},{256,320},{320,384},{384,448},... | collective-permute-start | bytes 776 | tf_op jit(solution)/shard_map/ppermute | solution.py:24
  206.9 9.4 %collective-permute-start.1 = (f32[8,8,1]{2,1,0:T(8,128)S(1)}, f32[8,8,1]{2,1,0:T(8,128)S(1)}, u32[]{:S(2)}, u32[]{:S(2)}) collective-permute-start(f32[8,8,1]{2,1,0:T(8,128)S(1)} %get-tuple-element.38), channel_id=1, source_target_pairs={{64,0},{128,64},{192,128},{256,192},{320,256},{384,320},{448,384},... | collective-permute-start | bytes 776 | tf_op jit(solution)/shard_map/ppermute | solution.py:25
  216.4 14.4 %collective-permute-start.2 = (f32[8,1,34]{2,1,0:T(1,128)S(1)}, f32[8,1,34]{2,1,0:T(1,128)S(1)}, u32[]{:S(2)}, u32[]{:S(2)}) collective-permute-start(f32[8,1,34]{2,1,0:T(1,128)S(1)} %get-tuple-element.35), channel_id=1, source_target_pairs={{0,4},{4,8},{8,12},{12,16},{16,20},{20,24},{24,28},{28,32},{32,36}... | collective-permute-start | bytes 3272 | tf_op jit(solution)/shard_map/ppermute | solution.py:24
  218.3 12.5 %collective-permute-start.3 = (f32[8,1,34]{2,1,0:T(1,128)S(1)}, f32[8,1,34]{2,1,0:T(1,128)S(1)}, u32[]{:S(2)}, u32[]{:S(2)}) collective-permute-start(f32[8,1,34]{2,1,0:T(1,128)S(1)} %get-tuple-element.36), channel_id=1, source_target_pairs={{4,0},{8,4},{12,8},{16,12},{20,16},{24,20},{28,24},{32,28},{36,32}... | collective-permute-start | bytes 3272 | tf_op jit(solution)/shard_map/ppermute | solution.py:25
  230.9 14.9 %collective-permute-start.4 = (f32[1,10,34]{2,1,0:T(8,128)S(1)}, f32[1,10,34]{2,1,0:T(8,128)S(1)}, u32[]{:S(2)}, u32[]{:S(2)}) collective-permute-start(f32[1,10,34]{2,1,0:T(8,128)S(1)} %get-tuple-element.33), channel_id=1, source_target_pairs={{0,1},{1,2},{2,3},{3,0},{4,5},{5,6},{6,7},{7,4},{8,9},{9,10},{10,1... | collective-permute-start | bytes 4088 | tf_op jit(solution)/shard_map/ppermute | solution.py:24
  239.4 8.9 %collective-permute-start.5 = (f32[1,10,34]{2,1,0:T(8,128)S(1)}, f32[1,10,34]{2,1,0:T(8,128)S(1)}, u32[]{:S(2)}, u32[]{:S(2)}) collective-permute-start(f32[1,10,34]{2,1,0:T(8,128)S(1)} %get-tuple-element.34), channel_id=1, source_target_pairs={{1,0},{2,1},{3,2},{0,3},{5,4},{6,5},{7,6},{4,7},{9,8},{10,9},{11,1... | collective-permute-start | bytes 4088 | tf_op jit(solution)/shard_map/ppermute | solution.py:25
  244.7 3.6 %copy-start.16 = (s32[128]{0:T(128)S(1)}, s32[128]{0:T(128)}, u32[]{:S(2)}) copy-start(s32[128]{0:T(128)} %get-tuple-element.43) | copy-start | bytes 1540
  244.7 3.6 %copy-start.17 = (s32[128]{0:T(128)S(1)}, s32[128]{0:T(128)}, u32[]{:S(2)}) copy-start(s32[128]{0:T(128)} %get-tuple-element.44) | copy-start | bytes 1540
  244.7 3.6 %copy-start.18 = (f32[128]{0:T(128)S(1)}, f32[128]{0:T(128)}, u32[]{:S(2)}) copy-start(f32[128]{0:T(128)} %get-tuple-element.45) | copy-start | bytes 1540
  244.8 3.6 %copy-start.19 = (f32[128]{0:T(128)S(1)}, f32[128]{0:T(128)}, u32[]{:S(2)}) copy-start(f32[128]{0:T(128)} %get-tuple-element.46) | copy-start | bytes 1540
  244.8 3.6 %copy-start.20 = (pred[128]{0:T(512)(128)(4,1)S(1)}, pred[128]{0:T(512)(128)(4,1)}, u32[]{:S(2)}) copy-start(pred[128]{0:T(512)(128)(4,1)} %get-tuple-element.47) | copy-start | bytes 388
  244.8 3.6 %copy-start.21 = (pred[128]{0:T(512)(128)(4,1)S(1)}, pred[128]{0:T(512)(128)(4,1)}, u32[]{:S(2)}) copy-start(pred[128]{0:T(512)(128)(4,1)} %get-tuple-element.48) | copy-start | bytes 388
  244.8 3.6 %copy-start.22 = (s32[128]{0:T(128)S(1)}, s32[128]{0:T(128)}, u32[]{:S(2)}) copy-start(s32[128]{0:T(128)} %broadcast_add_fusion.4) | copy-start | bytes 1540
  244.8 3.6 %copy-start.23 = (f32[128]{0:T(128)S(1)}, f32[128]{0:T(128)}, u32[]{:S(2)}) copy-start(f32[128]{0:T(128)} %fusion.231) | copy-start | bytes 1540
  244.8 3.9 %copy-start.3 = (f32[32]{0:T(128)S(1)}, f32[32]{0:T(128)}, u32[]{:S(2)}) copy-start(f32[32]{0:T(128)} %get-tuple-element.52) | copy-start | bytes 388
  244.8 3.9 %copy-start.4 = (pred[32]{0:T(512)(128)(4,1)S(1)}, pred[32]{0:T(512)(128)(4,1)}, u32[]{:S(2)}) copy-start(pred[32]{0:T(512)(128)(4,1)} %get-tuple-element.53) | copy-start | bytes 100
  244.8 3.9 %copy-start.5 = (pred[32]{0:T(512)(128)(4,1)S(1)}, pred[32]{0:T(512)(128)(4,1)}, u32[]{:S(2)}) copy-start(pred[32]{0:T(512)(128)(4,1)} %get-tuple-element.54) | copy-start | bytes 100
  244.8 3.9 %copy-start.6 = (s32[32]{0:T(128)S(1)}, s32[32]{0:T(128)}, u32[]{:S(2)}) copy-start(s32[32]{0:T(128)} %broadcast_add_fusion.6) | copy-start | bytes 388
  244.8 3.9 %copy-start.7 = (f32[32]{0:T(128)S(1)}, f32[32]{0:T(128)}, u32[]{:S(2)}) copy-start(f32[32]{0:T(128)} %fusion.232) | copy-start | bytes 388
where the time goes:
time: 256 us; the launch traced here: 251 us
  starting transfers between devices  87.8 us (34%)
  matrix products  52.1 us (20%)
  blocking collectives  41.4 us (16%)
  local copies, waits for them, and re-layouts  32.1 us (13%)
  other arithmetic  26.1 us (10%)
  waiting for transfers between devices  10.6 us (4%)
    dot_general x18, matrix products, contract(): return jnp.einsum(pattern, former, latter, precision=lax.Precision.HIGHEST)  52.1 us
    all_gather x1, blocking collectives, body(): gathered = lax.all_gather(charges, 'gy', axis=1, tiled=True)  41.4 us
    ppermute x6, starting transfers between devices, padded_2(): before = lax.ppermute(last, axis, up)  32.2 us
    ppermute x6, starting transfers between devices, padded_2(): after = lax.ppermute(leading, axis, down)  26.6 us
    reshape x1, local copies, waits for them, and re-layouts, body(): density.reshape(block_z, COARSEN, block_y, COARSEN, block_x, COARSEN)  19.4 us
    all_to_all x1, starting transfers between devices, body(): lax.all_to_all(spectrum, 'gx', split_axis=1, concat_axis=2, tiled=True)  9.3 us
    ppermute x6, waiting for transfers between devices, padded_2(): after = lax.ppermute(leading, axis, down)  8.88 us
    all_to_all x1, starting transfers between devices, body(): lax.all_to_all(lax.all_to_all(spectrum, 'gx', split_axis=1, concat_axis=2...  7.47 us
  transfers between devices with their start and end apart: 16, of which 6 were waited for; matrix products, arithmetic and copies ran while one was open for 27% of the time, Pallas kernels for 0%

commit v1 on v0

v1 whole, which is shorter than its diff:
```python
import math

import jax
import jax.numpy as jnp
import ml_dtypes
import numpy as np
from jax import lax
from jax.experimental import pallas as pl
from jax.experimental.pallas import tpu as pltpu
from jax.sharding import PartitionSpec as P

HALO = 8
COARSEN = 4
SCREEN = 6.0
SOFTEN = 0.25

NZ, NY, NX = 128, 512, 1024
GZ, GY, GX = 4, 16, 8
CZ, CY, CX = NZ // GZ, NY // GY, NX // GX
MZ, MY, MX = NZ // COARSEN, NY // COARSEN, NX // COARSEN
BZ, BY, BX = MZ // GZ, MY // GY, MX // GX
PZ, PY, PX = CZ + 2 * HALO, CY + 2 * HALO, CX + 2 * HALO
LANES = 256
GROUP = 3 * PY
BORDER_X = BX + 2

f32 = jnp.float32
bf16 = jnp.bfloat16
HIGHEST = lax.Precision.HIGHEST


def cas(a, b, points):
    angles = 2.0 * np.pi / points * (np.outer(a, b) % points)
    return np.cos(angles) + np.sin(angles)


def split(table):
    high = table.astype(np.float32).astype(ml_dtypes.bfloat16)
    low = (table - high.astype(np.float64)).astype(np.float32).astype(ml_dtypes.bfloat16)
    return high, low


def near_tables():
    reach = np.arange(HALO + 1)
    both = np.arange(-HALO, HALO + 1)
    squared = (
        reach[:, None, None] ** 2 + both[None, :, None] ** 2 + both[None, None, :] ** 2
    ).astype(np.float64)
    erfc = np.vectorize(math.erfc)
    kernel = erfc(np.sqrt(squared) / SCREEN) / (4.0 * math.pi * np.sqrt(squared + SOFTEN))
    cos_y = np.cos(2.0 * np.pi / PY * np.outer(np.arange(PY), both))
    cos_x = np.cos(2.0 * np.pi / PX * np.outer(np.arange(PX), both))
    spectral = np.einsum("dab,ka,lb->dkl", kernel, cos_y, cos_x) / (PY * PX)
    gains = np.zeros((HALO + 1, PY, LANES))
    gains[:, :, :PX] = spectral

    every_x, every_y = np.arange(PX), np.arange(PY)
    forward_x = np.zeros((PX, LANES))
    forward_x[:, :PX] = cas(every_x, every_x, PX)
    high, low = split(forward_x)
    own = slice(HALO, HALO + CX)
    ends = np.r_[0:HALO, HALO + CX : PX]
    into_x = np.zeros((512, LANES), ml_dtypes.bfloat16)
    into_x[0:128], into_x[128:256], into_x[256:384] = high[own], low[own], high[own]
    into_x[384:400], into_x[400:416], into_x[416:432] = high[ends], low[ends], high[ends]

    high, low = split(cas(every_y, every_y, PY))
    into_y = np.concatenate([high, low, high], axis=1)
    out_y = into_y[HALO : HALO + CY]

    back_x = np.zeros((LANES, CX))
    back_x[:PX] = cas(every_x, every_x[own], PX)
    high, low = split(back_x)
    out_x = np.concatenate([high, low, high], axis=0)
    return gains.astype(np.float32), into_x, into_y, out_y, out_x


def far_tables():
    every_y = cas(np.arange(MY), np.arange(MY), MY).reshape(GY, BY, GY, BY)
    first_y = np.einsum("gkbc,hi->ghkbic", every_y, np.eye(2)).reshape(GY, 2 * BY, GY * 2 * BY)

    full_x = cas(np.arange(MX), np.arange(MX), MX)
    full_z = cas(np.arange(MZ), np.arange(MZ), MZ)
    order = full_z.reshape(MZ, GZ, 2, 4).transpose(0, 3, 1, 2).reshape(MZ, MZ)
    into_z = np.kron(order, np.eye(BY))

    def waves(points):
        index = np.arange(points)
        signed = (index + points // 2) % points - points // 2
        laplace = 2.0 - 2.0 * np.cos(2.0 * np.pi / points * index)
        return laplace, (2.0 * np.pi / (points * COARSEN) * signed) ** 2

    (lap_z, wave_z), (lap_y, wave_y), (lap_x, wave_x) = waves(MZ), waves(MY), waves(MX)
    laplace = lap_z[:, None, None] + lap_y[None, :, None] + lap_x[None, None, :]
    wave = wave_z[:, None, None] + wave_y[None, :, None] + wave_x[None, None, :]
    laplace[0, 0, 0] = 1.0
    gain = np.exp(-(SCREEN * SCREEN / 4.0) * wave) / (COARSEN * laplace)
    gain[0, 0, 0] = 0.0
    gain = gain / (MZ * MY * MX)
    gain = gain.reshape(MZ, GY, BY, MX).transpose(1, 0, 2, 3).reshape(GY, MZ * BY, MX)

    out_z = np.zeros((GZ, 3, 4, BY, MZ, BY))
    for g in range(GZ):
        for plane in range(BZ + 2):
            z = (g * BZ - 1 + plane) % MZ
            for k in range(BY):
                out_z[g, plane % 3, plane // 3, k, :, k] = full_z[:, z]
    out_z = out_z.reshape(GZ, 3 * 4 * BY, MZ * BY)

    out_x = np.zeros((GX, MX, 128))
    for g in range(GX):
        out_x[g, :, :BORDER_X] = full_x[:, (g * BX - 1 + np.arange(BORDER_X)) % MX]

    def refine(coarse):
        matrix = np.zeros((COARSEN * coarse, coarse + 2))
        for fine in range(COARSEN * coarse):
            below, t = fine // COARSEN, (fine % COARSEN + 0.5) / COARSEN - 0.5
            matrix[fine, below + 1] = 1.0 - abs(t)
            matrix[fine, below if t < 0 else below + 2] = abs(t)
        return matrix

    last_y = np.zeros((GY, CY, MY))
    for g in range(GY):
        rows = (g * BY - 1 + np.arange(BY + 2)) % MY
        last_y[g] = refine(BY) @ cas(rows, np.arange(MY), MY)

    last_x = np.zeros((128, 3, CX))
    for low in range(3):
        last_x[low * BORDER_X : (low + 1) * BORDER_X, low] = refine(BX).T
    last_x = last_x.reshape(128, 3 * CX)
    tables = first_y, full_x, into_z, gain, out_z, out_x, last_y, last_x
    return tuple(table.astype(np.float32) for table in tables)


def dot(a, b):
    return jnp.dot(a, b, preferred_element_type=f32)


def exact_dot(a, b):
    return jnp.dot(a, b, preferred_element_type=f32, precision=HIGHEST)


def halves(x):
    high = x.astype(bf16)
    return high, (x - high.astype(f32)).astype(bf16)


def lane(shape):
    return lax.broadcasted_iota(jnp.int32, shape, len(shape) - 1)


def charge_kernel(density, out):
    parts = []
    for high in range(2):
        planes = []
        for low in range(4):
            z = (high * 4 + low) * COARSEN
            planes.append((density[z] + density[z + 1]) + (density[z + 2] + density[z + 3]))
        parts.append(jnp.concatenate(planes, axis=1))
    rows = jnp.concatenate(parts, axis=0)

    def pool(shape, fine, coarse):
        a = lax.broadcasted_iota(jnp.int32, shape, fine)
        b = lax.broadcasted_iota(jnp.int32, shape, coarse)
        return (a // COARSEN == b).astype(f32)

    rows = exact_dot(rows, pool((4 * CX, 128), 0, 1))
    rows = exact_dot(pool((2 * BY, 2 * CY), 1, 0), rows)
    for peer in range(GY):
        out[peer] = rows


def first_kernel(table, charges, out, held, sem):
    copy = pltpu.make_async_copy(table.at[lax.axis_index("gy")], held, sem)
    copy.start()
    rows = charges[...].reshape(GY * 2 * BY, 128)
    copy.wait()
    rows = exact_dot(held[...], rows)
    for peer in range(GX * GZ):
        out[peer] = rows


def filter_kernel(
    full_x, into_z, gain, out_z, out_x, spectrum, out, held_x, held_z, held_g, held_iz, held_ix, sems
):
    sources = (
        (full_x, held_x),
        (into_z, held_z),
        (gain.at[lax.axis_index("gy")], held_g),
        (out_z.at[lax.axis_index("gz")], held_iz),
        (out_x.at[lax.axis_index("gx")], held_ix),
    )
    copies = [
        pltpu.make_async_copy(source, held, sems.at[i]) for i, (source, held) in enumerate(sources)
    ]
    for copy in copies:
        copy.start()
    place = lane((GZ * 16, 128)) // BX
    blocks = []
    for low in range(4):
        sides = []
        for side in range(2):
            total = None
            for q in range(4):
                peer = spectrum[pl.ds((side * 4 + q) * GZ, GZ)].reshape(GZ * 16, 128)
                shift = (q - low) * BX % 128
                moved = pltpu.roll(peer, shift, 1) if shift else peer
                total = moved if q == 0 else jnp.where(place == q, moved, total)
            sides.append(total)
        blocks.append(jnp.concatenate(sides, axis=1))
    rows = jnp.concatenate(blocks, axis=0)
    copies[0].wait()
    rows = exact_dot(rows, held_x[...])
    copies[1].wait()
    rows = exact_dot(held_z[...], rows)
    copies[2].wait()
    rows = rows * held_g[...]
    copies[3].wait()
    rows = exact_dot(held_iz[...], rows)
    copies[4].wait()
    rows = exact_dot(rows, held_ix[...])
    total = rows[0:32] + pltpu.roll(rows[32:64], BORDER_X, 1) + pltpu.roll(rows[64:96], 2 * BORDER_X, 1)
    for peer in range(GY):
        out[peer] = total


def last_kernel(last_y, last_x, spectrum, near, out, held_y, held_x, sems):
    copies = [
        pltpu.make_async_copy(last_y.at[lax.axis_index("gy")], held_y, sems.at[0]),
        pltpu.make_async_copy(last_x, held_x, sems.at[1]),
    ]
    for copy in copies:
        copy.start()
    copies[0].wait()
    rows = []
    for high in range(4):
        rows.append(exact_dot(held_y[...], spectrum[:, pl.ds(high * BY, BY), :].reshape(MY, 128)))
    copies[1].wait()
    field = exact_dot(jnp.concatenate(rows, axis=0), held_x[...])

    def plane(z):
        high, low = z // 3, z % 3
        return field[high * CY : (high + 1) * CY, low * CX : (low + 1) * CX]

    for block in range(BZ):
        before, here, after = plane(block), plane(block + 1), plane(block + 2)
        for residue in range(COARSEN):
            t = (residue + 0.5) / COARSEN - 0.5
            value = (1.0 - abs(t)) * here + abs(t) * (before if t < 0 else after)
            z = block * COARSEN + residue
            out[z] = near[z] + value


def plane_rows(z, density, below, above, before, after):
    if z < HALO:
        middle = below[z]
    elif z < HALO + CZ:
        middle = density[z - HALO]
    else:
        middle = above[z - HALO - CZ]
    return jnp.concatenate([before[z], middle, after[z]], axis=0)


def edge_kernel(density, below, above, before, after, first, last):
    place = lane((GROUP, 128)) // HALO
    left = right = jnp.zeros((GROUP, 128), f32)
    for j in range(16):
        rows = jnp.concatenate(
            [plane_rows(3 * j + i, density, below, above, before, after) for i in range(3)], axis=0
        )
        shift = j * HALO
        left = jnp.where(place == j, pltpu.roll(rows, shift, 1) if shift else rows, left)
        shift = (j * HALO - (CX - HALO)) % 128
        right = jnp.where(place == j, pltpu.roll(rows, shift, 1) if shift else rows, right)
    first[...] = left
    last[...] = right


def near_kernel(
    density, below, above, before, after, left, right, gains, into_x, into_y, out_y, out_x, out, wave_x, wave_y, wave_z
):
    lanes = lane((GROUP, 128))
    for j in range(16):
        rows = jnp.concatenate(
            [plane_rows(3 * j + i, density, below, above, before, after) for i in range(3)], axis=0
        )
        ends = jnp.where(
            lanes < HALO,
            pltpu.roll(left[...], (-HALO * j) % 128, 1) if j else left[...],
            jnp.where(lanes < 2 * HALO, pltpu.roll(right[...], (HALO - HALO * j) % 128, 1), 0.0)
            if j != 1
            else jnp.where(lanes < 2 * HALO, right[...], 0.0),
        )
        high = ends.astype(bf16).astype(f32)
        low = ends - high
        ends = (high + pltpu.roll(high, 2 * HALO, 1) + pltpu.roll(low, 4 * HALO, 1)).astype(bf16)
        high, low = halves(rows)
        wave = dot(jnp.concatenate([high, high, low, ends], axis=1), into_x[...])
        for i in range(3):
            wave_x[3 * j + i] = wave[i * PY : (i + 1) * PY]

    @pl.loop(0, PZ, unroll=8)
    def _(z):
        high, low = halves(wave_x[z])
        wave_y[z] = dot(into_y[...], jnp.concatenate([high, high, low], axis=0))

    @pl.loop(0, PY // 8)
    def _(c):
        row = pl.ds(pl.multiple_of(c * 8, 8), 8)
        for side in range(LANES // 128):
            column = pl.ds(side * 128, 128)
            gain = [gains[d, row, column] for d in range(HALO + 1)]
            window = [wave_y[z, row, column] for z in range(2 * HALO)]
            for z in range(CZ):
                window.append(wave_y[z + 2 * HALO, row, column])
                total = gain[0] * window[HALO]
                for d in range(1, HALO + 1):
                    total = total + gain[d] * (window[HALO - d] + window[HALO + d])
                wave_z[z, row, column] = total
                window.pop(0)

    @pl.loop(0, CZ // 4, unroll=2)
    def _(step):
        rows = []
        for i in range(4):
            high, low = halves(wave_z[step * 4 + i])
            rows.append(dot(out_y[...], jnp.concatenate([high, high, low], axis=0)))
        high, low = halves(jnp.concatenate(rows, axis=0))
        field = dot(jnp.concatenate([high, high, low], axis=1), out_x[...])
        for i in range(4):
            out[step * 4 + i] = field[i * CY : (i + 1) * CY]


def call(kernel, outs, scratch=(), specs=None, name=None):
    vmem = pl.BlockSpec(memory_space=pltpu.VMEM)
    many = isinstance(outs, list)
    return pl.pallas_call(
        kernel,
        out_shape=[jax.ShapeDtypeStruct(s, f32) for s in outs] if many else jax.ShapeDtypeStruct(outs, f32),
        in_specs=specs,
        out_specs=[vmem] * len(outs) if many else vmem,
        scratch_shapes=list(scratch),
        compiler_params=pltpu.CompilerParams(vmem_limit_bytes=40 * 1024 * 1024),
        name=name,
    )


def both_ways(low_edge, high_edge, axis):
    peers = lax.axis_size(axis)
    up = [(i, (i + 1) % peers) for i in range(peers)]
    down = [(j, i) for i, j in up]
    return lax.ppermute(high_edge, axis, up), lax.ppermute(low_edge, axis, down)


def body(density):
    vmem, far = pl.BlockSpec(memory_space=pltpu.VMEM), pl.BlockSpec(memory_space=pl.ANY)
    dma = pltpu.SemaphoreType.DMA
    first_y, full_x, into_z, gain, out_z, out_x, last_y, last_x = (jnp.asarray(t) for t in far_tables())
    near_consts = [jnp.asarray(t) for t in near_tables()]

    charges = call(charge_kernel, (GY, 16, 128), specs=[vmem], name="charges")(density)
    charges = lax.all_to_all(charges, "gy", 0, 0, tiled=True)

    below, above = both_ways(density[:HALO], density[CZ - HALO :], "gz")

    def edge(start):
        rows = slice(start, start + HALO)
        return jnp.concatenate([below[:, rows], density[:, rows], above[:, rows]], axis=0)

    before, after = both_ways(edge(0), edge(CY - HALO), "gy")
    ends = call(edge_kernel, [(GROUP, 128)] * 2, specs=[vmem] * 5, name="edges")(
        density, below, above, before, after
    )
    left, right = both_ways(ends[0], ends[1], "gx")

    spectrum = call(
        first_kernel,
        (GX * GZ, 16, 128),
        [pltpu.VMEM((16, 256), f32), dma],
        [far, vmem],
        name="first_y",
    )(first_y, charges)
    spectrum = lax.all_to_all(spectrum, ("gx", "gz"), 0, 0, tiled=True)
    spectrum = call(
        filter_kernel,
        (GY, 32, 128),
        [
            pltpu.VMEM((MX, MX), f32),
            pltpu.VMEM((256, 256), f32),
            pltpu.VMEM((256, MX), f32),
            pltpu.VMEM((96, 256), f32),
            pltpu.VMEM((MX, 128), f32),
            dma((5,)),
        ],
        [far] * 5 + [vmem],
        name="filter",
    )(full_x, into_z, gain, out_z, out_x, spectrum)
    spectrum = lax.all_to_all(spectrum, "gy", 0, 0, tiled=True)

    near = call(
        near_kernel,
        (CZ, CY, CX),
        [
            pltpu.VMEM((PZ, PY, LANES), f32),
            pltpu.VMEM((PZ, PY, LANES), f32),
            pltpu.VMEM((CZ, PY, LANES), f32),
        ],
        [vmem] * 12,
        name="near",
    )(density, below, above, before, after, left, right, *near_consts)

    return call(
        last_kernel,
        (CZ, CY, CX),
        [pltpu.VMEM((CY, MY), f32), pltpu.VMEM((128, 3 * CX), f32), dma((2,))],
        [far, far, vmem, vmem],
        name="last",
    )(last_y, last_x, spectrum, near)


def solution(mesh):
    placed = P("gz", "gy", "gx")
    return jax.shard_map(body, mesh=mesh, in_specs=(placed,), out_specs=placed, check_vma=False)
```

time: 256 us -> 104 us (0.41); the launches traced: 251 us -> 103 us
  matrix products: 52.1 us -> 0 us
  blocking collectives: 41.4 us -> 0 us
  starting transfers between devices: 87.8 us -> 55.9 us
  other arithmetic: 26.1 us -> 0.03 us
  local copies, waits for them, and re-layouts: 32.1 us -> 10.3 us
  Pallas kernels: 0 us -> 14.8 us
  waiting for transfers between devices: 10.6 us -> 21.3 us
    dot_general x18 -> x0, matrix products: 52.1 us -> none  [contract(): return jnp.einsum(pattern, former, latter, precision=lax.Precision.HIGHEST)]
    all_gather x1 -> x0, blocking collectives: 41.4 us -> none  [body(): gathered = lax.all_gather(charges, 'gy', axis=1, tiled=True)]
    ppermute x12 -> x6, starting transfers between devices: 58.7 us -> 23.2 us  [the longest x3 11.7 us: both_ways(): lax.ppermute(high_edge, axis, up)]
    reshape x2 -> x0, local copies, waits for them, and re-layouts: 20.3 us -> none  [the longest x1 19.4 us: body(): density.reshape(block_z, COARSEN, block_y, COARSEN, block_x, COARSEN)]
    pallas_call x0 -> x6, Pallas kernels: none -> 14.8 us  [the longest x1 7.04 us: body(): call(near_kernel, (CZ, CY, CX), [pltpu.VMEM((PZ, PY, LANES), f32), pltpu....]
    all_to_all x4 -> x3, waiting for transfers between devices: 0.91 us -> 12.6 us  [the longest x1 12.6 us: body(): spectrum = lax.all_to_all(spectrum, ('gx', 'gz'), 0, 0, tiled=True)]
    reduce_sum x1 -> x0, other arithmetic: 7.06 us -> none  [body(): density.reshape(block_z, COARSEN, block_y, COARSEN, block_x, COARSEN)]
    unnamed x56 -> x30, local copies, waits for them, and re-layouts: 3.54 us -> 8.33 us
  transfers between devices with their start and end apart: 16 -> 9, of which waited for: 6 -> 4; matrix products, arithmetic and copies ran while one was open for 27% -> 2% of each run, Pallas kernels for 0% -> 8%
where the time goes in v1:
time: 104 us; the launch traced here: 103 us
  starting transfers between devices  55.9 us (54%)
  waiting for transfers between devices  21.3 us (20%)
  Pallas kernels  14.8 us (14%)
  local copies, waits for them, and re-layouts  10.3 us (10%)
    all_to_all x1, starting transfers between devices, body(): spectrum = lax.all_to_all(spectrum, ('gx', 'gz'), 0, 0, tiled=True)  16 us
    all_to_all x1, waiting for transfers between devices, body(): spectrum = lax.all_to_all(spectrum, ('gx', 'gz'), 0, 0, tiled=True)  12.6 us
    ppermute x3, starting transfers between devices, both_ways(): lax.ppermute(high_edge, axis, up)  11.7 us
    ppermute x3, starting transfers between devices, both_ways(): lax.ppermute(low_edge, axis, down)  11.5 us
    all_to_all x1, starting transfers between devices, body(): spectrum = lax.all_to_all(spectrum, 'gy', 0, 0, tiled=True)  8.72 us
    unnamed x30, local copies, waits for them, and re-layouts  8.33 us
    all_to_all x1, starting transfers between devices, body(): charges = lax.all_to_all(charges, 'gy', 0, 0, tiled=True)  7.99 us
    pallas_call x1, Pallas kernels, body(): call(near_kernel, (CZ, CY, CX), [pltpu.VMEM((PZ, PY, LANES), f32), pltpu....  7.04 us
  transfers between devices with their start and end apart: 9, of which 4 were waited for; matrix products, arithmetic and copies ran while one was open for 2% of the time, Pallas kernels for 8%

profile of v1, /device:TPU:1, one launch (start us, length us, event | category | flops | bytes accessed | tf_op | source)
XLA Modules:
  0.0 102.5 jit_solution(17577172167743293318)
XLA Ops:
  0.0 0.0 copy-start
  0.0 1.0 %copy-done = f32[32,32,128]{2,1,0:T(8,128)S(1)} copy-done((f32[32,32,128]{2,1,0:T(8,128)S(1)}, f32[32,32,128]{2,1,0:T(8,128)}, u32[]{:S(2)}) %copy-start) | copy-done | bytes 524312
  1.0 1.1 %charges.1 = f32[16,16,128]{2,1,0:T(8,128)} custom-call(f32[32,32,128]{2,1,0:T(8,128)S(1)} %copy-done), custom_call_target="tpu_custom_call" | custom-call | tf_op jit(solution)/shard_map/charges/pallas_call | solution.py:361
  2.2 8.0 %all-to-all-start = ((f32[16,16,128]{2,1,0:T(8,128)}), f32[16,16,128]{2,1,0:T(8,128)S(1)}, u32[]{:S(2)}, u32[]{:S(2)}) async-start(f32[16,16,128]{2,1,0:T(8,128)} %charges.1), calls=%async_computation | async-start | bytes 262144 | tf_op jit(solution)/shard_map/all_to_all | solution.py:362
  10.2 1.0 fusion.1
  11.1 5.6 %collective-permute-start = (f32[8,32,128]{2,1,0:T(8,128)S(1)}, f32[8,32,128]{2,1,0:T(8,128)S(1)}, u32[]{:S(2)}, u32[]{:S(2)}) collective-permute-start(f32[8,32,128]{2,1,0:T(8,128)S(1)} %get-tuple-element.12), channel_id=1, source_target_pairs={{0,1},{1,2},{2,3},{3,0},{4,5},{5,6},{6,7},{7,4},{8,9},{9,10},{10,1... | collective-permute-start | bytes 393224 | tf_op jit(solution)/shard_map/ppermute | solution.py:352
  16.8 1.9 %collective-permute-start.1 = (f32[8,32,128]{2,1,0:T(8,128)S(1)}, f32[8,32,128]{2,1,0:T(8,128)S(1)}, u32[]{:S(2)}, u32[]{:S(2)}) collective-permute-start(f32[8,32,128]{2,1,0:T(8,128)S(1)} %get-tuple-element.11), channel_id=1, source_target_pairs={{1,0},{2,1},{3,2},{0,3},{5,4},{6,5},{7,6},{4,7},{9,8},{10,9},{11,1... | collective-permute-start | bytes 393224 | tf_op jit(solution)/shard_map/ppermute | solution.py:352
  18.7 0.0 all-to-all-done.charges
  18.7 0.0 copy-start.9
  18.7 0.9 copy-done.9
  19.6 0.9 first_y.1
  20.6 16.0 %all-to-all-start.1 = ((f32[32,16,128]{2,1,0:T(8,128)}), f32[32,16,128]{2,1,0:T(8,128)S(1)}, u32[]{:S(2)}, u32[]{:S(2)}) async-start(f32[32,16,128]{2,1,0:T(8,128)} %first_y.1), calls=%async_computation.1 | async-start | bytes 524288 | tf_op jit(solution)/shard_map/all_to_all | solution.py:383
  36.5 1.0 fusion
  37.5 0.0 copy-start.1
  37.5 0.0 collective-permute-done.below
  37.6 0.0 collective-permute-done.1.above
  37.6 12.6 %all-to-all-done.1.spectrum = f32[32,16,128]{2,1,0:T(8,128)S(1)} async-done(((f32[32,16,128]{2,1,0:T(8,128)}), f32[32,16,128]{2,1,0:T(8,128)S(1)}, u32[]{:S(2)}, u32[]{:S(2)}) %all-to-all-start.1) | async-done | bytes 262176 | tf_op jit(solution)/shard_map/all_to_all | solution.py:383
  50.2 0.0 copy-start.2
  50.2 2.2 %copy-done.2 = f32[16,256,256]{2,1,0:T(8,128)S(1)} copy-done((f32[16,256,256]{2,1,0:T(8,128)S(1)}, f32[16,256,256]{2,1,0:T(8,128)}, u32[]{:S(2)}) %copy-start.2) | copy-done | bytes 4194328
  52.4 1.2 %copy-done.3 = f32[8,256,128]{2,1,0:T(8,128)S(1)} copy-done((f32[8,256,128]{2,1,0:T(8,128)S(1)}, f32[8,256,128]{2,1,0:T(8,128)}, u32[]{:S(2)}) %copy-start.3) | copy-done | bytes 1048600
  53.6 1.0 copy-done.5
  54.6 0.9 copy-done.7
  55.5 0.9 copy-done.8
  56.5 0.0 copy-start.14
  56.5 3.2 %filter.1 = f32[16,32,128]{2,1,0:T(8,128)} custom-call(f32[256,256]{1,0:T(8,128)S(1)} %copy-done.7, f32[256,256]{1,0:T(8,128)S(1)} %copy-done.8, f32[16,256,256]{2,1,0:T(8,128)S(1)} %copy-done.2, f32[4,96,256]{2,1,0:T(8,128)S(1)} %copy-done.5, f32[8,256,128]{2,1,0:T(8,128)S(1)} %copy-done.3, f32[32,16,128]{2,1,0:T(8,128)S(1)} %all-to-all-done.1.spectrum), custom_call_target="tpu_custom_call" | custom-call | tf_op jit(solution)/shard_map/filter/pallas_call | solution.py:384
  59.8 0.0 copy-start.6
  59.8 0.0 copy-start.11
  59.8 8.7 %all-to-all-start.2 = ((f32[16,32,128]{2,1,0:T(8,128)}), f32[16,32,128]{2,1,0:T(8,128)S(1)}, u32[]{:S(2)}, u32[]{:S(2)}) async-start(f32[16,32,128]{2,1,0:T(8,128)} %filter.1), calls=%async_computation.2 | async-start | bytes 524288 | tf_op jit(solution)/shard_map/all_to_all | solution.py:398
  68.5 3.3 %collective-permute-start.2 = (f32[48,8,128]{2,1,0:T(8,128)S(1)}, f32[48,8,128]{2,1,0:T(8,128)S(1)}, u32[]{:S(2)}, u32[]{:S(2)}) collective-permute-start(f32[48,8,128]{2,1,0:T(8,128)S(1)} %pad_maximum_fusion), channel_id=1, source_target_pairs={{0,4},{4,8},{8,12},{12,16},{16,20},{20,24},{24,28},{28,32},{32,36}... | collective-permute-start | bytes 589832 | tf_op jit(solution)/shard_map/ppermute | solution.py:352
  71.8 5.9 %collective-permute-start.3 = (f32[48,8,128]{2,1,0:T(8,128)S(1)}, f32[48,8,128]{2,1,0:T(8,128)S(1)}, u32[]{:S(2)}, u32[]{:S(2)}) collective-permute-start(f32[48,8,128]{2,1,0:T(8,128)S(1)} %pad_maximum_fusion.1), channel_id=1, source_target_pairs={{4,0},{8,4},{12,8},{16,12},{20,16},{24,20},{28,24},{32,28},{36,32}... | collective-permute-start | bytes 589832 | tf_op jit(solution)/shard_map/ppermute | solution.py:352
  77.8 3.4 %collective-permute-done.2.before = f32[48,8,128]{2,1,0:T(8,128)S(1)} collective-permute-done((f32[48,8,128]{2,1,0:T(8,128)S(1)}, f32[48,8,128]{2,1,0:T(8,128)S(1)}, u32[]{:S(2)}, u32[]{:S(2)}) %collective-permute-start.2) | collective-permute-done | bytes 196640 | tf_op jit(solution)/shard_map/ppermute | solution.py:352
  81.2 3.5 %collective-permute-done.3.after = f32[48,8,128]{2,1,0:T(8,128)S(1)} collective-permute-done((f32[48,8,128]{2,1,0:T(8,128)S(1)}, f32[48,8,128]{2,1,0:T(8,128)S(1)}, u32[]{:S(2)}, u32[]{:S(2)}) %collective-permute-start.3) | collective-permute-done | bytes 196640 | tf_op jit(solution)/shard_map/ppermute | solution.py:352
  84.7 0.0 copy-done.1
  84.7 0.6 edges.1
  85.3 2.9 %collective-permute-start.4 = (f32[144,128]{1,0:T(8,128)S(1)}, f32[144,128]{1,0:T(8,128)S(1)}, u32[]{:S(2)}, u32[]{:S(2)}) collective-permute-start(f32[144,128]{1,0:T(8,128)S(1)} %get-tuple-element.7), channel_id=1, source_target_pairs={{0,64},{64,128},{128,192},{192,256},{256,320},{320,384},{384,448},... | collective-permute-start | bytes 221192 | tf_op jit(solution)/shard_map/ppermute | solution.py:352
  88.2 3.6 %collective-permute-start.5 = (f32[144,128]{1,0:T(8,128)S(1)}, f32[144,128]{1,0:T(8,128)S(1)}, u32[]{:S(2)}, u32[]{:S(2)}) collective-permute-start(f32[144,128]{1,0:T(8,128)S(1)} %get-tuple-element.8), channel_id=1, source_target_pairs={{64,0},{128,64},{192,128},{256,192},{320,256},{384,320},{448,384},... | collective-permute-start | bytes 221192 | tf_op jit(solution)/shard_map/ppermute | solution.py:352
  91.9 0.0 collective-permute-done.4.left
  91.9 1.7 %collective-permute-done.5.right = f32[144,128]{1,0:T(8,128)S(1)} collective-permute-done((f32[144,128]{1,0:T(8,128)S(1)}, f32[144,128]{1,0:T(8,128)S(1)}, u32[]{:S(2)}, u32[]{:S(2)}) %collective-permute-start.5) | collective-permute-done | bytes 73760 | tf_op jit(solution)/shard_map/ppermute | solution.py:352
  93.6 0.0 copy-done.4
  93.6 0.0 copy-done.10
  93.6 0.0 copy-done.12
  93.6 0.0 copy-done.13
  93.6 0.0 copy-done.14
  93.6 7.0 %near.1 = f32[32,32,128]{2,1,0:T(8,128)S(1)} custom-call(f32[32,32,128]{2,1,0:T(8,128)S(1)} %copy-done.1, f32[8,32,128]{2,1,0:T(8,128)S(1)} %collective-permute-done.below, f32[8,32,128]{2,1,0:T(8,128)S(1)} %collective-permute-done.1.above, f32[48,8,128]{2,1,0:T(8,128)S(1)} %collective-permute-done.2.before, f32[48,8,128]{2,1,0:T(8,128)S(1)} %collective-permute-done.3.after, ...), custom_call_target="tpu_custom_call" | custom-call | tf_op jit(solution)/shard_map/near/pallas_call | solution.py:400
  100.7 0.0 all-to-all-done.2.spectrum
  100.7 0.0 copy-done.6
  100.7 0.0 copy-done.11
  100.7 1.8 %last.1 = f32[32,32,128]{2,1,0:T(8,128)} custom-call(f32[16,32,128]{2,1,0:T(8,128)S(1)} %copy-done.6, f32[128,384]{1,0:T(8,128)S(1)} %copy-done.11, f32[16,32,128]{2,1,0:T(8,128)S(1)} %all-to-all-done.2.spectrum, f32[32,32,128]{2,1,0:T(8,128)S(1)} %near.1), custom_call_target="tpu_custom_call" | custom-call | tf_op jit(solution)/shard_map/last/pallas_call | solution.py:412
  (12 shorter events, 0.1 us)
Async XLA Ops:
  0.0 1.0 %copy-start = (f32[32,32,128]{2,1,0:T(8,128)S(1)}, f32[32,32,128]{2,1,0:T(8,128)}, u32[]{:S(2)}) copy-start(f32[32,32,128]{2,1,0:T(8,128)} %density.5) | copy-start | bytes 1572868
  2.2 16.5 %all-to-all-start = ((f32[16,16,128]{2,1,0:T(8,128)}), f32[16,16,128]{2,1,0:T(8,128)S(1)}, u32[]{:S(2)}, u32[]{:S(2)}) async-start(f32[16,16,128]{2,1,0:T(8,128)} %charges.1), calls=%async_computation | async-start | bytes 262144 | tf_op jit(solution)/shard_map/all_to_all | solution.py:362
  11.1 26.4 %collective-permute-start = (f32[8,32,128]{2,1,0:T(8,128)S(1)}, f32[8,32,128]{2,1,0:T(8,128)S(1)}, u32[]{:S(2)}, u32[]{:S(2)}) collective-permute-start(f32[8,32,128]{2,1,0:T(8,128)S(1)} %get-tuple-element.12), channel_id=1, source_target_pairs={{0,1},{1,2},{2,3},{3,0},{4,5},{5,6},{6,7},{7,4},{8,9},{9,10},{10,1... | collective-permute-start | bytes 393224 | tf_op jit(solution)/shard_map/ppermute | solution.py:352
  16.8 20.8 %collective-permute-start.1 = (f32[8,32,128]{2,1,0:T(8,128)S(1)}, f32[8,32,128]{2,1,0:T(8,128)S(1)}, u32[]{:S(2)}, u32[]{:S(2)}) collective-permute-start(f32[8,32,128]{2,1,0:T(8,128)S(1)} %get-tuple-element.11), channel_id=1, source_target_pairs={{1,0},{2,1},{3,2},{0,3},{5,4},{6,5},{7,6},{4,7},{9,8},{10,9},{11,1... | collective-permute-start | bytes 393224 | tf_op jit(solution)/shard_map/ppermute | solution.py:352
  18.7 1.0 copy-start.9
  20.6 29.6 %all-to-all-start.1 = ((f32[32,16,128]{2,1,0:T(8,128)}), f32[32,16,128]{2,1,0:T(8,128)S(1)}, u32[]{:S(2)}, u32[]{:S(2)}) async-start(f32[32,16,128]{2,1,0:T(8,128)} %first_y.1), calls=%async_computation.1 | async-start | bytes 524288 | tf_op jit(solution)/shard_map/all_to_all | solution.py:383
  37.5 47.2 %copy-start.1 = (f32[32,32,128]{2,1,0:T(8,128)S(1)}, f32[32,32,128]{2,1,0:T(8,128)}, u32[]{:S(2)}) copy-start(f32[32,32,128]{2,1,0:T(8,128)} %density.5) | copy-start | bytes 1572868
  50.2 2.2 %copy-start.2 = (f32[16,256,256]{2,1,0:T(8,128)S(1)}, f32[16,256,256]{2,1,0:T(8,128)}, u32[]{:S(2)}) copy-start(f32[16,256,256]{2,1,0:T(8,128)} %constant.29.clone.gain) | copy-start | bytes 12582916
  52.4 1.2 %copy-start.3 = (f32[8,256,128]{2,1,0:T(8,128)S(1)}, f32[8,256,128]{2,1,0:T(8,128)}, u32[]{:S(2)}) copy-start(f32[8,256,128]{2,1,0:T(8,128)} %constant.31.clone.out_x) | copy-start | bytes 3145732
  53.6 1.0 copy-start.5
  54.6 0.9 copy-start.7
  55.5 0.9 copy-start.8
  56.5 37.1 %copy-start.4 = (f32[9,48,256]{2,1,0:T(8,128)S(1)}, f32[9,48,256]{2,1,0:T(8,128)}, u32[]{:S(2)}) copy-start(f32[9,48,256]{2,1,0:T(8,128)} %constant.34.clone.gains) | copy-start | bytes 1327108
  56.5 37.1 %copy-start.10 = (bf16[512,256]{1,0:T(8,128)(2,1)S(1)}, bf16[512,256]{1,0:T(8,128)(2,1)}, u32[]{:S(2)}) copy-start(bf16[512,256]{1,0:T(8,128)(2,1)} %constant.35.clone.into_x) | copy-start | bytes 786436
  56.5 37.1 %copy-start.12 = (bf16[768,128]{1,0:T(8,128)(2,1)S(1)}, bf16[768,128]{1,0:T(8,128)(2,1)}, u32[]{:S(2)}) copy-start(bf16[768,128]{1,0:T(8,128)(2,1)} %constant.38.clone.out_x) | copy-start | bytes 589828
  56.5 37.1 %copy-start.13 = (bf16[48,144]{1,0:T(8,128)(2,1)S(1)}, bf16[48,144]{1,0:T(8,128)(2,1)}, u32[]{:S(2)}) copy-start(bf16[48,144]{1,0:T(8,128)(2,1)} %constant.36.clone.into_y) | copy-start | bytes 41476
  56.5 37.1 %copy-start.14 = (bf16[32,144]{1,0:T(8,128)(2,1)S(1)}, bf16[32,144]{1,0:T(8,128)(2,1)}, u32[]{:S(2)}) copy-start(bf16[32,144]{1,0:T(8,128)(2,1)} %constant.37.clone.out_y) | copy-start | bytes 27652
  59.8 40.9 %copy-start.6 = (f32[16,32,128]{2,1,0:T(8,128)S(1)}, f32[16,32,128]{2,1,0:T(8,128)}, u32[]{:S(2)}) copy-start(f32[16,32,128]{2,1,0:T(8,128)} %constant.32.clone.last_y) | copy-start | bytes 786436
  59.8 40.9 %copy-start.11 = (f32[128,384]{1,0:T(8,128)S(1)}, f32[128,384]{1,0:T(8,128)}, u32[]{:S(2)}) copy-start(f32[128,384]{1,0:T(8,128)} %constant.33.clone.last_x) | copy-start | bytes 589828
  59.8 40.9 %all-to-all-start.2 = ((f32[16,32,128]{2,1,0:T(8,128)}), f32[16,32,128]{2,1,0:T(8,128)S(1)}, u32[]{:S(2)}, u32[]{:S(2)}) async-start(f32[16,32,128]{2,1,0:T(8,128)} %filter.1), calls=%async_computation.2 | async-start | bytes 524288 | tf_op jit(solution)/shard_map/all_to_all | solution.py:398
  68.5 12.6 %collective-permute-start.2 = (f32[48,8,128]{2,1,0:T(8,128)S(1)}, f32[48,8,128]{2,1,0:T(8,128)S(1)}, u32[]{:S(2)}, u32[]{:S(2)}) collective-permute-start(f32[48,8,128]{2,1,0:T(8,128)S(1)} %pad_maximum_fusion), channel_id=1, source_target_pairs={{0,4},{4,8},{8,12},{12,16},{16,20},{20,24},{24,28},{28,32},{32,36}... | collective-permute-start | bytes 589832 | tf_op jit(solution)/shard_map/ppermute | solution.py:352
  71.8 12.9 %collective-permute-start.3 = (f32[48,8,128]{2,1,0:T(8,128)S(1)}, f32[48,8,128]{2,1,0:T(8,128)S(1)}, u32[]{:S(2)}, u32[]{:S(2)}) collective-permute-start(f32[48,8,128]{2,1,0:T(8,128)S(1)} %pad_maximum_fusion.1), channel_id=1, source_target_pairs={{4,0},{8,4},{12,8},{16,12},{20,16},{24,20},{28,24},{32,28},{36,32}... | collective-permute-start | bytes 589832 | tf_op jit(solution)/shard_map/ppermute | solution.py:352
  85.3 6.5 %collective-permute-start.4 = (f32[144,128]{1,0:T(8,128)S(1)}, f32[144,128]{1,0:T(8,128)S(1)}, u32[]{:S(2)}, u32[]{:S(2)}) collective-permute-start(f32[144,128]{1,0:T(8,128)S(1)} %get-tuple-element.7), channel_id=1, source_target_pairs={{0,64},{64,128},{128,192},{192,256},{256,320},{320,384},{384,448},... | collective-permute-start | bytes 221192 | tf_op jit(solution)/shard_map/ppermute | solution.py:352
  88.2 5.4 %collective-permute-start.5 = (f32[144,128]{1,0:T(8,128)S(1)}, f32[144,128]{1,0:T(8,128)S(1)}, u32[]{:S(2)}, u32[]{:S(2)}) collective-permute-start(f32[144,128]{1,0:T(8,128)S(1)} %get-tuple-element.8), channel_id=1, source_target_pairs={{64,0},{128,64},{192,128},{256,192},{320,256},{384,320},{448,384},... | collective-permute-start | bytes 221192 | tf_op jit(solution)/shard_map/ppermute | solution.py:352

commit v2 on v1

v2 whole, which is shorter than its diff:
```python
import math

import jax
import jax.numpy as jnp
import ml_dtypes
import numpy as np
from jax import lax
from jax.experimental import pallas as pl
from jax.experimental.pallas import tpu as pltpu
from jax.sharding import PartitionSpec as P

HALO = 8
COARSEN = 4
SCREEN = 6.0
SOFTEN = 0.25

NZ, NY, NX = 128, 512, 1024
GZ, GY, GX = 4, 16, 8
CZ, CY, CX = NZ // GZ, NY // GY, NX // GX
MZ, MY, MX = NZ // COARSEN, NY // COARSEN, NX // COARSEN
BZ, BY, BX = MZ // GZ, MY // GY, MX // GX
PZ, PY, PX = CZ + 2 * HALO, CY + 2 * HALO, CX + 2 * HALO
LANES = 256
GROUP = 3 * PY
BORDER = BY + 2
SHARE = 2 * GX
KX = MX // SHARE

f32 = jnp.float32
bf16 = jnp.bfloat16
HIGHEST = lax.Precision.HIGHEST


def cas(a, b, points):
    angles = 2.0 * np.pi / points * (np.outer(a, b) % points)
    return np.cos(angles) + np.sin(angles)


def split(table):
    high = table.astype(np.float32).astype(ml_dtypes.bfloat16)
    low = (table - high.astype(np.float64)).astype(np.float32).astype(ml_dtypes.bfloat16)
    return high, low


def near_tables():
    reach = np.arange(HALO + 1)
    both = np.arange(-HALO, HALO + 1)
    squared = (
        reach[:, None, None] ** 2 + both[None, :, None] ** 2 + both[None, None, :] ** 2
    ).astype(np.float64)
    erfc = np.vectorize(math.erfc)
    kernel = erfc(np.sqrt(squared) / SCREEN) / (4.0 * math.pi * np.sqrt(squared + SOFTEN))
    cos_y = np.cos(2.0 * np.pi / PY * np.outer(np.arange(PY), both))
    cos_x = np.cos(2.0 * np.pi / PX * np.outer(np.arange(PX), both))
    spectral = np.einsum("dab,ka,lb->dkl", kernel, cos_y, cos_x) / (PY * PX)
    gains = np.zeros((HALO + 1, PY, LANES))
    gains[:, :, :PX] = spectral

    every_x, every_y = np.arange(PX), np.arange(PY)
    forward_x = np.zeros((PX, LANES))
    forward_x[:, :PX] = cas(every_x, every_x, PX)
    high, low = split(forward_x)
    own = slice(HALO, HALO + CX)
    ends = np.r_[0:HALO, HALO + CX : PX]
    into_x = np.zeros((512, LANES), ml_dtypes.bfloat16)
    into_x[0:128], into_x[128:256], into_x[256:384] = high[own], low[own], high[own]
    into_x[384:400], into_x[400:416], into_x[416:432] = high[ends], low[ends], high[ends]

    high, low = split(cas(every_y, every_y, PY))
    into_y = np.concatenate([high, low, high], axis=1)
    out_y = into_y[HALO : HALO + CY]

    back_x = np.zeros((LANES, CX))
    back_x[:PX] = cas(every_x, every_x[own], PX)
    high, low = split(back_x)
    out_x = np.concatenate([high, low, high], axis=0)
    return gains.astype(np.float32), into_x, into_y, out_y, out_x


def far_tables():
    full_x = cas(np.arange(MX), np.arange(MX), MX)
    full_y = cas(np.arange(MY), np.arange(MY), MY)
    full_z = cas(np.arange(MZ), np.arange(MZ), MZ)

    first_x = np.tile(full_x.reshape(MX, SHARE, KX).transpose(1, 0, 2), (1, 1, 8))
    into_z = np.kron(full_z, np.eye(8))

    def waves(points):
        index = np.arange(points)
        signed = (index + points // 2) % points - points // 2
        laplace = 2.0 - 2.0 * np.cos(2.0 * np.pi / points * index)
        return laplace, (2.0 * np.pi / (points * COARSEN) * signed) ** 2

    (lap_z, wave_z), (lap_y, wave_y), (lap_x, wave_x) = waves(MZ), waves(MY), waves(MX)
    laplace = lap_z[:, None, None] + lap_y[None, :, None] + lap_x[None, None, :]
    wave = wave_z[:, None, None] + wave_y[None, :, None] + wave_x[None, None, :]
    laplace[0, 0, 0] = 1.0
    gain = np.exp(-(SCREEN * SCREEN / 4.0) * wave) / (COARSEN * laplace)
    gain[0, 0, 0] = 0.0
    gain = gain / (MZ * MY * MX)
    gain = gain.reshape(MZ, MY, SHARE, 2, 8).transpose(2, 0, 4, 3, 1).reshape(SHARE, MZ * 8, 2 * MY)

    out_z = np.zeros((2, 2 * BORDER * 8, MZ * 8))
    for g in range(2):
        z = np.concatenate([(2 * g + c) * BZ - 1 + np.arange(BORDER) for c in range(2)]) % MZ
        out_z[g] = np.kron(full_z[z], np.eye(8))

    out_y = np.zeros((GY, MY, 128))
    for g in range(GY):
        out_y[g, :, :BORDER] = full_y[:, (g * BY - 1 + np.arange(BORDER)) % MY]

    def refine(coarse):
        matrix = np.zeros((COARSEN * coarse, coarse + 2))
        for fine in range(COARSEN * coarse):
            below, t = fine // COARSEN, (fine % COARSEN + 0.5) / COARSEN - 0.5
            matrix[fine, below + 1] = 1.0 - abs(t)
            matrix[fine, below if t < 0 else below + 2] = abs(t)
        return matrix

    last_x = np.zeros((GX, MX, CX))
    for g in range(GX):
        last_x[g] = full_x[:, (g * BX - 1 + np.arange(BX + 2)) % MX] @ refine(BX).T
    last_y = np.zeros((BORDER * CY, 128))
    last_y[:, : BORDER * BORDER] = np.kron(np.eye(BORDER), refine(BY))
    tables = first_x, full_y, into_z, gain, out_z, out_y, last_x, last_y
    return tuple(table.astype(np.float32) for table in tables)


def dot(a, b):
    return jnp.dot(a, b, preferred_element_type=f32)


def exact_dot(a, b):
    return jnp.dot(a, b, preferred_element_type=f32, precision=HIGHEST)


def halves(x):
    high = x.astype(bf16)
    return high, (x - high.astype(f32)).astype(bf16)


def lane(shape):
    return lax.broadcasted_iota(jnp.int32, shape, len(shape) - 1)


def transposed_dot(a, b):
    return lax.dot_general(a, b, (((0,), (0,)), ((), ())), preferred_element_type=f32, precision=HIGHEST)


def share():
    return lax.axis_index("gx") * 2 + lax.axis_index("core")


def is_even(axis):
    return lax.rem(lax.axis_index(axis), 2) == 0


def charge_kernel(density, out, even, odd):
    parts = []
    for high in range(2):
        planes = []
        for low in range(4):
            z = (high * 4 + low) * COARSEN
            planes.append((density[z] + density[z + 1]) + (density[z + 2] + density[z + 3]))
        parts.append(jnp.concatenate(planes, axis=1))
    rows = jnp.concatenate(parts, axis=0)

    def pool(shape, fine, coarse):
        a = lax.broadcasted_iota(jnp.int32, shape, fine)
        b = lax.broadcasted_iota(jnp.int32, shape, coarse)
        return (a // COARSEN == b).astype(f32)

    rows = exact_dot(rows, pool((4 * CX, 128), 0, 1))
    rows = exact_dot(pool((2 * BY, 2 * CY), 1, 0), rows)
    for peer in range(SHARE):
        out[peer] = rows
    start = jnp.where(is_even("core"), CZ - HALO, 0)
    even[...] = density[pl.ds(start, HALO)]
    odd[...] = density[pl.ds(CZ - HALO - start, HALO)]


def first_kernel(table, charges, out, held, sem):
    copy = pltpu.make_async_copy(table.at[share()], held, sem)
    copy.start()
    peers = charges[...].reshape(GX, 32, 128)
    place = lane((32, 128)) // BX
    blocks = []
    for low in range(4):
        sides = []
        for side in range(2):
            total = None
            for q in range(4):
                shift = (q - low) * BX % 128
                peer = peers[side * 4 + q]
                moved = pltpu.roll(peer, shift, 1) if shift else peer
                total = moved if q == 0 else jnp.where(place == q, moved, total)
            sides.append(total)
        blocks.append(jnp.concatenate(sides, axis=1))
    rows = jnp.concatenate(blocks, axis=0)
    copy.wait()
    rows = exact_dot(rows, held[...])
    place = lane((BY, 128)) // KX
    for core in range(2):
        total = None
        for z in range(BZ):
            start = (z % 4) * 32 + core * 16 + (z // 4) * 8
            piece = rows[start : start + 8]
            total = piece if z == 0 else jnp.where(place == z, piece, total)
        for peer in range(2 * GY):
            out[peer, core] = total


def filter_kernel(
    full_y, into_z, gain, out_z, out_y, spectrum, out, held_y, held_z, held_g, held_iz, held_iy, sems
):
    sources = (
        (full_y, held_y),
        (into_z, held_z),
        (gain.at[share()], held_g),
        (out_z.at[lax.axis_index("yh")], held_iz),
        (out_y.at[lax.axis_index("gy")], held_iy),
    )
    copies = [
        pltpu.make_async_copy(source, held, sems.at[i]) for i, (source, held) in enumerate(sources)
    ]
    for copy in copies:
        copy.start()
    blocks = spectrum[...].reshape(GY, 4, BY, 128)
    copies[0].wait()
    waves = [transposed_dot(blocks[:, b].reshape(MY, 128), held_y[...]) for b in range(4)]
    rows = jnp.concatenate(waves, axis=0).reshape(MZ, 2, 8, MY)
    rows = jnp.concatenate([rows[:, half].reshape(MZ * 8, MY) for half in range(2)], axis=1)
    copies[1].wait()
    rows = exact_dot(held_z[...], rows)
    copies[2].wait()
    rows = rows * held_g[...]
    copies[3].wait()
    rows = exact_dot(held_iz[...], rows)
    copies[4].wait()
    rows = jnp.concatenate([rows[:, :MY], rows[:, MY:]], axis=0)
    rows = exact_dot(rows, held_iy[...])
    for core in range(2):
        sides = []
        for half in range(2):
            total = None
            for z in range(BORDER):
                start = ((half * 2 + core) * BORDER + z) * 8
                piece = rows[start : start + 8]
                total = piece if z == 0 else total + pltpu.roll(piece, z * BORDER, 1)
            sides.append(total)
        message = jnp.concatenate(sides, axis=0)
        for peer in range(GX):
            out[peer * 2 + core] = message


def last_kernel(last_x, last_y, spectrum, near, out, held_x, held_y, sems):
    copies = [
        pltpu.make_async_copy(last_x.at[lax.axis_index("gx")], held_x, sems.at[0]),
        pltpu.make_async_copy(last_y, held_y, sems.at[1]),
    ]
    for copy in copies:
        copy.start()
    rows = spectrum[...].reshape(MX, 128)
    copies[0].wait()
    field = transposed_dot(rows, held_x[...])
    copies[1].wait()
    field = exact_dot(held_y[...], field)

    def plane(z):
        return field[z * CY : (z + 1) * CY]

    for block in range(BZ):
        before, here, after = plane(block), plane(block + 1), plane(block + 2)
        for residue in range(COARSEN):
            t = (residue + 0.5) / COARSEN - 0.5
            value = (1.0 - abs(t)) * here + abs(t) * (before if t < 0 else after)
            z = block * COARSEN + residue
            out[z] = near[z] + value


def edge_y_kernel(density, z_even, z_odd, even, odd):
    lower = is_even("core")
    start = jnp.where(is_even("gy"), CY - HALO, 0)
    for target, first in ((even, start), (odd, CY - HALO - start)):
        rows = pl.ds(pl.multiple_of(first, 8), HALO)
        one, two = z_even[:, rows], z_odd[:, rows]
        target[0:HALO] = jnp.where(lower, two, one)
        target[HALO : HALO + CZ] = density[:, rows]
        target[HALO + CZ : PZ] = jnp.where(lower, one, two)


def edge_x_kernel(density, z_even, z_odd, y_even, y_odd, padded, even, odd):
    lower = is_even("core")
    one, two = z_even[...], z_odd[...]
    middle = slice(HALO, HALO + CY)
    padded[0:HALO, middle] = jnp.where(lower, two, one)
    padded[HALO : HALO + CZ, middle] = density[...]
    padded[HALO + CZ : PZ, middle] = jnp.where(lower, one, two)
    lower = is_even("gy")
    one, two = y_even[...], y_odd[...]
    padded[:, 0:HALO] = jnp.where(lower, two, one)
    padded[:, HALO + CY : PY] = jnp.where(lower, one, two)

    place = lane((GROUP, 128)) // HALO
    left = right = jnp.zeros((GROUP, 128), f32)
    for j in range(16):
        rows = padded[3 * j : 3 * j + 3].reshape(GROUP, 128)
        shift = j * HALO
        left = jnp.where(place == j, pltpu.roll(rows, shift, 1) if shift else rows, left)
        shift = (j * HALO - (CX - HALO)) % 128
        right = jnp.where(place == j, pltpu.roll(rows, shift, 1) if shift else rows, right)
    lower = is_even("gx")
    even[...] = jnp.where(lower, right, left)
    odd[...] = jnp.where(lower, left, right)


def near_kernel(
    padded, x_even, x_odd, gains, into_x, into_y, out_y, out_x, out, wave_x, wave_y, wave_z
):
    lanes = lane((GROUP, 128))
    lower = is_even("gx")
    one, two = x_even[...], x_odd[...]
    left, right = jnp.where(lower, two, one), jnp.where(lower, one, two)
    for j in range(16):
        rows = padded[3 * j : 3 * j + 3].reshape(GROUP, 128)
        to_left, to_right = (-HALO * j) % 128, (HALO - HALO * j) % 128
        ends = jnp.where(
            lanes < HALO,
            pltpu.roll(left, to_left, 1) if to_left else left,
            pltpu.roll(right, to_right, 1) if to_right else right,
        )
        ends = jnp.where(lanes < 2 * HALO, ends, 0.0)
        high = ends.astype(bf16).astype(f32)
        low = ends - high
        ends = (high + pltpu.roll(high, 2 * HALO, 1) + pltpu.roll(low, 4 * HALO, 1)).astype(bf16)
        high, low = halves(rows)
        wave = dot(jnp.concatenate([high, high, low, ends], axis=1), into_x[...])
        for i in range(3):
            wave_x[3 * j + i] = wave[i * PY : (i + 1) * PY]

    @pl.loop(0, PZ, unroll=8)
    def _(z):
        high, low = halves(wave_x[z])
        wave_y[z] = dot(into_y[...], jnp.concatenate([high, high, low], axis=0))

    @pl.loop(0, PY // 8)
    def _(c):
        row = pl.ds(pl.multiple_of(c * 8, 8), 8)
        for side in range(LANES // 128):
            column = pl.ds(side * 128, 128)
            gain = [gains[d, row, column] for d in range(HALO + 1)]
            window = [wave_y[z, row, column] for z in range(2 * HALO)]
            for z in range(CZ):
                window.append(wave_y[z + 2 * HALO, row, column])
                total = gain[0] * window[HALO]
                for d in range(1, HALO + 1):
                    total = total + gain[d] * (window[HALO - d] + window[HALO + d])
                wave_z[z, row, column] = total
                window.pop(0)

    @pl.loop(0, CZ // 4, unroll=2)
    def _(step):
        rows = []
        for i in range(4):
            high, low = halves(wave_z[step * 4 + i])
            rows.append(dot(out_y[...], jnp.concatenate([high, high, low], axis=0)))
        high, low = halves(jnp.concatenate(rows, axis=0))
        field = dot(jnp.concatenate([high, high, low], axis=1), out_x[...])
        for i in range(4):
            out[step * 4 + i] = field[i * CY : (i + 1) * CY]


def call(kernel, outs, scratch=(), specs=None, name=None):
    vmem = pl.BlockSpec(memory_space=pltpu.VMEM)
    many = isinstance(outs, list)
    return pl.pallas_call(
        kernel,
        out_shape=[jax.ShapeDtypeStruct(s, f32) for s in outs] if many else jax.ShapeDtypeStruct(outs, f32),
        in_specs=specs,
        out_specs=[vmem] * len(outs) if many else vmem,
        scratch_shapes=list(scratch),
        compiler_params=pltpu.CompilerParams(vmem_limit_bytes=40 * 1024 * 1024),
        name=name,
    )


def exchange(even, odd, axis):
    peers = lax.axis_size(axis)
    low_first = [(i, i + 1 if i % 2 == 0 else i - 1) for i in range(peers)]
    high_first = [(i, (i + 1 if i % 2 else i - 1) % peers) for i in range(peers)]
    odd = lax.ppermute(odd, axis, high_first)
    return lax.ppermute(even, axis, low_first), odd


def body(density):
    vmem, far = pl.BlockSpec(memory_space=pltpu.VMEM), pl.BlockSpec(memory_space=pltpu.HBM)
    dma = pltpu.SemaphoreType.DMA
    first_x, full_y, into_z, gain, out_z, out_y, last_x, last_y = (jnp.asarray(t) for t in far_tables())
    near_consts = [jnp.asarray(t) for t in near_tables()]

    charges, even, odd = call(
        charge_kernel, [(SHARE, 16, 128), (HALO, CY, CX), (HALO, CY, CX)], specs=[vmem], name="charges"
    )(density)
    charges = lax.all_to_all(charges, ("gx", "core"), 0, 0, tiled=True)
    z_ends = exchange(even, odd, ("yh", "core"))
    spectrum = call(
        first_kernel,
        (2 * GY, 2, 8, 128),
        [pltpu.VMEM((MX, 128), f32), dma],
        [far, vmem],
        name="first_x",
    )(first_x, charges)
    spectrum = lax.all_to_all(spectrum, ("gy", "yh"), 0, 0, tiled=True)

    y_ends = call(edge_y_kernel, [(PZ, HALO, CX)] * 2, specs=[vmem] * 3, name="edges_y")(density, *z_ends)
    y_ends = exchange(*y_ends, "gy")
    padded, even, odd = call(
        edge_x_kernel, [(PZ, PY, CX), (GROUP, 128), (GROUP, 128)], specs=[vmem] * 5, name="edges_x"
    )(density, *z_ends, *y_ends)
    x_ends = exchange(even, odd, "gx")

    spectrum, x_ends = lax.optimization_barrier((spectrum, x_ends))
    spectrum = call(
        filter_kernel,
        (SHARE, KX, 128),
        [
            pltpu.VMEM((MY, MY), f32),
            pltpu.VMEM((256, 256), f32),
            pltpu.VMEM((256, 256), f32),
            pltpu.VMEM((2 * BORDER * 8, 256), f32),
            pltpu.VMEM((MY, 128), f32),
            dma((5,)),
        ],
        [far] * 5 + [vmem],
        name="filter",
    )(full_y, into_z, gain, out_z, out_y, spectrum)
    spectrum = lax.all_to_all(spectrum, ("gx", "core"), 0, 0, tiled=True)

    near = call(
        near_kernel,
        (CZ, CY, CX),
        [
            pltpu.VMEM((PZ, PY, LANES), f32),
            pltpu.VMEM((PZ, PY, LANES), f32),
            pltpu.VMEM((CZ, PY, LANES), f32),
        ],
        [vmem] * 8,
        name="near",
    )(padded, *x_ends, *near_consts)

    return call(
        last_kernel,
        (CZ, CY, CX),
        [pltpu.VMEM((MX, CX), f32), pltpu.VMEM((BORDER * CY, 128), f32), dma((2,))],
        [far, far, vmem, vmem],
        name="last",
    )(last_x, last_y, spectrum, near)


def solution(mesh):
    devices = mesh.devices.reshape(GX, GY, 2, 2)
    parts = jax.sharding.Mesh(devices, ("gx", "gy", "yh", "core"))
    placed = P(("yh", "core"), "gy", "gx")
    return jax.shard_map(body, mesh=parts, in_specs=(placed,), out_specs=placed, check_vma=False)
```

time: 104 us -> 106 us (1.019)
  blocking collectives: 0 us -> 20.8 us
  starting transfers between devices: 55.9 us -> 39.5 us
  waiting for transfers between devices: 21.3 us -> 17.7 us
  local copies, waits for them, and re-layouts: 10.3 us -> 12.6 us
    all_to_all x0 -> x1, blocking collectives: none -> 20.8 us  [body(): charges = lax.all_to_all(charges, ('gx', 'core'), 0, 0, tiled=True)]
    all_to_all x3 -> x2, starting transfers between devices: 32.7 us -> 17.2 us  [the longest x1 9.68 us: body(): spectrum = lax.all_to_all(spectrum, ('gy', 'yh'), 0, 0, tiled=True)]
    all_to_all x3 -> x2, waiting for transfers between devices: 12.6 us -> 0.01 us  [the longest x1 0.01 us: body(): spectrum = lax.all_to_all(spectrum, ('gy', 'yh'), 0, 0, tiled=True)]
    ppermute x6, waiting for transfers between devices: 8.68 us -> 17.7 us  [the longest x3 17.2 us: exchange(): odd = lax.ppermute(odd, axis, high_first)]
    unnamed x30 -> x34, local copies, waits for them, and re-layouts: 8.33 us -> 12.6 us
    slice x4 -> x0, local copies, waits for them, and re-layouts: 1.99 us -> none  [the longest x1 0.99 us: edge(): density[:, rows]]
    pallas_call x5 -> x6, Pallas kernels: 7.72 us -> 7.23 us  [the longest x1 2.96 us: body(): call(filter_kernel, (SHARE, KX, 128), [pltpu.VMEM((MY, MY), f32), pltpu.V...]
  transfers between devices with their start and end apart: 9 -> 8, of which waited for: 4 -> 4; matrix products, arithmetic and copies ran while one was open for 2% -> 0% of each run, Pallas kernels for 8% -> 7%
where the time goes in v2:
time: 106 us; the launch traced here: 105 us
  starting transfers between devices  39.5 us (37%)
  blocking collectives  20.8 us (20%)
  waiting for transfers between devices  17.7 us (17%)
  Pallas kernels  14.3 us (13%)
  local copies, waits for them, and re-layouts  12.6 us (12%)
    all_to_all x1, blocking collectives, body(): charges = lax.all_to_all(charges, ('gx', 'core'), 0, 0, tiled=True)  20.8 us
    ppermute x3, waiting for transfers between devices, exchange(): odd = lax.ppermute(odd, axis, high_first)  17.2 us
    ppermute x3, starting transfers between devices, exchange(): odd = lax.ppermute(odd, axis, high_first)  15.7 us
    unnamed x34, local copies, waits for them, and re-layouts  12.6 us
    all_to_all x1, starting transfers between devices, body(): spectrum = lax.all_to_all(spectrum, ('gy', 'yh'), 0, 0, tiled=True)  9.68 us
    all_to_all x1, starting transfers between devices, body(): spectrum = lax.all_to_all(spectrum, ('gx', 'core'), 0, 0, tiled=True)  7.5 us
    pallas_call x1, Pallas kernels, body(): call(near_kernel, (CZ, CY, CX), [pltpu.VMEM((PZ, PY, LANES), f32), pltpu....  7.04 us
    ppermute x3, starting transfers between devices, exchange(): return (lax.ppermute(even, axis, low_first), odd)  6.59 us
  transfers between devices with their start and end apart: 8, of which 4 were waited for; matrix products, arithmetic and copies ran while one was open for 0% of the time, Pallas kernels for 7%

profile of v2, /device:TPU:1, one launch (start us, length us, event | category | flops | bytes accessed | tf_op | source)
XLA Modules:
  0.0 105.1 jit_solution(4768611387028297715)
XLA Ops:
  0.0 0.0 copy-start
  0.0 1.0 copy-done
  1.0 0.0 copy-start.1
  1.0 0.5 charges.1
  1.5 20.8 %all_to_all.15.charges = f32[16,16,128]{2,1,0:T(8,128)S(1)} all-to-all(f32[16,16,128]{2,1,0:T(8,128)S(1)} %get-tuple-element.16), channel_id=1, replica_groups=mesh['gx'=8,'gy'=16,'yh'=2,'core'=2] {'gx','core'}, dimensions={0} | all-to-all | bytes 262144 | tf_op jit(solution)/shard_map/all_to_all | solution.py:404
  22.3 0.0 copy-start.3
  22.3 1.6 %copy-done.3 = f32[16,256,128]{2,1,0:T(8,128)S(1)} copy-done((f32[16,256,128]{2,1,0:T(8,128)S(1)}, f32[16,256,128]{2,1,0:T(8,128)}, u32[]{:S(2)}) %copy-start.3) | copy-done | bytes 2097176
  23.9 0.0 copy-start.5
  23.9 1.3 %first_x.1 = f32[32,2,8,128]{3,2,1,0:T(8,128)} custom-call(f32[16,256,128]{2,1,0:T(8,128)S(1)} %copy-done.3, f32[16,16,128]{2,1,0:T(8,128)S(1)} %all_to_all.15.charges), custom_call_target="tpu_custom_call" | custom-call | tf_op jit(solution)/shard_map/first_x/pallas_call | solution.py:406
  25.2 9.7 %all-to-all-start.1 = ((f32[32,2,8,128]{3,2,1,0:T(8,128)}), f32[32,2,8,128]{3,2,1,0:T(8,128)S(1)}, u32[]{:S(2)}, u32[]{:S(2)}) async-start(f32[32,2,8,128]{3,2,1,0:T(8,128)} %first_x.1), calls=%async_computation.1 | async-start | bytes 524288 | tf_op jit(solution)/shard_map/all_to_all | solution.py:413
  34.9 1.9 %collective-permute-start = (f32[8,32,128]{2,1,0:T(8,128)S(1)}, f32[8,32,128]{2,1,0:T(8,128)S(1)}, u32[]{:S(2)}, u32[]{:S(2)}) collective-permute-start(f32[8,32,128]{2,1,0:T(8,128)S(1)} %get-tuple-element.17), channel_id=1, source_target_pairs={{0,1},{1,0},{2,3},{3,2},{4,5},{5,4},{6,7},{7,6},{8,9},{9,8},{10,11... | collective-permute-start | bytes 393224 | tf_op jit(solution)/shard_map/ppermute | solution.py:392
  36.8 7.4 %collective-permute-start.1 = (f32[8,32,128]{2,1,0:T(8,128)S(1)}, f32[8,32,128]{2,1,0:T(8,128)S(1)}, u32[]{:S(2)}, u32[]{:S(2)}) collective-permute-start(f32[8,32,128]{2,1,0:T(8,128)S(1)} %get-tuple-element.18), channel_id=1, source_target_pairs={{0,3},{1,2},{2,1},{3,0},{4,7},{5,6},{6,5},{7,4},{8,11},{9,10},{10,... | collective-permute-start | bytes 393224 | tf_op jit(solution)/shard_map/ppermute | solution.py:391
  44.3 0.0 collective-permute-done.z_even
  44.3 8.0 %collective-permute-done.1.z_odd = f32[8,32,128]{2,1,0:T(8,128)S(1)} collective-permute-done((f32[8,32,128]{2,1,0:T(8,128)S(1)}, f32[8,32,128]{2,1,0:T(8,128)S(1)}, u32[]{:S(2)}, u32[]{:S(2)}) %collective-permute-start.1) | collective-permute-done | bytes 131104 | tf_op jit(solution)/shard_map/ppermute | solution.py:391
  52.3 0.0 copy-done.1
  52.3 0.1 edges_y.1
  52.3 2.4 %collective-permute-start.2 = (f32[48,8,128]{2,1,0:T(8,128)S(1)}, f32[48,8,128]{2,1,0:T(8,128)S(1)}, u32[]{:S(2)}, u32[]{:S(2)}) collective-permute-start(f32[48,8,128]{2,1,0:T(8,128)S(1)} %get-tuple-element.19), channel_id=1, source_target_pairs={{0,4},{4,0},{8,12},{12,8},{16,20},{20,16},{24,28},{28,24},{32,36},... | collective-permute-start | bytes 589832 | tf_op jit(solution)/shard_map/ppermute | solution.py:392
  54.8 5.0 %collective-permute-start.3 = (f32[48,8,128]{2,1,0:T(8,128)S(1)}, f32[48,8,128]{2,1,0:T(8,128)S(1)}, u32[]{:S(2)}, u32[]{:S(2)}) collective-permute-start(f32[48,8,128]{2,1,0:T(8,128)S(1)} %get-tuple-element.20), channel_id=1, source_target_pairs={{0,60},{4,8},{8,4},{12,16},{16,12},{20,24},{24,20},{28,32},{32,28}... | collective-permute-start | bytes 589832 | tf_op jit(solution)/shard_map/ppermute | solution.py:391
  59.8 0.5 collective-permute-done.2.y_even
  60.4 6.2 %collective-permute-done.3.y_odd = f32[48,8,128]{2,1,0:T(8,128)S(1)} collective-permute-done((f32[48,8,128]{2,1,0:T(8,128)S(1)}, f32[48,8,128]{2,1,0:T(8,128)S(1)}, u32[]{:S(2)}, u32[]{:S(2)}) %collective-permute-start.3) | collective-permute-done | bytes 196640 | tf_op jit(solution)/shard_map/ppermute | solution.py:391
  66.5 0.6 edges_x.1
  67.2 2.2 %collective-permute-start.4 = (f32[144,128]{1,0:T(8,128)S(1)}, f32[144,128]{1,0:T(8,128)S(1)}, u32[]{:S(2)}, u32[]{:S(2)}) collective-permute-start(f32[144,128]{1,0:T(8,128)S(1)} %get-tuple-element.21), channel_id=1, source_target_pairs={{0,64},{64,0},{128,192},{192,128},{256,320},{320,256},{384,448},{4... | collective-permute-start | bytes 221192 | tf_op jit(solution)/shard_map/ppermute | solution.py:392
  69.4 3.3 %collective-permute-start.5 = (f32[144,128]{1,0:T(8,128)S(1)}, f32[144,128]{1,0:T(8,128)S(1)}, u32[]{:S(2)}, u32[]{:S(2)}) collective-permute-start(f32[144,128]{1,0:T(8,128)S(1)} %get-tuple-element.22), channel_id=1, source_target_pairs={{0,448},{64,128},{128,64},{192,256},{256,192},{320,384},{384,320},... | collective-permute-start | bytes 221192 | tf_op jit(solution)/shard_map/ppermute | solution.py:391
  72.7 0.0 collective-permute-done.4.x_even
  72.7 3.0 %collective-permute-done.5.x_odd = f32[144,128]{1,0:T(8,128)S(1)} collective-permute-done((f32[144,128]{1,0:T(8,128)S(1)}, f32[144,128]{1,0:T(8,128)S(1)}, u32[]{:S(2)}, u32[]{:S(2)}) %collective-permute-start.5) | collective-permute-done | bytes 73760 | tf_op jit(solution)/shard_map/ppermute | solution.py:391
  75.7 0.6 copy-done.12
  76.4 0.0 all-to-all-done.1.spectrum
  76.4 0.0 copy-done.5
  76.4 2.2 %copy-done.2 = f32[16,256,256]{2,1,0:T(8,128)S(1)} copy-done((f32[16,256,256]{2,1,0:T(8,128)S(1)}, f32[16,256,256]{2,1,0:T(8,128)}, u32[]{:S(2)}) %copy-start.2) | copy-done | bytes 4194328
  78.6 1.0 copy-done.7
  79.5 0.9 copy-done.8
  80.5 0.8 copy-done.14
  81.3 3.0 %filter.1 = f32[16,16,128]{2,1,0:T(8,128)} custom-call(f32[128,128]{1,0:T(8,128)S(1)} %copy-done.14, f32[256,256]{1,0:T(8,128)S(1)} %copy-done.8, f32[16,256,256]{2,1,0:T(8,128)S(1)} %copy-done.2, f32[2,160,256]{2,1,0:T(8,128)S(1)} %copy-done.7, f32[16,128,128]{2,1,0:T(8,128)S(1)} %copy-done.5, f32[32,2,8,128]{3,2,1,0:T(8,128)S(1)} %all-to-all-done.1.spectrum), custom_call_target="tpu_custom_call" | custom-call | tf_op jit(solution)/shard_map/filter/pallas_call | solution.py:423
  84.3 0.0 copy-start.4
  84.3 7.5 %all-to-all-start.2 = ((f32[16,16,128]{2,1,0:T(8,128)}), f32[16,16,128]{2,1,0:T(8,128)S(1)}, u32[]{:S(2)}, u32[]{:S(2)}) async-start(f32[16,16,128]{2,1,0:T(8,128)} %filter.1), calls=%async_computation.2 | async-start | bytes 262144 | tf_op jit(solution)/shard_map/all_to_all | solution.py:437
  91.8 0.0 copy-done.6
  91.8 0.0 copy-done.15
  91.8 0.0 copy-start.9
  91.8 0.9 copy-done.9
  92.8 0.9 copy-done.10
  93.7 0.9 copy-done.13
  94.6 0.7 copy-done.16
  95.3 7.0 %near.1 = f32[32,32,128]{2,1,0:T(8,128)S(1)} custom-call(f32[48,48,128]{2,1,0:T(8,128)S(1)} %get-tuple-element.24.padded, f32[144,128]{1,0:T(8,128)S(1)} %collective-permute-done.4.x_even, f32[144,128]{1,0:T(8,128)S(1)} %copy-done.13, f32[9,48,256]{2,1,0:T(8,128)S(1)} %copy-done.6, bf16[512,256]{1,0:T(8,128)(2,1)S(1)} %copy-done.9, ...), custom_call_target="tpu_custom_call" | custom-call | tf_op jit(solution)/shard_map/near/pallas_call | solution.py:439
  102.4 0.0 all-to-all-done.2.spectrum
  102.4 0.0 copy-done.4
  102.4 0.0 copy-start.11
  102.4 0.9 copy-done.11
  103.3 1.8 %last.1 = f32[32,32,128]{2,1,0:T(8,128)} custom-call(f32[8,256,128]{2,1,0:T(8,128)S(1)} %copy-done.4, f32[320,128]{1,0:T(8,128)S(1)} %copy-done.11, f32[16,16,128]{2,1,0:T(8,128)S(1)} %all-to-all-done.2.spectrum, f32[32,32,128]{2,1,0:T(8,128)S(1)} %near.1), custom_call_target="tpu_custom_call" | custom-call | tf_op jit(solution)/shard_map/last/pallas_call | solution.py:451
  (10 shorter events, 0.0 us)
Async XLA Ops:
  0.0 1.0 copy-start
  1.0 51.2 %copy-start.1 = (f32[32,32,128]{2,1,0:T(8,128)S(1)}, f32[32,32,128]{2,1,0:T(8,128)}, u32[]{:S(2)}) copy-start(f32[32,32,128]{2,1,0:T(8,128)} %density.5) | copy-start | bytes 1572868
  22.3 1.6 %copy-start.3 = (f32[16,256,128]{2,1,0:T(8,128)S(1)}, f32[16,256,128]{2,1,0:T(8,128)}, u32[]{:S(2)}) copy-start(f32[16,256,128]{2,1,0:T(8,128)} %constant.26.clone.table) | copy-start | bytes 6291460
  23.9 52.5 %copy-start.5 = (f32[16,128,128]{2,1,0:T(8,128)S(1)}, f32[16,128,128]{2,1,0:T(8,128)}, u32[]{:S(2)}) copy-start(f32[16,128,128]{2,1,0:T(8,128)} %constant.31.clone.out_y) | copy-start | bytes 3145732
  25.2 51.1 %all-to-all-start.1 = ((f32[32,2,8,128]{3,2,1,0:T(8,128)}), f32[32,2,8,128]{3,2,1,0:T(8,128)S(1)}, u32[]{:S(2)}, u32[]{:S(2)}) async-start(f32[32,2,8,128]{3,2,1,0:T(8,128)} %first_x.1), calls=%async_computation.1 | async-start | bytes 524288 | tf_op jit(solution)/shard_map/all_to_all | solution.py:413
  34.9 9.4 %collective-permute-start = (f32[8,32,128]{2,1,0:T(8,128)S(1)}, f32[8,32,128]{2,1,0:T(8,128)S(1)}, u32[]{:S(2)}, u32[]{:S(2)}) collective-permute-start(f32[8,32,128]{2,1,0:T(8,128)S(1)} %get-tuple-element.17), channel_id=1, source_target_pairs={{0,1},{1,0},{2,3},{3,2},{4,5},{5,4},{6,7},{7,6},{8,9},{9,8},{10,11... | collective-permute-start | bytes 393224 | tf_op jit(solution)/shard_map/ppermute | solution.py:392
  36.8 15.4 %collective-permute-start.1 = (f32[8,32,128]{2,1,0:T(8,128)S(1)}, f32[8,32,128]{2,1,0:T(8,128)S(1)}, u32[]{:S(2)}, u32[]{:S(2)}) collective-permute-start(f32[8,32,128]{2,1,0:T(8,128)S(1)} %get-tuple-element.18), channel_id=1, source_target_pairs={{0,3},{1,2},{2,1},{3,0},{4,7},{5,6},{6,5},{7,4},{8,11},{9,10},{10,... | collective-permute-start | bytes 393224 | tf_op jit(solution)/shard_map/ppermute | solution.py:391
  52.3 8.0 %collective-permute-start.2 = (f32[48,8,128]{2,1,0:T(8,128)S(1)}, f32[48,8,128]{2,1,0:T(8,128)S(1)}, u32[]{:S(2)}, u32[]{:S(2)}) collective-permute-start(f32[48,8,128]{2,1,0:T(8,128)S(1)} %get-tuple-element.19), channel_id=1, source_target_pairs={{0,4},{4,0},{8,12},{12,8},{16,20},{20,16},{24,28},{28,24},{32,36},... | collective-permute-start | bytes 589832 | tf_op jit(solution)/shard_map/ppermute | solution.py:392
  54.8 11.8 %collective-permute-start.3 = (f32[48,8,128]{2,1,0:T(8,128)S(1)}, f32[48,8,128]{2,1,0:T(8,128)S(1)}, u32[]{:S(2)}, u32[]{:S(2)}) collective-permute-start(f32[48,8,128]{2,1,0:T(8,128)S(1)} %get-tuple-element.20), channel_id=1, source_target_pairs={{0,60},{4,8},{8,4},{12,16},{16,12},{20,24},{24,20},{28,32},{32,28}... | collective-permute-start | bytes 589832 | tf_op jit(solution)/shard_map/ppermute | solution.py:391
  67.2 5.5 %collective-permute-start.4 = (f32[144,128]{1,0:T(8,128)S(1)}, f32[144,128]{1,0:T(8,128)S(1)}, u32[]{:S(2)}, u32[]{:S(2)}) collective-permute-start(f32[144,128]{1,0:T(8,128)S(1)} %get-tuple-element.21), channel_id=1, source_target_pairs={{0,64},{64,0},{128,192},{192,128},{256,320},{320,256},{384,448},{4... | collective-permute-start | bytes 221192 | tf_op jit(solution)/shard_map/ppermute | solution.py:392
  69.4 6.3 %collective-permute-start.5 = (f32[144,128]{1,0:T(8,128)S(1)}, f32[144,128]{1,0:T(8,128)S(1)}, u32[]{:S(2)}, u32[]{:S(2)}) collective-permute-start(f32[144,128]{1,0:T(8,128)S(1)} %get-tuple-element.22), channel_id=1, source_target_pairs={{0,448},{64,128},{128,64},{192,256},{256,192},{320,384},{384,320},... | collective-permute-start | bytes 221192 | tf_op jit(solution)/shard_map/ppermute | solution.py:391
  75.7 0.6 copy-start.12
  76.4 2.2 %copy-start.2 = (f32[16,256,256]{2,1,0:T(8,128)S(1)}, f32[16,256,256]{2,1,0:T(8,128)}, u32[]{:S(2)}) copy-start(f32[16,256,256]{2,1,0:T(8,128)} %constant.29.clone.gain) | copy-start | bytes 12582916
  78.6 1.0 copy-start.7
  79.5 0.9 copy-start.8
  80.5 0.8 copy-start.14
  81.3 10.5 %copy-start.6 = (f32[9,48,256]{2,1,0:T(8,128)S(1)}, f32[9,48,256]{2,1,0:T(8,128)}, u32[]{:S(2)}) copy-start(f32[9,48,256]{2,1,0:T(8,128)} %constant.34.clone.gains) | copy-start | bytes 1327108
  81.3 10.5 %copy-start.15 = (bf16[48,144]{1,0:T(8,128)(2,1)S(1)}, bf16[48,144]{1,0:T(8,128)(2,1)}, u32[]{:S(2)}) copy-start(bf16[48,144]{1,0:T(8,128)(2,1)} %constant.36.clone.into_y) | copy-start | bytes 41476
  84.3 18.1 %copy-start.4 = (f32[8,256,128]{2,1,0:T(8,128)S(1)}, f32[8,256,128]{2,1,0:T(8,128)}, u32[]{:S(2)}) copy-start(f32[8,256,128]{2,1,0:T(8,128)} %constant.32.clone.last_x) | copy-start | bytes 3145732
  84.3 18.0 %all-to-all-start.2 = ((f32[16,16,128]{2,1,0:T(8,128)}), f32[16,16,128]{2,1,0:T(8,128)S(1)}, u32[]{:S(2)}, u32[]{:S(2)}) async-start(f32[16,16,128]{2,1,0:T(8,128)} %filter.1), calls=%async_computation.2 | async-start | bytes 262144 | tf_op jit(solution)/shard_map/all_to_all | solution.py:437
  91.8 1.0 copy-start.9
  92.8 0.9 copy-start.10
  93.7 0.9 copy-start.13
  94.6 0.7 copy-start.16
  102.4 0.9 copy-start.11

commit v3 on v2

--- a/solution.py
+++ b/solution.py
@@ -25,6 +25,8 @@
 BORDER = BY + 2
 SHARE = 2 * GX
 KX = MX // SHARE
+VMEM_MIB = 44
+TABLE_ROWS = 24 * 2048
 
 f32 = jnp.float32
 bf16 = jnp.bfloat16
@@ -53,8 +55,8 @@
     cos_y = np.cos(2.0 * np.pi / PY * np.outer(np.arange(PY), both))
     cos_x = np.cos(2.0 * np.pi / PX * np.outer(np.arange(PX), both))
     spectral = np.einsum("dab,ka,lb->dkl", kernel, cos_y, cos_x) / (PY * PX)
-    gains = np.zeros((HALO + 1, PY, LANES))
-    gains[:, :, :PX] = spectral
+    gains = np.zeros(((HALO + 1) * PY, LANES))
+    gains[:, :PX] = spectral.reshape(-1, PX)
 
     every_x, every_y = np.arange(PX), np.arange(PY)
     forward_x = np.zeros((PX, LANES))
@@ -62,19 +64,19 @@
     high, low = split(forward_x)
     own = slice(HALO, HALO + CX)
     ends = np.r_[0:HALO, HALO + CX : PX]
-    into_x = np.zeros((512, LANES), ml_dtypes.bfloat16)
+    into_x = np.zeros((512, LANES))
     into_x[0:128], into_x[128:256], into_x[256:384] = high[own], low[own], high[own]
     into_x[384:400], into_x[400:416], into_x[416:432] = high[ends], low[ends], high[ends]
 
     high, low = split(cas(every_y, every_y, PY))
-    into_y = np.concatenate([high, low, high], axis=1)
-    out_y = into_y[HALO : HALO + CY]
+    into_y = np.zeros((PY, LANES))
+    into_y[:, : 3 * PY] = np.concatenate([high, low, high], axis=1)
 
     back_x = np.zeros((LANES, CX))
     back_x[:PX] = cas(every_x, every_x[own], PX)
     high, low = split(back_x)
     out_x = np.concatenate([high, low, high], axis=0)
-    return gains.astype(np.float32), into_x, into_y, out_y, out_x
+    return {"gains": gains, "into_x": into_x, "into_y": into_y, "out_x": out_x}
 
 
 def far_tables():
@@ -122,8 +124,66 @@
         last_x[g] = full_x[:, (g * BX - 1 + np.arange(BX + 2)) % MX] @ refine(BX).T
     last_y = np.zeros((BORDER * CY, 128))
     last_y[:, : BORDER * BORDER] = np.kron(np.eye(BORDER), refine(BY))
-    tables = first_x, full_y, into_z, gain, out_z, out_y, last_x, last_y
-    return tuple(table.astype(np.float32) for table in tables)
+    return {
+        "first_x": first_x,
+        "full_y": full_y,
+        "into_z": into_z,
+        "gain": gain,
+        "out_z": out_z,
+        "out_y": out_y,
+        "last_x": last_x,
+        "last_y": last_y,
+    }
+
+
+class Tables:
+    def __init__(self):
+        self.place, rows, pieces = {}, 0, []
+        for name, table in (near_tables() | far_tables()).items():
+            count, lanes = table.shape[-2:]
+            halves = lanes // 128
+            flat = table.reshape(-1, count, halves, 128).swapaxes(1, 2).reshape(-1, 128)
+            self.place[name] = rows, count, halves
+            rows += flat.shape[0]
+            pieces.append(flat)
+        self.array = np.zeros((TABLE_ROWS, 128), np.float32)
+        self.array[:rows] = np.concatenate(pieces)
+
+    def shape(self, name):
+        _, count, halves = self.place[name]
+        return pltpu.VMEM((halves, count, 128), f32)
+
+    def copies(self, ref, held, sems, index):
+        made = []
+        for i, (name, target) in enumerate(held.items()):
+            first, count, halves = self.place[name]
+            rows = halves * count
+            start = first + index.get(name, 0) * rows
+            if name in index:
+                start = pl.multiple_of(start, 8)
+            for half in range(halves):
+                source = ref.at[pl.ds(start + half * count, count)]
+                made.append(pltpu.make_async_copy(source, target.at[half], sems.at[i]))
+        for copy in made:
+            copy.start()
+        pairs, at = {}, 0
+        for name in held:
+            halves = self.place[name][2]
+            pairs[name] = made[at : at + halves]
+            at += halves
+
+        def wait(name):
+            for copy in pairs[name]:
+                copy.wait()
+            target = held[name]
+            if len(pairs[name]) == 1:
+                return target[0]
+            return jnp.concatenate([target[0], target[1]], axis=1)
+
+        return wait
+
+
+TABLES = Tables()
 
 
 def dot(a, b):
@@ -179,9 +239,8 @@
     odd[...] = density[pl.ds(CZ - HALO - start, HALO)]
 
 
-def first_kernel(table, charges, out, held, sem):
-    copy = pltpu.make_async_copy(table.at[share()], held, sem)
-    copy.start()
+def first_kernel(table, charges, out, held, sems):
+    wait = TABLES.copies(table, {"first_x": held}, sems, {"first_x": share()})
     peers = charges[...].reshape(GX, 32, 128)
     place = lane((32, 128)) // BX
     blocks = []
@@ -197,8 +256,7 @@
             sides.append(total)
         blocks.append(jnp.concatenate(sides, axis=1))
     rows = jnp.concatenate(blocks, axis=0)
-    copy.wait()
-    rows = exact_dot(rows, held[...])
+    rows = exact_dot(rows, wait("first_x"))
     place = lane((BY, 128)) // KX
     for core in range(2):
         total = None
@@ -210,35 +268,20 @@
             out[peer, core] = total
 
 
-def filter_kernel(
-    full_y, into_z, gain, out_z, out_y, spectrum, out, held_y, held_z, held_g, held_iz, held_iy, sems
-):
-    sources = (
-        (full_y, held_y),
-        (into_z, held_z),
-        (gain.at[share()], held_g),
-        (out_z.at[lax.axis_index("yh")], held_iz),
-        (out_y.at[lax.axis_index("gy")], held_iy),
-    )
-    copies = [
-        pltpu.make_async_copy(source, held, sems.at[i]) for i, (source, held) in enumerate(sources)
-    ]
-    for copy in copies:
-        copy.start()
+def filter_kernel(table, spectrum, out, held_y, held_z, held_g, held_iz, held_iy, sems):
+    held = {"full_y": held_y, "into_z": held_z, "gain": held_g, "out_z": held_iz, "out_y": held_iy}
+    index = {"gain": share(), "out_z": lax.axis_index("yh"), "out_y": lax.axis_index("gy")}
+    wait = TABLES.copies(table, held, sems, index)
     blocks = spectrum[...].reshape(GY, 4, BY, 128)
-    copies[0].wait()
-    waves = [transposed_dot(blocks[:, b].reshape(MY, 128), held_y[...]) for b in range(4)]
+    full_y = wait("full_y")
+    waves = [transposed_dot(blocks[:, b].reshape(MY, 128), full_y) for b in range(4)]
     rows = jnp.concatenate(waves, axis=0).reshape(MZ, 2, 8, MY)
     rows = jnp.concatenate([rows[:, half].reshape(MZ * 8, MY) for half in range(2)], axis=1)
-    copies[1].wait()
-    rows = exact_dot(held_z[...], rows)
-    copies[2].wait()
-    rows = rows * held_g[...]
-    copies[3].wait()
-    rows = exact_dot(held_iz[...], rows)
-    copies[4].wait()
+    rows = exact_dot(wait("into_z"), rows)
+    rows = rows * wait("gain")
+    rows = exact_dot(wait("out_z"), rows)
     rows = jnp.concatenate([rows[:, :MY], rows[:, MY:]], axis=0)
-    rows = exact_dot(rows, held_iy[...])
+    rows = exact_dot(rows, wait("out_y"))
     for core in range(2):
         sides = []
         for half in range(2):
@@ -253,18 +296,12 @@
             out[peer * 2 + core] = message
 
 
-def last_kernel(last_x, last_y, spectrum, near, out, held_x, held_y, sems):
-    copies = [
-        pltpu.make_async_copy(last_x.at[lax.axis_index("gx")], held_x, sems.at[0]),
-        pltpu.make_async_copy(last_y, held_y, sems.at[1]),
-    ]
-    for copy in copies:
-        copy.start()
+def last_kernel(table, spectrum, near, out, held_x, held_y, sems):
+    held = {"last_x": held_x, "last_y": held_y}
+    wait = TABLES.copies(table, held, sems, {"last_x": lax.axis_index("gx")})
     rows = spectrum[...].reshape(MX, 128)
-    copies[0].wait()
-    field = transposed_dot(rows, held_x[...])
-    copies[1].wait()
-    field = exact_dot(held_y[...], field)
+    field = transposed_dot(rows, wait("last_x"))
+    field = exact_dot(wait("last_y"), field)
 
     def plane(z):
         return field[z * CY : (z + 1) * CY]
@@ -289,7 +326,8 @@
         target[HALO + CZ : PZ] = jnp.where(lower, one, two)
 
 
-def edge_x_kernel(density, z_even, z_odd, y_even, y_odd, padded, even, odd):
+def edge_x_kernel(table, density, z_even, z_odd, y_even, y_odd, waves, even, odd, padded, held, sems):
+    wait = TABLES.copies(table, {"into_y": held}, sems, {})
     lower = is_even("core")
     one, two = z_even[...], z_odd[...]
     middle = slice(HALO, HALO + CY)
@@ -301,28 +339,40 @@
     padded[:, 0:HALO] = jnp.where(lower, two, one)
     padded[:, HALO + CY : PY] = jnp.where(lower, one, two)
 
+    into_y = wait("into_y")[:, : 3 * PY].astype(bf16)
     place = lane((GROUP, 128)) // HALO
     left = right = jnp.zeros((GROUP, 128), f32)
-    for j in range(16):
-        rows = padded[3 * j : 3 * j + 3].reshape(GROUP, 128)
-        shift = j * HALO
-        left = jnp.where(place == j, pltpu.roll(rows, shift, 1) if shift else rows, left)
-        shift = (j * HALO - (CX - HALO)) % 128
-        right = jnp.where(place == j, pltpu.roll(rows, shift, 1) if shift else rows, right)
+    for j in range(8):
+        rows = []
+        for pair in range(3):
+            z = 6 * j + 2 * pair
+            high, low = halves(jnp.concatenate([padded[z], padded[z + 1]], axis=1))
+            wave = dot(into_y, jnp.concatenate([high, high, low], axis=0))
+            waves[z], waves[z + 1] = wave[:, :128], wave[:, 128:]
+            rows += [wave[:, :128], wave[:, 128:]]
+        for i in range(2):
+            group = jnp.concatenate(rows[3 * i : 3 * i + 3], axis=0)
+            shift = (2 * j + i) * HALO
+            left = jnp.where(place == 2 * j + i, pltpu.roll(group, shift, 1) if shift else group, left)
+            shift = (shift - (CX - HALO)) % 128
+            right = jnp.where(place == 2 * j + i, pltpu.roll(group, shift, 1) if shift else group, right)
     lower = is_even("gx")
     even[...] = jnp.where(lower, right, left)
     odd[...] = jnp.where(lower, left, right)
 
 
 def near_kernel(
-    padded, x_even, x_odd, gains, into_x, into_y, out_y, out_x, out, wave_x, wave_y, wave_z
+    table, waves, x_even, x_odd, out, wave_x, wave_z, held_g, held_ix, held_y, held_ox, sems
 ):
+    held = {"into_x": held_ix, "gains": held_g, "into_y": held_y, "out_x": held_ox}
+    wait = TABLES.copies(table, held, sems, {})
     lanes = lane((GROUP, 128))
     lower = is_even("gx")
     one, two = x_even[...], x_odd[...]
     left, right = jnp.where(lower, two, one), jnp.where(lower, one, two)
+    into_x = wait("into_x").astype(bf16)
     for j in range(16):
-        rows = padded[3 * j : 3 * j + 3].reshape(GROUP, 128)
+        rows = waves[3 * j : 3 * j + 3].reshape(GROUP, 128)
         to_left, to_right = (-HALO * j) % 128, (HALO - HALO * j) % 128
         ends = jnp.where(
             lanes < HALO,
@@ -334,53 +384,60 @@
         low = ends - high
         ends = (high + pltpu.roll(high, 2 * HALO, 1) + pltpu.roll(low, 4 * HALO, 1)).astype(bf16)
         high, low = halves(rows)
-        wave = dot(jnp.concatenate([high, high, low, ends], axis=1), into_x[...])
+        wave = dot(jnp.concatenate([high, high, low, ends], axis=1), into_x)
         for i in range(3):
             wave_x[3 * j + i] = wave[i * PY : (i + 1) * PY]
 
-    @pl.loop(0, PZ, unroll=8)
-    def _(z):
-        high, low = halves(wave_x[z])
-        wave_y[z] = dot(into_y[...], jnp.concatenate([high, high, low], axis=0))
+    wait("gains")
 
     @pl.loop(0, PY // 8)
     def _(c):
-        row = pl.ds(pl.multiple_of(c * 8, 8), 8)
         for side in range(LANES // 128):
-            column = pl.ds(side * 128, 128)
-            gain = [gains[d, row, column] for d in range(HALO + 1)]
-            window = [wave_y[z, row, column] for z in range(2 * HALO)]
+            gain = [
+                held_g[side, pl.ds(pl.multiple_of(d * PY + c * 8, 8), 8)] for d in range(HALO + 1)
+            ]
+            row, column = pl.ds(pl.multiple_of(c * 8, 8), 8), pl.ds(side * 128, 128)
+            window = [wave_x[z, row, column] for z in range(2 * HALO)]
             for z in range(CZ):
-                window.append(wave_y[z + 2 * HALO, row, column])
+                window.append(wave_x[z + 2 * HALO, row, column])
                 total = gain[0] * window[HALO]
                 for d in range(1, HALO + 1):
                     total = total + gain[d] * (window[HALO - d] + window[HALO + d])
                 wave_z[z, row, column] = total
                 window.pop(0)
 
-    @pl.loop(0, CZ // 4, unroll=2)
-    def _(step):
+    out_y = wait("into_y")[HALO : HALO + CY, : 3 * PY].astype(bf16)
+    out_x = wait("out_x").astype(bf16)
+
+    for step in range(CZ // 4):
         rows = []
         for i in range(4):
             high, low = halves(wave_z[step * 4 + i])
-            rows.append(dot(out_y[...], jnp.concatenate([high, high, low], axis=0)))
+            rows.append(dot(out_y, jnp.concatenate([high, high, low], axis=0)))
         high, low = halves(jnp.concatenate(rows, axis=0))
-        field = dot(jnp.concatenate([high, high, low], axis=1), out_x[...])
+        field = dot(jnp.concatenate([high, high, low], axis=1), out_x)
         for i in range(4):
             out[step * 4 + i] = field[i * CY : (i + 1) * CY]
 
 
-def call(kernel, outs, scratch=(), specs=None, name=None):
+def call(kernel, outs, arrays=0, tables=(), scratch=(), us=1.0):
     vmem = pl.BlockSpec(memory_space=pltpu.VMEM)
     many = isinstance(outs, list)
+    specs = [vmem] * arrays
+    scratch = list(scratch)
+    if tables:
+        specs = [pl.BlockSpec(memory_space=pltpu.HBM)] + specs
+        scratch += [TABLES.shape(name) for name in tables]
+        scratch.append(pltpu.SemaphoreType.DMA((len(tables),)))
     return pl.pallas_call(
         kernel,
         out_shape=[jax.ShapeDtypeStruct(s, f32) for s in outs] if many else jax.ShapeDtypeStruct(outs, f32),
         in_specs=specs,
         out_specs=[vmem] * len(outs) if many else vmem,
-        scratch_shapes=list(scratch),
-        compiler_params=pltpu.CompilerParams(vmem_limit_bytes=40 * 1024 * 1024),
-        name=name,
+        scratch_shapes=scratch,
+        compiler_params=pltpu.CompilerParams(vmem_limit_bytes=VMEM_MIB * 1024 * 1024),
+        cost_estimate=pl.CostEstimate(flops=int(us * 1e9), bytes_accessed=int(us * 3e6), transcendentals=0),
+        name=kernel.__name__,
     )
 
 
@@ -393,68 +450,40 @@
 
 
 def body(density):
-    vmem, far = pl.BlockSpec(memory_space=pltpu.VMEM), pl.BlockSpec(memory_space=pltpu.HBM)
-    dma = pltpu.SemaphoreType.DMA
-    first_x, full_y, into_z, gain, out_z, out_y, last_x, last_y = (jnp.asarray(t) for t in far_tables())
-    near_consts = [jnp.asarray(t) for t in near_tables()]
-
-    charges, even, odd = call(
-        charge_kernel, [(SHARE, 16, 128), (HALO, CY, CX), (HALO, CY, CX)], specs=[vmem], name="charges"
-    )(density)
+    table = jnp.asarray(TABLES.array)
+    charges, even, odd = call(charge_kernel, [(SHARE, 16, 128), (HALO, CY, CX), (HALO, CY, CX)], 1, us=0.5)(density)
     charges = lax.all_to_all(charges, ("gx", "core"), 0, 0, tiled=True)
     z_ends = exchange(even, odd, ("yh", "core"))
-    spectrum = call(
-        first_kernel,
-        (2 * GY, 2, 8, 128),
-        [pltpu.VMEM((MX, 128), f32), dma],
-        [far, vmem],
-        name="first_x",
-    )(first_x, charges)
+    charges, z_ends = lax.optimization_barrier((charges, z_ends))
+    spectrum = call(first_kernel, (2 * GY, 2, 8, 128), 1, ["first_x"], us=1.3)(table, charges)
     spectrum = lax.all_to_all(spectrum, ("gy", "yh"), 0, 0, tiled=True)
 
-    y_ends = call(edge_y_kernel, [(PZ, HALO, CX)] * 2, specs=[vmem] * 3, name="edges_y")(density, *z_ends)
+    y_ends = call(edge_y_kernel, [(PZ, HALO, CX)] * 2, 3, us=0.2)(density, *z_ends)
+    spectrum, _ = lax.optimization_barrier((spectrum, y_ends))
     y_ends = exchange(*y_ends, "gy")
-    padded, even, odd = call(
-        edge_x_kernel, [(PZ, PY, CX), (GROUP, 128), (GROUP, 128)], specs=[vmem] * 5, name="edges_x"
-    )(density, *z_ends, *y_ends)
+    spectrum = call(filter_kernel, (SHARE, KX, 128), 1, ["full_y", "into_z", "gain", "out_z", "out_y"], us=3.0)(
+        table, spectrum
+    )
+    y_ends, _ = lax.optimization_barrier((y_ends, spectrum))
+    spectrum = lax.all_to_all(spectrum, ("gx", "core"), 0, 0, tiled=True)
+    waves, even, odd = call(
+        edge_x_kernel,
+        [(PZ, PY, CX), (GROUP, 128), (GROUP, 128)],
+        5,
+        ["into_y"],
+        [pltpu.VMEM((PZ, PY, CX), f32)],
+        us=2.0,
+    )(table, density, *z_ends, *y_ends)
     x_ends = exchange(even, odd, "gx")
-
-    spectrum, x_ends = lax.optimization_barrier((spectrum, x_ends))
-    spectrum = call(
-        filter_kernel,
-        (SHARE, KX, 128),
-        [
-            pltpu.VMEM((MY, MY), f32),
-            pltpu.VMEM((256, 256), f32),
-            pltpu.VMEM((256, 256), f32),
-            pltpu.VMEM((2 * BORDER * 8, 256), f32),
-            pltpu.VMEM((MY, 128), f32),
-            dma((5,)),
-        ],
-        [far] * 5 + [vmem],
-        name="filter",
-    )(full_y, into_z, gain, out_z, out_y, spectrum)
-    spectrum = lax.all_to_all(spectrum, ("gx", "core"), 0, 0, tiled=True)
-
     near = call(
         near_kernel,
         (CZ, CY, CX),
-        [
-            pltpu.VMEM((PZ, PY, LANES), f32),
-            pltpu.VMEM((PZ, PY, LANES), f32),
-            pltpu.VMEM((CZ, PY, LANES), f32),
-        ],
-        [vmem] * 8,
-        name="near",
-    )(padded, *x_ends, *near_consts)
-
-    return call(
-        last_kernel,
-        (CZ, CY, CX),
-        [pltpu.VMEM((MX, CX), f32), pltpu.VMEM((BORDER * CY, 128), f32), dma((2,))],
-        [far, far, vmem, vmem],
-        name="last",
-    )(last_x, last_y, spectrum, near)
+        3,
+        ["gains", "into_x", "into_y", "out_x"],
+        [pltpu.VMEM((PZ, PY, LANES), f32), pltpu.VMEM((CZ, PY, LANES), f32)],
+        us=6.0,
+    )(table, waves, *x_ends)
+    return call(last_kernel, (CZ, CY, CX), 2, ["last_x", "last_y"], us=1.8)(table, spectrum, near)
 
 
 def solution(mesh):

time: 106 us -> 88.4 us (0.83)
  blocking collectives: 20.8 us -> 0 us
  starting transfers between devices: 39.5 us -> 56.1 us
  local copies, waits for them, and re-layouts: 12.6 us -> 1.04 us
  waiting for transfers between devices: 17.7 us -> 13.8 us
  Pallas kernels: 14.3 us -> 16.7 us
    all_to_all x1 -> x0, blocking collectives: 20.8 us -> none  [body(): charges = lax.all_to_all(charges, ('gx', 'core'), 0, 0, tiled=True)]
    all_to_all x0 -> x1, starting transfers between devices: none -> 11.8 us  [body(): charges = lax.all_to_all(charges, ('gx', 'core'), 0, 0, tiled=True)]
    unnamed x34 -> x4, local copies, waits for them, and re-layouts: 12.6 us -> 1.04 us
    ppermute x3, waiting for transfers between devices: 17.2 us -> 9.67 us  [exchange(): odd = lax.ppermute(odd, axis, high_first)]
    all_to_all x1, waiting for transfers between devices: 0.01 us -> 2.98 us  [body(): spectrum = lax.all_to_all(spectrum, ('gx', 'core'), 0, 0, tiled=True)]
    all_to_all x1, starting transfers between devices: 9.68 us -> 12.4 us  [body(): spectrum = lax.all_to_all(spectrum, ('gy', 'yh'), 0, 0, tiled=True)]
    all_to_all x1, starting transfers between devices: 7.5 us -> 4.9 us  [body(): spectrum = lax.all_to_all(spectrum, ('gx', 'core'), 0, 0, tiled=True)]
    ppermute x3, starting transfers between devices: 15.7 us -> 18.2 us  [exchange(): odd = lax.ppermute(odd, axis, high_first)]
  transfers between devices with their start and end apart: 8 -> 9, of which waited for: 4 -> 4; matrix products, arithmetic and copies ran while one was open for 0% -> 0% of each run, Pallas kernels for 7% -> 11%
where the time goes in v3:
time: 88.4 us; the launch traced here: 87.7 us
  starting transfers between devices  56.1 us (63%)
  Pallas kernels  16.7 us (19%)
  waiting for transfers between devices  13.8 us (16%)
  local copies, waits for them, and re-layouts  1.04 us (1%)
    ppermute x3, starting transfers between devices, exchange(): odd = lax.ppermute(odd, axis, high_first)  18.2 us
    all_to_all x1, starting transfers between devices, body(): spectrum = lax.all_to_all(spectrum, ('gy', 'yh'), 0, 0, tiled=True)  12.4 us
    all_to_all x1, starting transfers between devices, body(): charges = lax.all_to_all(charges, ('gx', 'core'), 0, 0, tiled=True)  11.8 us
    ppermute x3, waiting for transfers between devices, exchange(): odd = lax.ppermute(odd, axis, high_first)  9.67 us
    ppermute x3, starting transfers between devices, exchange(): return (lax.ppermute(even, axis, low_first), odd)  8.8 us
    pallas_call x1, Pallas kernels, body(): call(near_kernel, (CZ, CY, CX), 3, ['gains', 'into_x', 'into_y', 'out_x']...  6.17 us
    all_to_all x1, starting transfers between devices, body(): spectrum = lax.all_to_all(spectrum, ('gx', 'core'), 0, 0, tiled=True)  4.9 us
    pallas_call x1, Pallas kernels, body(): call(filter_kernel, (SHARE, KX, 128), 1, ['full_y', 'into_z', 'gain', 'ou...  3.39 us
  transfers between devices with their start and end apart: 9, of which 4 were waited for; matrix products, arithmetic and copies ran while one was open for 0% of the time, Pallas kernels for 11%

profile of v3, /device:TPU:1, one launch (start us, length us, event | category | flops | bytes accessed | tf_op | source)
XLA Modules:
  0.0 87.7 jit_solution(17074381465187695476)
XLA Ops:
  0.0 0.0 copy-start
  0.0 1.0 %copy-done = f32[32,32,128]{2,1,0:T(8,128)S(1)} copy-done((f32[32,32,128]{2,1,0:T(8,128)S(1)}, f32[32,32,128]{2,1,0:T(8,128)}, u32[]{:S(2)}) %copy-start) | copy-done | bytes 524312
  1.0 0.0 copy-start.1
  1.0 1.1 %charge_kernel.1 = (f32[16,16,128]{2,1,0:T(8,128)}, f32[8,32,128]{2,1,0:T(8,128)S(1)}, f32[8,32,128]{2,1,0:T(8,128)S(1)}) custom-call(f32[32,32,128]{2,1,0:T(8,128)S(1)} %copy-done), custom_call_target="tpu_custom_call" | custom-call | flops 500000000 | bytes 1500000 | tf_op jit(solution)/shard_map/charge_kernel/pallas_call | solution.py:454
  2.2 11.8 %all-to-all-start = ((f32[16,16,128]{2,1,0:T(8,128)}), f32[16,16,128]{2,1,0:T(8,128)S(1)}, u32[]{:S(2)}, u32[]{:S(2)}) async-start(f32[16,16,128]{2,1,0:T(8,128)} %get-tuple-element.19), calls=%async_computation | async-start | bytes 262144 | tf_op jit(solution)/shard_map/all_to_all | solution.py:455
  14.0 2.0 %collective-permute-start = (f32[8,32,128]{2,1,0:T(8,128)S(1)}, f32[8,32,128]{2,1,0:T(8,128)S(1)}, u32[]{:S(2)}, u32[]{:S(2)}) collective-permute-start(f32[8,32,128]{2,1,0:T(8,128)S(1)} %get-tuple-element.20), channel_id=1, source_target_pairs={{0,1},{1,0},{2,3},{3,2},{4,5},{5,4},{6,7},{7,6},{8,9},{9,8},{10,11... | collective-permute-start | bytes 393224 | tf_op jit(solution)/shard_map/ppermute | solution.py:449
  16.0 7.7 %collective-permute-start.1 = (f32[8,32,128]{2,1,0:T(8,128)S(1)}, f32[8,32,128]{2,1,0:T(8,128)S(1)}, u32[]{:S(2)}, u32[]{:S(2)}) collective-permute-start(f32[8,32,128]{2,1,0:T(8,128)S(1)} %get-tuple-element.21), channel_id=1, source_target_pairs={{0,3},{1,2},{2,1},{3,0},{4,7},{5,6},{6,5},{7,4},{8,11},{9,10},{10,... | collective-permute-start | bytes 393224 | tf_op jit(solution)/shard_map/ppermute | solution.py:448
  23.8 0.0 collective-permute-done.z_even
  23.8 3.7 %collective-permute-done.1.z_odd = f32[8,32,128]{2,1,0:T(8,128)S(1)} collective-permute-done((f32[8,32,128]{2,1,0:T(8,128)S(1)}, f32[8,32,128]{2,1,0:T(8,128)S(1)}, u32[]{:S(2)}, u32[]{:S(2)}) %collective-permute-start.1) | collective-permute-done | bytes 131104 | tf_op jit(solution)/shard_map/ppermute | solution.py:448
  27.4 0.0 all-to-all-done.charges
  27.4 2.0 %first_kernel.1 = f32[32,2,8,128]{3,2,1,0:T(8,128)} custom-call(f32[49152,128]{1,0:T(8,128)} %constant.2.clone.table, f32[16,16,128]{2,1,0:T(8,128)S(1)} %all-to-all-done.charges), custom_call_target="tpu_custom_call" | custom-call | flops 1300000000 | bytes 3900000 | tf_op jit(solution)/shard_map/first_kernel/pallas_call | solution.py:458
  29.4 12.4 %all-to-all-start.1 = ((f32[32,2,8,128]{3,2,1,0:T(8,128)}), f32[32,2,8,128]{3,2,1,0:T(8,128)S(1)}, u32[]{:S(2)}, u32[]{:S(2)}) async-start(f32[32,2,8,128]{3,2,1,0:T(8,128)} %first_kernel.1), calls=%async_computation.1 | async-start | bytes 524288 | tf_op jit(solution)/shard_map/all_to_all | solution.py:459
  41.8 0.0 copy-done.1
  41.8 0.1 edge_y_kernel.1
  41.9 3.1 %collective-permute-start.2 = (f32[48,8,128]{2,1,0:T(8,128)S(1)}, f32[48,8,128]{2,1,0:T(8,128)S(1)}, u32[]{:S(2)}, u32[]{:S(2)}) collective-permute-start(f32[48,8,128]{2,1,0:T(8,128)S(1)} %get-tuple-element.25), channel_id=1, source_target_pairs={{0,4},{4,0},{8,12},{12,8},{16,20},{20,16},{24,28},{28,24},{32,36},... | collective-permute-start | bytes 589832 | tf_op jit(solution)/shard_map/ppermute | solution.py:449
  45.1 6.2 %collective-permute-start.3 = (f32[48,8,128]{2,1,0:T(8,128)S(1)}, f32[48,8,128]{2,1,0:T(8,128)S(1)}, u32[]{:S(2)}, u32[]{:S(2)}) collective-permute-start(f32[48,8,128]{2,1,0:T(8,128)S(1)} %get-tuple-element.26), channel_id=1, source_target_pairs={{0,60},{4,8},{8,4},{12,16},{16,12},{20,24},{24,20},{28,32},{32,28}... | collective-permute-start | bytes 589832 | tf_op jit(solution)/shard_map/ppermute | solution.py:448
  51.2 1.1 %all-to-all-done.1.spectrum = f32[32,2,8,128]{3,2,1,0:T(8,128)S(1)} async-done(((f32[32,2,8,128]{3,2,1,0:T(8,128)}), f32[32,2,8,128]{3,2,1,0:T(8,128)S(1)}, u32[]{:S(2)}, u32[]{:S(2)}) %all-to-all-start.1) | async-done | bytes 262176 | tf_op jit(solution)/shard_map/all_to_all | solution.py:459
  52.4 3.4 %filter_kernel.1 = f32[16,16,128]{2,1,0:T(8,128)} custom-call(f32[49152,128]{1,0:T(8,128)} %constant.2.clone.table, f32[32,2,8,128]{3,2,1,0:T(8,128)S(1)} %all-to-all-done.1.spectrum), custom_call_target="tpu_custom_call" | custom-call | flops 3000000000 | bytes 9000000 | tf_op jit(solution)/shard_map/filter_kernel/pallas_call | solution.py:464
  55.8 0.0 collective-permute-done.2.y_even
  55.8 6.0 %collective-permute-done.3.y_odd = f32[48,8,128]{2,1,0:T(8,128)S(1)} collective-permute-done((f32[48,8,128]{2,1,0:T(8,128)S(1)}, f32[48,8,128]{2,1,0:T(8,128)S(1)}, u32[]{:S(2)}, u32[]{:S(2)}) %collective-permute-start.3) | collective-permute-done | bytes 196640 | tf_op jit(solution)/shard_map/ppermute | solution.py:448
  61.8 1.6 %edge_x_kernel.1 = (f32[48,48,128]{2,1,0:T(8,128)S(1)}, f32[144,128]{1,0:T(8,128)S(1)}, f32[144,128]{1,0:T(8,128)S(1)}) custom-call(f32[49152,128]{1,0:T(8,128)} %constant.2.clone.table, f32[32,32,128]{2,1,0:T(8,128)S(1)} %copy-done.1, f32[8,32,128]{2,1,0:T(8,128)S(1)} %collective-permute-done.z_even, f32[8,32,128]{2,1,0:T(8,128)S(1)} %collective-permute-done.1.z_odd, ...), custom_call_target="tpu_custom_call" | custom-call | flops 2000000000 | bytes 6000000 | tf_op jit(solution)/shard_map/edge_x_kernel/pallas_call | solution.py:469
  63.4 3.7 %collective-permute-start.4 = (f32[144,128]{1,0:T(8,128)S(1)}, f32[144,128]{1,0:T(8,128)S(1)}, u32[]{:S(2)}, u32[]{:S(2)}) collective-permute-start(f32[144,128]{1,0:T(8,128)S(1)} %get-tuple-element.31), channel_id=1, source_target_pairs={{0,64},{64,0},{128,192},{192,128},{256,320},{320,256},{384,448},{4... | collective-permute-start | bytes 221192 | tf_op jit(solution)/shard_map/ppermute | solution.py:449
  67.0 4.3 %collective-permute-start.5 = (f32[144,128]{1,0:T(8,128)S(1)}, f32[144,128]{1,0:T(8,128)S(1)}, u32[]{:S(2)}, u32[]{:S(2)}) collective-permute-start(f32[144,128]{1,0:T(8,128)S(1)} %get-tuple-element.32), channel_id=1, source_target_pairs={{0,448},{64,128},{128,64},{192,256},{256,192},{320,384},{384,320},... | collective-permute-start | bytes 221192 | tf_op jit(solution)/shard_map/ppermute | solution.py:448
  71.3 4.9 %all-to-all-start.2 = ((f32[16,16,128]{2,1,0:T(8,128)}), f32[16,16,128]{2,1,0:T(8,128)S(1)}, u32[]{:S(2)}, u32[]{:S(2)}) async-start(f32[16,16,128]{2,1,0:T(8,128)} %filter_kernel.1), calls=%async_computation.2 | async-start | bytes 262144 | tf_op jit(solution)/shard_map/all_to_all | solution.py:468
  76.2 0.0 collective-permute-done.4.x_even
  76.2 0.0 collective-permute-done.5.x_odd
  76.3 6.2 %near_kernel.1.near = f32[32,32,128]{2,1,0:T(8,128)S(1)} custom-call(f32[49152,128]{1,0:T(8,128)} %constant.2.clone.table, f32[48,48,128]{2,1,0:T(8,128)S(1)} %get-tuple-element.30.waves, f32[144,128]{1,0:T(8,128)S(1)} %collective-permute-done.4.x_even, f32[144,128]{1,0:T(8,128)S(1)} %collective-permute-done.5.x_odd), custom_call_target="tpu_custom_call" | custom-call | flops 6000000000 | bytes 18000000 | tf_op jit(solution)/shard_map/near_kernel/pallas_call | solution.py:478
  82.4 3.0 %all-to-all-done.2.spectrum = f32[16,16,128]{2,1,0:T(8,128)S(1)} async-done(((f32[16,16,128]{2,1,0:T(8,128)}), f32[16,16,128]{2,1,0:T(8,128)S(1)}, u32[]{:S(2)}, u32[]{:S(2)}) %all-to-all-start.2) | async-done | bytes 131104 | tf_op jit(solution)/shard_map/all_to_all | solution.py:468
  85.4 2.3 %last_kernel.1 = f32[32,32,128]{2,1,0:T(8,128)} custom-call(f32[49152,128]{1,0:T(8,128)} %constant.2.clone.table, f32[16,16,128]{2,1,0:T(8,128)S(1)} %all-to-all-done.2.spectrum, f32[32,32,128]{2,1,0:T(8,128)S(1)} %near_kernel.1.near), custom_call_target="tpu_custom_call" | custom-call | flops 1800000000 | bytes 5400000 | tf_op jit(solution)/shard_map/last_kernel/pallas_call | solution.py:486
Async XLA Ops:
  0.0 1.0 %copy-start = (f32[32,32,128]{2,1,0:T(8,128)S(1)}, f32[32,32,128]{2,1,0:T(8,128)}, u32[]{:S(2)}) copy-start(f32[32,32,128]{2,1,0:T(8,128)} %density.5) | copy-start | bytes 1572868
  1.0 40.8 %copy-start.1 = (f32[32,32,128]{2,1,0:T(8,128)S(1)}, f32[32,32,128]{2,1,0:T(8,128)}, u32[]{:S(2)}) copy-start(f32[32,32,128]{2,1,0:T(8,128)} %density.5) | copy-start | bytes 1572868
  2.2 25.3 %all-to-all-start = ((f32[16,16,128]{2,1,0:T(8,128)}), f32[16,16,128]{2,1,0:T(8,128)S(1)}, u32[]{:S(2)}, u32[]{:S(2)}) async-start(f32[16,16,128]{2,1,0:T(8,128)} %get-tuple-element.19), calls=%async_computation | async-start | bytes 262144 | tf_op jit(solution)/shard_map/all_to_all | solution.py:455
  14.0 9.8 %collective-permute-start = (f32[8,32,128]{2,1,0:T(8,128)S(1)}, f32[8,32,128]{2,1,0:T(8,128)S(1)}, u32[]{:S(2)}, u32[]{:S(2)}) collective-permute-start(f32[8,32,128]{2,1,0:T(8,128)S(1)} %get-tuple-element.20), channel_id=1, source_target_pairs={{0,1},{1,0},{2,3},{3,2},{4,5},{5,4},{6,7},{7,6},{8,9},{9,8},{10,11... | collective-permute-start | bytes 393224 | tf_op jit(solution)/shard_map/ppermute | solution.py:449
  16.0 11.4 %collective-permute-start.1 = (f32[8,32,128]{2,1,0:T(8,128)S(1)}, f32[8,32,128]{2,1,0:T(8,128)S(1)}, u32[]{:S(2)}, u32[]{:S(2)}) collective-permute-start(f32[8,32,128]{2,1,0:T(8,128)S(1)} %get-tuple-element.21), channel_id=1, source_target_pairs={{0,3},{1,2},{2,1},{3,0},{4,7},{5,6},{6,5},{7,4},{8,11},{9,10},{10,... | collective-permute-start | bytes 393224 | tf_op jit(solution)/shard_map/ppermute | solution.py:448
  29.4 22.9 %all-to-all-start.1 = ((f32[32,2,8,128]{3,2,1,0:T(8,128)}), f32[32,2,8,128]{3,2,1,0:T(8,128)S(1)}, u32[]{:S(2)}, u32[]{:S(2)}) async-start(f32[32,2,8,128]{3,2,1,0:T(8,128)} %first_kernel.1), calls=%async_computation.1 | async-start | bytes 524288 | tf_op jit(solution)/shard_map/all_to_all | solution.py:459
  41.9 13.8 %collective-permute-start.2 = (f32[48,8,128]{2,1,0:T(8,128)S(1)}, f32[48,8,128]{2,1,0:T(8,128)S(1)}, u32[]{:S(2)}, u32[]{:S(2)}) collective-permute-start(f32[48,8,128]{2,1,0:T(8,128)S(1)} %get-tuple-element.25), channel_id=1, source_target_pairs={{0,4},{4,0},{8,12},{12,8},{16,20},{20,16},{24,28},{28,24},{32,36},... | collective-permute-start | bytes 589832 | tf_op jit(solution)/shard_map/ppermute | solution.py:449
  45.1 16.7 %collective-permute-start.3 = (f32[48,8,128]{2,1,0:T(8,128)S(1)}, f32[48,8,128]{2,1,0:T(8,128)S(1)}, u32[]{:S(2)}, u32[]{:S(2)}) collective-permute-start(f32[48,8,128]{2,1,0:T(8,128)S(1)} %get-tuple-element.26), channel_id=1, source_target_pairs={{0,60},{4,8},{8,4},{12,16},{16,12},{20,24},{24,20},{28,32},{32,28}... | collective-permute-start | bytes 589832 | tf_op jit(solution)/shard_map/ppermute | solution.py:448
  63.4 12.9 %collective-permute-start.4 = (f32[144,128]{1,0:T(8,128)S(1)}, f32[144,128]{1,0:T(8,128)S(1)}, u32[]{:S(2)}, u32[]{:S(2)}) collective-permute-start(f32[144,128]{1,0:T(8,128)S(1)} %get-tuple-element.31), channel_id=1, source_target_pairs={{0,64},{64,0},{128,192},{192,128},{256,320},{320,256},{384,448},{4... | collective-permute-start | bytes 221192 | tf_op jit(solution)/shard_map/ppermute | solution.py:449
  67.0 9.2 %collective-permute-start.5 = (f32[144,128]{1,0:T(8,128)S(1)}, f32[144,128]{1,0:T(8,128)S(1)}, u32[]{:S(2)}, u32[]{:S(2)}) collective-permute-start(f32[144,128]{1,0:T(8,128)S(1)} %get-tuple-element.32), channel_id=1, source_target_pairs={{0,448},{64,128},{128,64},{192,256},{256,192},{320,384},{384,320},... | collective-permute-start | bytes 221192 | tf_op jit(solution)/shard_map/ppermute | solution.py:448
  71.3 14.1 %all-to-all-start.2 = ((f32[16,16,128]{2,1,0:T(8,128)}), f32[16,16,128]{2,1,0:T(8,128)S(1)}, u32[]{:S(2)}, u32[]{:S(2)}) async-start(f32[16,16,128]{2,1,0:T(8,128)} %filter_kernel.1), calls=%async_computation.2 | async-start | bytes 262144 | tf_op jit(solution)/shard_map/all_to_all | solution.py:468

commit v4 on v3

--- a/solution.py
+++ b/solution.py
@@ -21,7 +21,8 @@
 BZ, BY, BX = MZ // GZ, MY // GY, MX // GX
 PZ, PY, PX = CZ + 2 * HALO, CY + 2 * HALO, CX + 2 * HALO
 LANES = 256
-GROUP = 3 * PY
+EDGE = 2 * CY
+TAIL = PX - CX
 BORDER = BY + 2
 SHARE = 2 * GX
 KX = MX // SHARE
@@ -215,7 +216,7 @@
     return lax.rem(lax.axis_index(axis), 2) == 0
 
 
-def charge_kernel(density, out, even, odd):
+def charge_kernel(density, out):
     parts = []
     for high in range(2):
         planes = []
@@ -234,9 +235,6 @@
     rows = exact_dot(pool((2 * BY, 2 * CY), 1, 0), rows)
     for peer in range(SHARE):
         out[peer] = rows
-    start = jnp.where(is_even("core"), CZ - HALO, 0)
-    even[...] = density[pl.ds(start, HALO)]
-    odd[...] = density[pl.ds(CZ - HALO - start, HALO)]
 
 
 def first_kernel(table, charges, out, held, sems):
@@ -296,83 +294,29 @@
             out[peer * 2 + core] = message
 
 
-def last_kernel(table, spectrum, near, out, held_x, held_y, sems):
-    held = {"last_x": held_x, "last_y": held_y}
-    wait = TABLES.copies(table, held, sems, {"last_x": lax.axis_index("gx")})
-    rows = spectrum[...].reshape(MX, 128)
-    field = transposed_dot(rows, wait("last_x"))
-    field = exact_dot(wait("last_y"), field)
-
-    def plane(z):
-        return field[z * CY : (z + 1) * CY]
-
-    for block in range(BZ):
-        before, here, after = plane(block), plane(block + 1), plane(block + 2)
-        for residue in range(COARSEN):
-            t = (residue + 0.5) / COARSEN - 0.5
-            value = (1.0 - abs(t)) * here + abs(t) * (before if t < 0 else after)
-            z = block * COARSEN + residue
-            out[z] = near[z] + value
-
-
-def edge_y_kernel(density, z_even, z_odd, even, odd):
-    lower = is_even("core")
-    start = jnp.where(is_even("gy"), CY - HALO, 0)
-    for target, first in ((even, start), (odd, CY - HALO - start)):
-        rows = pl.ds(pl.multiple_of(first, 8), HALO)
-        one, two = z_even[:, rows], z_odd[:, rows]
-        target[0:HALO] = jnp.where(lower, two, one)
-        target[HALO : HALO + CZ] = density[:, rows]
-        target[HALO + CZ : PZ] = jnp.where(lower, one, two)
-
-
-def edge_x_kernel(table, density, z_even, z_odd, y_even, y_odd, waves, even, odd, padded, held, sems):
-    wait = TABLES.copies(table, {"into_y": held}, sems, {})
-    lower = is_even("core")
-    one, two = z_even[...], z_odd[...]
-    middle = slice(HALO, HALO + CY)
-    padded[0:HALO, middle] = jnp.where(lower, two, one)
-    padded[HALO : HALO + CZ, middle] = density[...]
-    padded[HALO + CZ : PZ, middle] = jnp.where(lower, one, two)
-    lower = is_even("gy")
-    one, two = y_even[...], y_odd[...]
-    padded[:, 0:HALO] = jnp.where(lower, two, one)
-    padded[:, HALO + CY : PY] = jnp.where(lower, one, two)
-
-    into_y = wait("into_y")[:, : 3 * PY].astype(bf16)
-    place = lane((GROUP, 128)) // HALO
-    left = right = jnp.zeros((GROUP, 128), f32)
-    for j in range(8):
-        rows = []
-        for pair in range(3):
-            z = 6 * j + 2 * pair
-            high, low = halves(jnp.concatenate([padded[z], padded[z + 1]], axis=1))
-            wave = dot(into_y, jnp.concatenate([high, high, low], axis=0))
-            waves[z], waves[z + 1] = wave[:, :128], wave[:, 128:]
-            rows += [wave[:, :128], wave[:, 128:]]
-        for i in range(2):
-            group = jnp.concatenate(rows[3 * i : 3 * i + 3], axis=0)
-            shift = (2 * j + i) * HALO
-            left = jnp.where(place == 2 * j + i, pltpu.roll(group, shift, 1) if shift else group, left)
-            shift = (shift - (CX - HALO)) % 128
-            right = jnp.where(place == 2 * j + i, pltpu.roll(group, shift, 1) if shift else group, right)
+def edge_x_kernel(density, even, odd):
+    place = lane((EDGE, 128)) // HALO
+    left = right = jnp.zeros((EDGE, 128), f32)
+    for j in range(16):
+        rows = density[2 * j : 2 * j + 2].reshape(EDGE, 128)
+        shift = j * HALO
+        left = jnp.where(place == j, pltpu.roll(rows, shift, 1) if shift else rows, left)
+        shift = (shift - (CX - HALO)) % 128
+        right = jnp.where(place == j, pltpu.roll(rows, shift, 1) if shift else rows, right)
     lower = is_even("gx")
     even[...] = jnp.where(lower, right, left)
     odd[...] = jnp.where(lower, left, right)
 
 
-def near_kernel(
-    table, waves, x_even, x_odd, out, wave_x, wave_z, held_g, held_ix, held_y, held_ox, sems
-):
-    held = {"into_x": held_ix, "gains": held_g, "into_y": held_y, "out_x": held_ox}
-    wait = TABLES.copies(table, held, sems, {})
-    lanes = lane((GROUP, 128))
+def near_x_kernel(table, density, x_even, x_odd, waves, even, odd, held, sems):
+    wait = TABLES.copies(table, {"into_x": held}, sems, {})
+    lanes = lane((EDGE, 128))
     lower = is_even("gx")
     one, two = x_even[...], x_odd[...]
     left, right = jnp.where(lower, two, one), jnp.where(lower, one, two)
-    into_x = wait("into_x").astype(bf16)
+    groups = []
     for j in range(16):
-        rows = waves[3 * j : 3 * j + 3].reshape(GROUP, 128)
+        rows = density[2 * j : 2 * j + 2].reshape(EDGE, 128)
         to_left, to_right = (-HALO * j) % 128, (HALO - HALO * j) % 128
         ends = jnp.where(
             lanes < HALO,
@@ -384,40 +328,161 @@
         low = ends - high
         ends = (high + pltpu.roll(high, 2 * HALO, 1) + pltpu.roll(low, 4 * HALO, 1)).astype(bf16)
         high, low = halves(rows)
-        wave = dot(jnp.concatenate([high, high, low, ends], axis=1), into_x)
-        for i in range(3):
-            wave_x[3 * j + i] = wave[i * PY : (i + 1) * PY]
-
+        groups.append(jnp.concatenate([high, high, low, ends], axis=1))
+    into_x = wait("into_x").astype(bf16)
+    for j in range(4):
+        wave = dot(jnp.concatenate(groups[4 * j : 4 * j + 4], axis=0), into_x)
+        waves[8 * j : 8 * j + 8] = wave.reshape(8, CY, LANES)
+
+    place = lane((4 * HALO, 128)) // TAIL
+    start = jnp.where(is_even("gy"), CY - HALO, 0)
+    for target, first in ((even, start), (odd, CY - HALO - start)):
+        rows = pl.ds(pl.multiple_of(first, 8), HALO)
+        target[0:CZ] = waves[:, rows, pl.ds(0, 128)]
+        total = None
+        for j in range(8):
+            tail = waves[4 * j : 4 * j + 4, rows, pl.ds(128, 128)].reshape(4 * HALO, 128)
+            total = tail if j == 0 else jnp.where(place == j, pltpu.roll(tail, j * TAIL, 1), total)
+        target[CZ : CZ + 4] = total.reshape(4, HALO, 128)
+
+
+def near_y_kernel(table, waves_x, y_even, y_odd, waves, even, odd, held, sems):
+    wait = TABLES.copies(table, {"into_y": held}, sems, {})
+    lower = is_even("gy")
+    one, two = y_even[...], y_odd[...]
+    before, after = jnp.where(lower, two, one), jnp.where(lower, one, two)
+    into_y = wait("into_y")[:, : 3 * PY].astype(bf16)
+    tails = [ends[CZ : CZ + 4].reshape(4 * HALO, 128) for ends in (before, after)]
+    for j in range(8):
+        ends = [pltpu.roll(tail, -j * TAIL % 128, 1) if j else tail for tail in tails]
+        for i in range(4):
+            z, rows = 4 * j + i, slice(i * HALO, (i + 1) * HALO)
+            high, low = halves(
+                jnp.concatenate(
+                    [
+                        jnp.concatenate([before[z], ends[0][rows]], axis=1),
+                        waves_x[z],
+                        jnp.concatenate([after[z], ends[1][rows]], axis=1),
+                    ],
+                    axis=0,
+                )
+            )
+            waves[z] = dot(into_y, jnp.concatenate([high, high, low], axis=0))
+
+    place = lane((PY, 128)) // TAIL
+    start = jnp.where(is_even("core"), CZ - HALO, 0)
+    for target, first in ((even, start), (odd, CZ - HALO - start)):
+        target[0:HALO] = waves[pl.ds(first, HALO), :, pl.ds(0, 128)]
+        total = None
+        for j in range(HALO):
+            tail = waves[first + j, :, pl.ds(128, 128)]
+            total = tail if j == 0 else jnp.where(place == j, pltpu.roll(tail, j * TAIL, 1), total)
+        target[HALO] = total
+
+
+def sum_planes(gains, count, load, store):
+    window = [load(z) for z in range(2 * HALO)]
+    for z in range(count):
+        window.append(load(z + 2 * HALO))
+        total = gains[0] * window[HALO]
+        for d in range(1, HALO + 1):
+            total = total + gains[d] * (window[HALO - d] + window[HALO + d])
+        store(z, total)
+        window.pop(0)
+
+
+def back(planes, out_y, out_x):
+    rows = []
+    for plane in planes:
+        high, low = halves(plane)
+        rows.append(dot(out_y, jnp.concatenate([high, high, low], axis=0)))
+    high, low = halves(jnp.concatenate(rows, axis=0))
+    field = dot(jnp.concatenate([high, high, low], axis=1), out_x)
+    return [field[i * CY : (i + 1) * CY] for i in range(len(planes))]
+
+
+def inner_kernel(
+    table, waves, spectrum, out, sums, held_g, held_y, held_ox, held_lx, held_ly, sems
+):
+    held = {"gains": held_g, "into_y": held_y, "out_x": held_ox, "last_x": held_lx, "last_y": held_ly}
+    wait = TABLES.copies(table, held, sems, {"last_x": lax.axis_index("gx")})
     wait("gains")
 
     @pl.loop(0, PY // 8)
     def _(c):
-        for side in range(LANES // 128):
-            gain = [
-                held_g[side, pl.ds(pl.multiple_of(d * PY + c * 8, 8), 8)] for d in range(HALO + 1)
-            ]
-            row, column = pl.ds(pl.multiple_of(c * 8, 8), 8), pl.ds(side * 128, 128)
-            window = [wave_x[z, row, column] for z in range(2 * HALO)]
-            for z in range(CZ):
-                window.append(wave_x[z + 2 * HALO, row, column])
-                total = gain[0] * window[HALO]
-                for d in range(1, HALO + 1):
-                    total = total + gain[d] * (window[HALO - d] + window[HALO + d])
-                wave_z[z, row, column] = total
-                window.pop(0)
+        row = pl.ds(pl.multiple_of(c * 8, 8), 8)
+        for side in range(2):
+            column = pl.ds(side * 128, 128)
+            gains = [held_g[side, pl.ds(pl.multiple_of(d * PY + c * 8, 8), 8)] for d in range(HALO + 1)]
+
+            def store(i, value):
+                sums[i, row, column] = value
+
+            sum_planes(gains, CZ - 2 * HALO, lambda z: waves[z, row, column], store)
+
+    rows = spectrum[...].reshape(MX, 128)
+    field = transposed_dot(rows, wait("last_x"))
+    field = exact_dot(wait("last_y"), field)
+
+    def plane(z):
+        return field[z * CY : (z + 1) * CY]
 
     out_y = wait("into_y")[HALO : HALO + CY, : 3 * PY].astype(bf16)
     out_x = wait("out_x").astype(bf16)
-
-    for step in range(CZ // 4):
-        rows = []
+    for block in range(BZ):
+        before, here, after = plane(block), plane(block + 1), plane(block + 2)
+        inner = 2 <= block < 6
+        near = back([sums[4 * (block - 2) + i] for i in range(4)], out_y, out_x) if inner else None
+        for residue in range(COARSEN):
+            t = (residue + 0.5) / COARSEN - 0.5
+            value = (1.0 - abs(t)) * here + abs(t) * (before if t < 0 else after)
+            out[block * COARSEN + residue] = near[residue] + value if inner else value
+
+
+def outer_kernel(
+    table, waves, z_even, z_odd, inner, out, ends, sums, held_g, held_y, held_ox, sems
+):
+    held = {"gains": held_g, "into_y": held_y, "out_x": held_ox}
+    wait = TABLES.copies(table, held, sems, {})
+    out[HALO : CZ - HALO] = inner[HALO : CZ - HALO]
+    lower = is_even("core")
+    one, two = z_even[...], z_odd[...]
+    for i, end in enumerate((jnp.where(lower, two, one), jnp.where(lower, one, two))):
+        for j in range(HALO):
+            ends[i, j, :, 0:128] = end[j]
+            ends[i, j, :, 128:256] = pltpu.roll(end[HALO], -j * TAIL % 128, 1) if j else end[HALO]
+    wait("gains")
+
+    @pl.loop(0, PY // 8)
+    def _(c):
+        row = pl.ds(pl.multiple_of(c * 8, 8), 8)
+        for side in range(2):
+            column = pl.ds(side * 128, 128)
+            gains = [held_g[side, pl.ds(pl.multiple_of(d * PY + c * 8, 8), 8)] for d in range(HALO + 1)]
+
+            def low(z):
+                return ends[0, z, row, column] if z < HALO else waves[z - HALO, row, column]
+
+            def high(z):
+                z += CZ - 2 * HALO
+                return waves[z, row, column] if z < CZ else ends[1, z - CZ, row, column]
+
+            def store(first):
+                def put(i, value):
+                    sums[first + i, row, column] = value
+
+                return put
+
+            sum_planes(gains, HALO, low, store(0))
+            sum_planes(gains, HALO, high, store(HALO))
+
+    out_y = wait("into_y")[HALO : HALO + CY, : 3 * PY].astype(bf16)
+    out_x = wait("out_x").astype(bf16)
+    for step in range(4):
+        near = back([sums[4 * step + i] for i in range(4)], out_y, out_x)
+        first = 4 * step + (CZ - 2 * HALO if step >= 2 else 0)
         for i in range(4):
-            high, low = halves(wave_z[step * 4 + i])
-            rows.append(dot(out_y, jnp.concatenate([high, high, low], axis=0)))
-        high, low = halves(jnp.concatenate(rows, axis=0))
-        field = dot(jnp.concatenate([high, high, low], axis=1), out_x)
-        for i in range(4):
-            out[step * 4 + i] = field[i * CY : (i + 1) * CY]
+            out[first + i] = inner[first + i] + near[i]
 
 
 def call(kernel, outs, arrays=0, tables=(), scratch=(), us=1.0):
@@ -445,45 +510,55 @@
     peers = lax.axis_size(axis)
     low_first = [(i, i + 1 if i % 2 == 0 else i - 1) for i in range(peers)]
     high_first = [(i, (i + 1 if i % 2 else i - 1) % peers) for i in range(peers)]
-    odd = lax.ppermute(odd, axis, high_first)
-    return lax.ppermute(even, axis, low_first), odd
+    even = lax.ppermute(even, axis, low_first)
+    return even, lax.ppermute(odd, axis, high_first)
 
 
 def body(density):
     table = jnp.asarray(TABLES.array)
-    charges, even, odd = call(charge_kernel, [(SHARE, 16, 128), (HALO, CY, CX), (HALO, CY, CX)], 1, us=0.5)(density)
+    charges = call(charge_kernel, (SHARE, 16, 128), 1, us=1.0)(density)
     charges = lax.all_to_all(charges, ("gx", "core"), 0, 0, tiled=True)
-    z_ends = exchange(even, odd, ("yh", "core"))
-    charges, z_ends = lax.optimization_barrier((charges, z_ends))
-    spectrum = call(first_kernel, (2 * GY, 2, 8, 128), 1, ["first_x"], us=1.3)(table, charges)
+
+    x_ends = call(edge_x_kernel, [(EDGE, 128)] * 2, 1, us=0.2)(density)
+    x_ends = exchange(*x_ends, "gx")
+    charges, x_ends = lax.optimization_barrier((charges, x_ends))
+
+    spectrum = call(first_kernel, (2 * GY, 2, 8, 128), 1, ["first_x"], us=1.5)(table, charges)
     spectrum = lax.all_to_all(spectrum, ("gy", "yh"), 0, 0, tiled=True)
 
-    y_ends = call(edge_y_kernel, [(PZ, HALO, CX)] * 2, 3, us=0.2)(density, *z_ends)
+    waves_x, *y_ends = call(
+        near_x_kernel, [(CZ, CY, LANES), (CZ + 4, HALO, 128), (CZ + 4, HALO, 128)], 3, ["into_x"], us=1.0
+    )(table, density, *x_ends)
     spectrum, _ = lax.optimization_barrier((spectrum, y_ends))
     y_ends = exchange(*y_ends, "gy")
-    spectrum = call(filter_kernel, (SHARE, KX, 128), 1, ["full_y", "into_z", "gain", "out_z", "out_y"], us=3.0)(
-        table, spectrum
-    )
+
+    spectrum = call(
+        filter_kernel, (SHARE, KX, 128), 1, ["full_y", "into_z", "gain", "out_z", "out_y"], us=3.0
+    )(table, spectrum)
     y_ends, _ = lax.optimization_barrier((y_ends, spectrum))
     spectrum = lax.all_to_all(spectrum, ("gx", "core"), 0, 0, tiled=True)
-    waves, even, odd = call(
-        edge_x_kernel,
-        [(PZ, PY, CX), (GROUP, 128), (GROUP, 128)],
-        5,
-        ["into_y"],
-        [pltpu.VMEM((PZ, PY, CX), f32)],
-        us=2.0,
-    )(table, density, *z_ends, *y_ends)
-    x_ends = exchange(even, odd, "gx")
-    near = call(
-        near_kernel,
+
+    waves, *z_ends = call(
+        near_y_kernel, [(CZ, PY, LANES), (HALO + 1, PY, 128), (HALO + 1, PY, 128)], 3, ["into_y"], us=1.5
+    )(table, waves_x, *y_ends)
+    z_ends = exchange(*z_ends, ("yh", "core"))
+
+    inner = call(
+        inner_kernel,
         (CZ, CY, CX),
-        3,
-        ["gains", "into_x", "into_y", "out_x"],
-        [pltpu.VMEM((PZ, PY, LANES), f32), pltpu.VMEM((CZ, PY, LANES), f32)],
-        us=6.0,
-    )(table, waves, *x_ends)
-    return call(last_kernel, (CZ, CY, CX), 2, ["last_x", "last_y"], us=1.8)(table, spectrum, near)
+        2,
+        ["gains", "into_y", "out_x", "last_x", "last_y"],
+        [pltpu.VMEM((CZ - 2 * HALO, PY, LANES), f32)],
+        us=4.0,
+    )(table, waves, spectrum)
+    return call(
+        outer_kernel,
+        (CZ, CY, CX),
+        4,
+        ["gains", "into_y", "out_x"],
+        [pltpu.VMEM((2, HALO, PY, LANES), f32), pltpu.VMEM((2 * HALO, PY, LANES), f32)],
+        us=3.0,
+    )(table, waves, *z_ends, inner)
 
 
 def solution(mesh):

time: 88.4 us -> 86.5 us (0.979)
  waiting for transfers between devices: 13.8 us -> 10.7 us
  Pallas kernels: 16.7 us -> 18.2 us
  starting transfers between devices: 56.1 us -> 54.6 us
  local copies, waits for them, and re-layouts: 1.04 us -> 2.08 us
    all_to_all x1, starting transfers between devices: 4.9 us -> 8.68 us  [body(): spectrum = lax.all_to_all(spectrum, ('gx', 'core'), 0, 0, tiled=True)]
    all_to_all x1, waiting for transfers between devices: 2.98 us -> 0.19 us  [body(): spectrum = lax.all_to_all(spectrum, ('gx', 'core'), 0, 0, tiled=True)]
    all_to_all x1, starting transfers between devices: 12.4 us -> 9.68 us  [body(): spectrum = lax.all_to_all(spectrum, ('gy', 'yh'), 0, 0, tiled=True)]
    ppermute x6, starting transfers between devices: 27 us -> 24.4 us  [the longest x3 16 us: exchange(): return (even, lax.ppermute(odd, axis, high_first))]
    pallas_call x6 -> x7, Pallas kernels: 13.3 us -> 14.8 us  [the longest x1 3.56 us: body(): call(outer_kernel, (CZ, CY, CX), 4, ['gains', 'into_y', 'out_x'], [pltpu....]
    all_to_all x1, waiting for transfers between devices: 1.11 us -> 0.01 us  [body(): spectrum = lax.all_to_all(spectrum, ('gy', 'yh'), 0, 0, tiled=True)]
    unnamed x4 -> x6, local copies, waits for them, and re-layouts: 1.04 us -> 2.08 us
  transfers between devices with their start and end apart: 9 -> 9, of which waited for: 4 -> 3; matrix products, arithmetic and copies ran while one was open for 0% -> 0% of each run, Pallas kernels for 11% -> 13%
where the time goes in v4:
time: 86.5 us; the launch traced here: 85.7 us
  starting transfers between devices  54.6 us (63%)
  Pallas kernels  18.2 us (21%)
  waiting for transfers between devices  10.7 us (12%)
  local copies, waits for them, and re-layouts  2.08 us (2%)
    ppermute x3, starting transfers between devices, exchange(): return (even, lax.ppermute(odd, axis, high_first))  16 us
    all_to_all x1, starting transfers between devices, body(): charges = lax.all_to_all(charges, ('gx', 'core'), 0, 0, tiled=True)  11.8 us
    ppermute x3, waiting for transfers between devices, exchange(): return (even, lax.ppermute(odd, axis, high_first))  10.5 us
    all_to_all x1, starting transfers between devices, body(): spectrum = lax.all_to_all(spectrum, ('gy', 'yh'), 0, 0, tiled=True)  9.68 us
    all_to_all x1, starting transfers between devices, body(): spectrum = lax.all_to_all(spectrum, ('gx', 'core'), 0, 0, tiled=True)  8.68 us
    ppermute x3, starting transfers between devices, exchange(): even = lax.ppermute(even, axis, low_first)  8.45 us
    pallas_call x1, Pallas kernels, body(): call(outer_kernel, (CZ, CY, CX), 4, ['gains', 'into_y', 'out_x'], [pltpu....  3.56 us
    pallas_call x1, Pallas kernels, body(): call(inner_kernel, (CZ, CY, CX), 2, ['gains', 'into_y', 'out_x', 'last_x'...  3.49 us
  transfers between devices with their start and end apart: 9, of which 3 were waited for; matrix products, arithmetic and copies ran while one was open for 0% of the time, Pallas kernels for 13%

profile of v4, /device:TPU:1, one launch (start us, length us, event | category | flops | bytes accessed | tf_op | source)
XLA Modules:
  0.0 85.7 jit_solution(2208557846318428135)
XLA Ops:
  0.0 0.0 copy-start
  0.0 1.0 %copy-done = f32[32,32,128]{2,1,0:T(8,128)S(1)} copy-done((f32[32,32,128]{2,1,0:T(8,128)S(1)}, f32[32,32,128]{2,1,0:T(8,128)}, u32[]{:S(2)}) %copy-start) | copy-done | bytes 524312
  1.0 0.0 copy-start.2
  1.0 1.1 %charge_kernel.1 = f32[16,16,128]{2,1,0:T(8,128)} custom-call(f32[32,32,128]{2,1,0:T(8,128)S(1)} %copy-done), custom_call_target="tpu_custom_call" | custom-call | flops 1000000000 | bytes 3000000 | tf_op jit(solution)/shard_map/charge_kernel/pallas_call | solution.py:519
  2.2 11.8 %all-to-all-start = ((f32[16,16,128]{2,1,0:T(8,128)}), f32[16,16,128]{2,1,0:T(8,128)S(1)}, u32[]{:S(2)}, u32[]{:S(2)}) async-start(f32[16,16,128]{2,1,0:T(8,128)} %charge_kernel.1), calls=%async_computation | async-start | bytes 262144 | tf_op jit(solution)/shard_map/all_to_all | solution.py:520
  14.0 0.0 copy-start.1
  14.0 1.0 %copy-done.1 = f32[32,32,128]{2,1,0:T(8,128)S(1)} copy-done((f32[32,32,128]{2,1,0:T(8,128)S(1)}, f32[32,32,128]{2,1,0:T(8,128)}, u32[]{:S(2)}) %copy-start.1) | copy-done | bytes 524312
  15.0 0.3 edge_x_kernel.1
  15.4 3.3 %collective-permute-start = (f32[64,128]{1,0:T(8,128)S(1)}, f32[64,128]{1,0:T(8,128)S(1)}, u32[]{:S(2)}, u32[]{:S(2)}) collective-permute-start(f32[64,128]{1,0:T(8,128)S(1)} %get-tuple-element.19), channel_id=1, source_target_pairs={{0,64},{64,0},{128,192},{192,128},{256,320},{320,256},{384,448},{4... | collective-permute-start | bytes 98312 | tf_op jit(solution)/shard_map/ppermute | solution.py:513
  18.7 4.3 %collective-permute-start.1 = (f32[64,128]{1,0:T(8,128)S(1)}, f32[64,128]{1,0:T(8,128)S(1)}, u32[]{:S(2)}, u32[]{:S(2)}) collective-permute-start(f32[64,128]{1,0:T(8,128)S(1)} %get-tuple-element.20), channel_id=1, source_target_pairs={{0,448},{64,128},{128,64},{192,256},{256,192},{320,384},{384,320},... | collective-permute-start | bytes 98312 | tf_op jit(solution)/shard_map/ppermute | solution.py:514
  23.0 0.0 collective-permute-done.x_even
  23.0 1.5 %collective-permute-done.1.x_odd = f32[64,128]{1,0:T(8,128)S(1)} collective-permute-done((f32[64,128]{1,0:T(8,128)S(1)}, f32[64,128]{1,0:T(8,128)S(1)}, u32[]{:S(2)}, u32[]{:S(2)}) %collective-permute-start.1) | collective-permute-done | bytes 32800 | tf_op jit(solution)/shard_map/ppermute | solution.py:514
  24.5 0.0 all-to-all-done.charges
  24.5 2.0 %first_kernel.1 = f32[32,2,8,128]{3,2,1,0:T(8,128)} custom-call(f32[49152,128]{1,0:T(8,128)} %constant.2.clone.table, f32[16,16,128]{2,1,0:T(8,128)S(1)} %all-to-all-done.charges), custom_call_target="tpu_custom_call" | custom-call | flops 1500000000 | bytes 4500000 | tf_op jit(solution)/shard_map/first_kernel/pallas_call | solution.py:526
  26.5 9.7 %all-to-all-start.1 = ((f32[32,2,8,128]{3,2,1,0:T(8,128)}), f32[32,2,8,128]{3,2,1,0:T(8,128)S(1)}, u32[]{:S(2)}, u32[]{:S(2)}) async-start(f32[32,2,8,128]{3,2,1,0:T(8,128)} %first_kernel.1), calls=%async_computation.1 | async-start | bytes 524288 | tf_op jit(solution)/shard_map/all_to_all | solution.py:527
  36.2 0.0 copy-done.2
  36.2 2.9 %near_x_kernel.1 = (f32[32,32,256]{2,1,0:T(8,128)S(1)}, f32[36,8,128]{2,1,0:T(8,128)S(1)}, f32[36,8,128]{2,1,0:T(8,128)S(1)}) custom-call(f32[49152,128]{1,0:T(8,128)} %constant.2.clone.table, f32[32,32,128]{2,1,0:T(8,128)S(1)} %copy-done.2, f32[64,128]{1,0:T(8,128)S(1)} %collective-permute-done.x_even, f32[64,128]{1,0:T(8,128)S(1)} %collective-permute-done.1.x_odd), custom_call_target="tpu_custom_call" | custom-call | flops 1000000000 | bytes 3000000 | tf_op jit(solution)/shard_map/near_x_kernel/pallas_call | solution.py:529
  39.1 3.1 %collective-permute-start.2 = (f32[36,8,128]{2,1,0:T(8,128)S(1)}, f32[36,8,128]{2,1,0:T(8,128)S(1)}, u32[]{:S(2)}, u32[]{:S(2)}) collective-permute-start(f32[36,8,128]{2,1,0:T(8,128)S(1)} %get-tuple-element.24), channel_id=1, source_target_pairs={{0,4},{4,0},{8,12},{12,8},{16,20},{20,16},{24,28},{28,24},{32,36},... | collective-permute-start | bytes 442376 | tf_op jit(solution)/shard_map/ppermute | solution.py:513
  42.3 6.2 %collective-permute-start.3 = (f32[36,8,128]{2,1,0:T(8,128)S(1)}, f32[36,8,128]{2,1,0:T(8,128)S(1)}, u32[]{:S(2)}, u32[]{:S(2)}) collective-permute-start(f32[36,8,128]{2,1,0:T(8,128)S(1)} %get-tuple-element.25), channel_id=1, source_target_pairs={{0,60},{4,8},{8,4},{12,16},{16,12},{20,24},{24,20},{28,32},{32,28}... | collective-permute-start | bytes 442376 | tf_op jit(solution)/shard_map/ppermute | solution.py:514
  48.4 0.0 all-to-all-done.1.spectrum
  48.5 3.4 %filter_kernel.1 = f32[16,16,128]{2,1,0:T(8,128)} custom-call(f32[49152,128]{1,0:T(8,128)} %constant.2.clone.table, f32[32,2,8,128]{3,2,1,0:T(8,128)S(1)} %all-to-all-done.1.spectrum), custom_call_target="tpu_custom_call" | custom-call | flops 3000000000 | bytes 9000000 | tf_op jit(solution)/shard_map/filter_kernel/pallas_call | solution.py:535
  51.9 8.7 %all-to-all-start.2 = ((f32[16,16,128]{2,1,0:T(8,128)}), f32[16,16,128]{2,1,0:T(8,128)S(1)}, u32[]{:S(2)}, u32[]{:S(2)}) async-start(f32[16,16,128]{2,1,0:T(8,128)} %filter_kernel.1), calls=%async_computation.2 | async-start | bytes 262144 | tf_op jit(solution)/shard_map/all_to_all | solution.py:539
  60.5 0.0 collective-permute-done.2.y_even
  60.5 0.0 collective-permute-done.3.y_odd
  60.6 1.4 %near_y_kernel.1 = (f32[32,48,256]{2,1,0:T(8,128)S(1)}, f32[9,48,128]{2,1,0:T(8,128)S(1)}, f32[9,48,128]{2,1,0:T(8,128)S(1)}) custom-call(f32[49152,128]{1,0:T(8,128)} %constant.2.clone.table, f32[32,32,256]{2,1,0:T(8,128)S(1)} %get-tuple-element.23.waves_x, f32[36,8,128]{2,1,0:T(8,128)S(1)} %collective-permute-done.2.y_even, ...), custom_call_target="tpu_custom_call" | custom-call | flops 1500000000 | bytes 4500000 | tf_op jit(solution)/shard_map/near_y_kernel/pallas_call | solution.py:541
  62.0 2.0 %collective-permute-start.4 = (f32[9,48,128]{2,1,0:T(8,128)S(1)}, f32[9,48,128]{2,1,0:T(8,128)S(1)}, u32[]{:S(2)}, u32[]{:S(2)}) collective-permute-start(f32[9,48,128]{2,1,0:T(8,128)S(1)} %get-tuple-element.31), channel_id=1, source_target_pairs={{0,1},{1,0},{2,3},{3,2},{4,5},{5,4},{6,7},{7,6},{8,9},{9,8},{10,11... | collective-permute-start | bytes 663560 | tf_op jit(solution)/shard_map/ppermute | solution.py:513
  64.0 5.5 %collective-permute-start.5 = (f32[9,48,128]{2,1,0:T(8,128)S(1)}, f32[9,48,128]{2,1,0:T(8,128)S(1)}, u32[]{:S(2)}, u32[]{:S(2)}) collective-permute-start(f32[9,48,128]{2,1,0:T(8,128)S(1)} %get-tuple-element.32), channel_id=1, source_target_pairs={{0,3},{1,2},{2,1},{3,0},{4,7},{5,6},{6,5},{7,4},{8,11},{9,10},{10,... | collective-permute-start | bytes 663560 | tf_op jit(solution)/shard_map/ppermute | solution.py:514
  69.5 0.2 all-to-all-done.2.spectrum
  69.7 3.5 %inner_kernel.1.inner = f32[32,32,128]{2,1,0:T(8,128)S(1)} custom-call(f32[49152,128]{1,0:T(8,128)} %constant.2.clone.table, f32[32,48,256]{2,1,0:T(8,128)S(1)} %get-tuple-element.30.waves, f32[16,16,128]{2,1,0:T(8,128)S(1)} %all-to-all-done.2.spectrum), custom_call_target="tpu_custom_call" | custom-call | flops 4000000000 | bytes 12000000 | tf_op jit(solution)/shard_map/inner_kernel/pallas_call | solution.py:546
  73.2 0.0 collective-permute-done.4.z_even
  73.2 9.0 %collective-permute-done.5.z_odd = f32[9,48,128]{2,1,0:T(8,128)S(1)} collective-permute-done((f32[9,48,128]{2,1,0:T(8,128)S(1)}, f32[9,48,128]{2,1,0:T(8,128)S(1)}, u32[]{:S(2)}, u32[]{:S(2)}) %collective-permute-start.5) | collective-permute-done | bytes 221216 | tf_op jit(solution)/shard_map/ppermute | solution.py:514
  82.2 3.6 %outer_kernel.1 = f32[32,32,128]{2,1,0:T(8,128)} custom-call(f32[49152,128]{1,0:T(8,128)} %constant.2.clone.table, f32[32,48,256]{2,1,0:T(8,128)S(1)} %get-tuple-element.30.waves, f32[9,48,128]{2,1,0:T(8,128)S(1)} %collective-permute-done.4.z_even, f32[9,48,128]{2,1,0:T(8,128)S(1)} %collective-permute-done.5.z_odd, f32[32,32,128]{2,1,0:T(8,128)S(1)} %inner_kernel.1.inner), custom_call_target="tpu_custom_call" | custom-call | flops 3000000000 | bytes 9000000 | tf_op jit(solution)/shard_map/outer_kernel/pallas_call | solution.py:554
Async XLA Ops:
  0.0 1.0 %copy-start = (f32[32,32,128]{2,1,0:T(8,128)S(1)}, f32[32,32,128]{2,1,0:T(8,128)}, u32[]{:S(2)}) copy-start(f32[32,32,128]{2,1,0:T(8,128)} %density.5) | copy-start | bytes 1572868
  1.0 35.2 %copy-start.2 = (f32[32,32,128]{2,1,0:T(8,128)S(1)}, f32[32,32,128]{2,1,0:T(8,128)}, u32[]{:S(2)}) copy-start(f32[32,32,128]{2,1,0:T(8,128)} %density.5) | copy-start | bytes 1572868
  2.2 22.4 %all-to-all-start = ((f32[16,16,128]{2,1,0:T(8,128)}), f32[16,16,128]{2,1,0:T(8,128)S(1)}, u32[]{:S(2)}, u32[]{:S(2)}) async-start(f32[16,16,128]{2,1,0:T(8,128)} %charge_kernel.1), calls=%async_computation | async-start | bytes 262144 | tf_op jit(solution)/shard_map/all_to_all | solution.py:520
  14.0 1.0 %copy-start.1 = (f32[32,32,128]{2,1,0:T(8,128)S(1)}, f32[32,32,128]{2,1,0:T(8,128)}, u32[]{:S(2)}) copy-start(f32[32,32,128]{2,1,0:T(8,128)} %density.5) | copy-start | bytes 1572868
  15.4 7.6 %collective-permute-start = (f32[64,128]{1,0:T(8,128)S(1)}, f32[64,128]{1,0:T(8,128)S(1)}, u32[]{:S(2)}, u32[]{:S(2)}) collective-permute-start(f32[64,128]{1,0:T(8,128)S(1)} %get-tuple-element.19), channel_id=1, source_target_pairs={{0,64},{64,0},{128,192},{192,128},{256,320},{320,256},{384,448},{4... | collective-permute-start | bytes 98312 | tf_op jit(solution)/shard_map/ppermute | solution.py:513
  18.7 5.9 %collective-permute-start.1 = (f32[64,128]{1,0:T(8,128)S(1)}, f32[64,128]{1,0:T(8,128)S(1)}, u32[]{:S(2)}, u32[]{:S(2)}) collective-permute-start(f32[64,128]{1,0:T(8,128)S(1)} %get-tuple-element.20), channel_id=1, source_target_pairs={{0,448},{64,128},{128,64},{192,256},{256,192},{320,384},{384,320},... | collective-permute-start | bytes 98312 | tf_op jit(solution)/shard_map/ppermute | solution.py:514
  26.5 21.9 %all-to-all-start.1 = ((f32[32,2,8,128]{3,2,1,0:T(8,128)}), f32[32,2,8,128]{3,2,1,0:T(8,128)S(1)}, u32[]{:S(2)}, u32[]{:S(2)}) async-start(f32[32,2,8,128]{3,2,1,0:T(8,128)} %first_kernel.1), calls=%async_computation.1 | async-start | bytes 524288 | tf_op jit(solution)/shard_map/all_to_all | solution.py:527
  39.1 21.4 %collective-permute-start.2 = (f32[36,8,128]{2,1,0:T(8,128)S(1)}, f32[36,8,128]{2,1,0:T(8,128)S(1)}, u32[]{:S(2)}, u32[]{:S(2)}) collective-permute-start(f32[36,8,128]{2,1,0:T(8,128)S(1)} %get-tuple-element.24), channel_id=1, source_target_pairs={{0,4},{4,0},{8,12},{12,8},{16,20},{20,16},{24,28},{28,24},{32,36},... | collective-permute-start | bytes 442376 | tf_op jit(solution)/shard_map/ppermute | solution.py:513
  42.3 18.3 %collective-permute-start.3 = (f32[36,8,128]{2,1,0:T(8,128)S(1)}, f32[36,8,128]{2,1,0:T(8,128)S(1)}, u32[]{:S(2)}, u32[]{:S(2)}) collective-permute-start(f32[36,8,128]{2,1,0:T(8,128)S(1)} %get-tuple-element.25), channel_id=1, source_target_pairs={{0,60},{4,8},{8,4},{12,16},{16,12},{20,24},{24,20},{28,32},{32,28}... | collective-permute-start | bytes 442376 | tf_op jit(solution)/shard_map/ppermute | solution.py:514
  51.9 17.8 %all-to-all-start.2 = ((f32[16,16,128]{2,1,0:T(8,128)}), f32[16,16,128]{2,1,0:T(8,128)S(1)}, u32[]{:S(2)}, u32[]{:S(2)}) async-start(f32[16,16,128]{2,1,0:T(8,128)} %filter_kernel.1), calls=%async_computation.2 | async-start | bytes 262144 | tf_op jit(solution)/shard_map/all_to_all | solution.py:539
  62.0 11.2 %collective-permute-start.4 = (f32[9,48,128]{2,1,0:T(8,128)S(1)}, f32[9,48,128]{2,1,0:T(8,128)S(1)}, u32[]{:S(2)}, u32[]{:S(2)}) collective-permute-start(f32[9,48,128]{2,1,0:T(8,128)S(1)} %get-tuple-element.31), channel_id=1, source_target_pairs={{0,1},{1,0},{2,3},{3,2},{4,5},{5,4},{6,7},{7,6},{8,9},{9,8},{10,11... | collective-permute-start | bytes 663560 | tf_op jit(solution)/shard_map/ppermute | solution.py:513
  64.0 18.2 %collective-permute-start.5 = (f32[9,48,128]{2,1,0:T(8,128)S(1)}, f32[9,48,128]{2,1,0:T(8,128)S(1)}, u32[]{:S(2)}, u32[]{:S(2)}) collective-permute-start(f32[9,48,128]{2,1,0:T(8,128)S(1)} %get-tuple-element.32), channel_id=1, source_target_pairs={{0,3},{1,2},{2,1},{3,0},{4,7},{5,6},{6,5},{7,4},{8,11},{9,10},{10,... | collective-permute-start | bytes 663560 | tf_op jit(solution)/shard_map/ppermute | solution.py:514

commit v5 on v3

--- a/solution.py
+++ b/solution.py
@@ -296,7 +296,7 @@
             out[peer * 2 + core] = message
 
 
-def last_kernel(table, spectrum, near, out, held_x, held_y, sems):
+def far_kernel(table, spectrum, out, held_x, held_y, sems):
     held = {"last_x": held_x, "last_y": held_y}
     wait = TABLES.copies(table, held, sems, {"last_x": lax.axis_index("gx")})
     rows = spectrum[...].reshape(MX, 128)
@@ -312,7 +312,7 @@
             t = (residue + 0.5) / COARSEN - 0.5
             value = (1.0 - abs(t)) * here + abs(t) * (before if t < 0 else after)
             z = block * COARSEN + residue
-            out[z] = near[z] + value
+            out[z] = value
 
 
 def edge_y_kernel(density, z_even, z_odd, even, odd):
@@ -362,7 +362,7 @@
 
 
 def near_kernel(
-    table, waves, x_even, x_odd, out, wave_x, wave_z, held_g, held_ix, held_y, held_ox, sems
+    table, waves, x_even, x_odd, far, out, wave_x, wave_z, held_g, held_ix, held_y, held_ox, sems
 ):
     held = {"into_x": held_ix, "gains": held_g, "into_y": held_y, "out_x": held_ox}
     wait = TABLES.copies(table, held, sems, {})
@@ -417,7 +417,7 @@
         high, low = halves(jnp.concatenate(rows, axis=0))
         field = dot(jnp.concatenate([high, high, low], axis=1), out_x)
         for i in range(4):
-            out[step * 4 + i] = field[i * CY : (i + 1) * CY]
+            out[step * 4 + i] = far[step * 4 + i] + field[i * CY : (i + 1) * CY]
 
 
 def call(kernel, outs, arrays=0, tables=(), scratch=(), us=1.0):
@@ -451,14 +451,15 @@
 
 def body(density):
     table = jnp.asarray(TABLES.array)
-    charges, even, odd = call(charge_kernel, [(SHARE, 16, 128), (HALO, CY, CX), (HALO, CY, CX)], 1, us=0.5)(density)
+    charges, *z_ends = call(
+        charge_kernel, [(SHARE, 16, 128), (HALO, CY, CX), (HALO, CY, CX)], 1, us=1.0
+    )(density)
     charges = lax.all_to_all(charges, ("gx", "core"), 0, 0, tiled=True)
-    z_ends = exchange(even, odd, ("yh", "core"))
-    charges, z_ends = lax.optimization_barrier((charges, z_ends))
+    z_ends = exchange(*z_ends, ("yh", "core"))
     spectrum = call(first_kernel, (2 * GY, 2, 8, 128), 1, ["first_x"], us=1.3)(table, charges)
     spectrum = lax.all_to_all(spectrum, ("gy", "yh"), 0, 0, tiled=True)
 
-    y_ends = call(edge_y_kernel, [(PZ, HALO, CX)] * 2, 3, us=0.2)(density, *z_ends)
+    y_ends = call(edge_y_kernel, [(PZ, HALO, CX)] * 2, 3, us=10.0)(density, *z_ends)
     spectrum, _ = lax.optimization_barrier((spectrum, y_ends))
     y_ends = exchange(*y_ends, "gy")
     spectrum = call(filter_kernel, (SHARE, KX, 128), 1, ["full_y", "into_z", "gain", "out_z", "out_y"], us=3.0)(
@@ -472,18 +473,18 @@
         5,
         ["into_y"],
         [pltpu.VMEM((PZ, PY, CX), f32)],
-        us=2.0,
+        us=10.0,
     )(table, density, *z_ends, *y_ends)
     x_ends = exchange(even, odd, "gx")
-    near = call(
+    far = call(far_kernel, (CZ, CY, CX), 1, ["last_x", "last_y"], us=5.0)(table, spectrum)
+    return call(
         near_kernel,
         (CZ, CY, CX),
-        3,
+        4,
         ["gains", "into_x", "into_y", "out_x"],
         [pltpu.VMEM((PZ, PY, LANES), f32), pltpu.VMEM((CZ, PY, LANES), f32)],
-        us=6.0,
-    )(table, waves, *x_ends)
-    return call(last_kernel, (CZ, CY, CX), 2, ["last_x", "last_y"], us=1.8)(table, spectrum, near)
+        us=0.1,
+    )(table, waves, *x_ends, far)
 
 
 def solution(mesh):

time: 88.4 us -> 74.2 us (0.84)
  waiting for transfers between devices: 13.8 us -> 2.77 us
  starting transfers between devices: 56.1 us -> 52.9 us
    ppermute x3, waiting for transfers between devices: 9.67 us -> 0.37 us  [exchange(): odd = lax.ppermute(odd, axis, high_first)]
    all_to_all x1, starting transfers between devices: 12.4 us -> 9.08 us  [body(): spectrum = lax.all_to_all(spectrum, ('gy', 'yh'), 0, 0, tiled=True)]
    all_to_all x1, waiting for transfers between devices: 2.98 us -> 0.01 us  [body(): spectrum = lax.all_to_all(spectrum, ('gx', 'core'), 0, 0, tiled=True)]
    all_to_all x1, waiting for transfers between devices: 1.11 us -> 2.39 us  [body(): spectrum = lax.all_to_all(spectrum, ('gy', 'yh'), 0, 0, tiled=True)]
  transfers between devices with their start and end apart: 9 -> 9, of which waited for: 4 -> 2; matrix products, arithmetic and copies ran while one was open for 0% -> 0% of each run, Pallas kernels for 11% -> 12%
where the time goes in v5:
time: 74.2 us; the launch traced here: 73.5 us
  starting transfers between devices  52.9 us (71%)
  Pallas kernels  16.7 us (23%)
  waiting for transfers between devices  2.77 us (4%)
  local copies, waits for them, and re-layouts  1.04 us (1%)
    ppermute x3, starting transfers between devices, exchange(): odd = lax.ppermute(odd, axis, high_first)  18.3 us
    all_to_all x1, starting transfers between devices, body(): charges = lax.all_to_all(charges, ('gx', 'core'), 0, 0, tiled=True)  11.8 us
    all_to_all x1, starting transfers between devices, body(): spectrum = lax.all_to_all(spectrum, ('gy', 'yh'), 0, 0, tiled=True)  9.08 us
    ppermute x3, starting transfers between devices, exchange(): return (lax.ppermute(even, axis, low_first), odd)  8.45 us
    pallas_call x1, Pallas kernels, body(): call(near_kernel, (CZ, CY, CX), 4, ['gains', 'into_x', 'into_y', 'out_x']...  6.97 us
    all_to_all x1, starting transfers between devices, body(): spectrum = lax.all_to_all(spectrum, ('gx', 'core'), 0, 0, tiled=True)  5.23 us
    pallas_call x1, Pallas kernels, body(): call(filter_kernel, (SHARE, KX, 128), 1, ['full_y', 'into_z', 'gain', 'ou...  3.38 us
    all_to_all x1, waiting for transfers between devices, body(): spectrum = lax.all_to_all(spectrum, ('gy', 'yh'), 0, 0, tiled=True)  2.39 us
  transfers between devices with their start and end apart: 9, of which 2 were waited for; matrix products, arithmetic and copies ran while one was open for 0% of the time, Pallas kernels for 12%

profile of v5, /device:TPU:1, one launch (start us, length us, event | category | flops | bytes accessed | tf_op | source)
XLA Modules:
  0.0 73.5 jit_solution(14826401464576824230)
XLA Ops:
  0.0 0.0 copy-start
  0.0 1.0 %copy-done = f32[32,32,128]{2,1,0:T(8,128)S(1)} copy-done((f32[32,32,128]{2,1,0:T(8,128)S(1)}, f32[32,32,128]{2,1,0:T(8,128)}, u32[]{:S(2)}) %copy-start) | copy-done | bytes 524312
  1.0 0.0 copy-start.1
  1.0 1.1 %charge_kernel.1 = (f32[16,16,128]{2,1,0:T(8,128)}, f32[8,32,128]{2,1,0:T(8,128)S(1)}, f32[8,32,128]{2,1,0:T(8,128)S(1)}) custom-call(f32[32,32,128]{2,1,0:T(8,128)S(1)} %copy-done), custom_call_target="tpu_custom_call" | custom-call | flops 1000000000 | bytes 3000000 | tf_op jit(solution)/shard_map/charge_kernel/pallas_call | solution.py:454
  2.2 11.8 %all-to-all-start = ((f32[16,16,128]{2,1,0:T(8,128)}), f32[16,16,128]{2,1,0:T(8,128)S(1)}, u32[]{:S(2)}, u32[]{:S(2)}) async-start(f32[16,16,128]{2,1,0:T(8,128)} %get-tuple-element.20), calls=%async_computation | async-start | bytes 262144 | tf_op jit(solution)/shard_map/all_to_all | solution.py:457
  14.0 2.0 %collective-permute-start = (f32[8,32,128]{2,1,0:T(8,128)S(1)}, f32[8,32,128]{2,1,0:T(8,128)S(1)}, u32[]{:S(2)}, u32[]{:S(2)}) collective-permute-start(f32[8,32,128]{2,1,0:T(8,128)S(1)} %get-tuple-element.16), channel_id=1, source_target_pairs={{0,1},{1,0},{2,3},{3,2},{4,5},{5,4},{6,7},{7,6},{8,9},{9,8},{10,11... | collective-permute-start | bytes 393224 | tf_op jit(solution)/shard_map/ppermute | solution.py:449
  16.0 7.7 %collective-permute-start.1 = (f32[8,32,128]{2,1,0:T(8,128)S(1)}, f32[8,32,128]{2,1,0:T(8,128)S(1)}, u32[]{:S(2)}, u32[]{:S(2)}) collective-permute-start(f32[8,32,128]{2,1,0:T(8,128)S(1)} %get-tuple-element.17), channel_id=1, source_target_pairs={{0,3},{1,2},{2,1},{3,0},{4,7},{5,6},{6,5},{7,4},{8,11},{9,10},{10,... | collective-permute-start | bytes 393224 | tf_op jit(solution)/shard_map/ppermute | solution.py:448
  23.8 0.0 all-to-all-done.charges
  23.8 2.0 %first_kernel.1 = f32[32,2,8,128]{3,2,1,0:T(8,128)} custom-call(f32[49152,128]{1,0:T(8,128)} %constant.2.clone.table, f32[16,16,128]{2,1,0:T(8,128)S(1)} %all-to-all-done.charges), custom_call_target="tpu_custom_call" | custom-call | flops 1300000000 | bytes 3900000 | tf_op jit(solution)/shard_map/first_kernel/pallas_call | solution.py:459
  25.8 9.1 %all-to-all-start.1 = ((f32[32,2,8,128]{3,2,1,0:T(8,128)}), f32[32,2,8,128]{3,2,1,0:T(8,128)S(1)}, u32[]{:S(2)}, u32[]{:S(2)}) async-start(f32[32,2,8,128]{3,2,1,0:T(8,128)} %first_kernel.1), calls=%async_computation.1 | async-start | bytes 524288 | tf_op jit(solution)/shard_map/all_to_all | solution.py:460
  34.9 0.0 collective-permute-done.z_even
  34.9 0.0 collective-permute-done.1.z_odd
  34.9 0.0 copy-done.1
  34.9 0.1 edge_y_kernel.1
  35.0 3.1 %collective-permute-start.2 = (f32[48,8,128]{2,1,0:T(8,128)S(1)}, f32[48,8,128]{2,1,0:T(8,128)S(1)}, u32[]{:S(2)}, u32[]{:S(2)}) collective-permute-start(f32[48,8,128]{2,1,0:T(8,128)S(1)} %get-tuple-element.18), channel_id=1, source_target_pairs={{0,4},{4,0},{8,12},{12,8},{16,20},{20,16},{24,28},{28,24},{32,36},... | collective-permute-start | bytes 589832 | tf_op jit(solution)/shard_map/ppermute | solution.py:449
  38.1 6.2 %collective-permute-start.3 = (f32[48,8,128]{2,1,0:T(8,128)S(1)}, f32[48,8,128]{2,1,0:T(8,128)S(1)}, u32[]{:S(2)}, u32[]{:S(2)}) collective-permute-start(f32[48,8,128]{2,1,0:T(8,128)S(1)} %get-tuple-element.19), channel_id=1, source_target_pairs={{0,60},{4,8},{8,4},{12,16},{16,12},{20,24},{24,20},{28,32},{32,28}... | collective-permute-start | bytes 589832 | tf_op jit(solution)/shard_map/ppermute | solution.py:448
  44.3 2.4 %all-to-all-done.1.spectrum = f32[32,2,8,128]{3,2,1,0:T(8,128)S(1)} async-done(((f32[32,2,8,128]{3,2,1,0:T(8,128)}), f32[32,2,8,128]{3,2,1,0:T(8,128)S(1)}, u32[]{:S(2)}, u32[]{:S(2)}) %all-to-all-start.1) | async-done | bytes 262176 | tf_op jit(solution)/shard_map/all_to_all | solution.py:460
  46.7 3.4 %filter_kernel.1 = f32[16,16,128]{2,1,0:T(8,128)} custom-call(f32[49152,128]{1,0:T(8,128)} %constant.2.clone.table, f32[32,2,8,128]{3,2,1,0:T(8,128)S(1)} %all-to-all-done.1.spectrum), custom_call_target="tpu_custom_call" | custom-call | flops 3000000000 | bytes 9000000 | tf_op jit(solution)/shard_map/filter_kernel/pallas_call | solution.py:465
  50.1 5.2 %all-to-all-start.2 = ((f32[16,16,128]{2,1,0:T(8,128)}), f32[16,16,128]{2,1,0:T(8,128)S(1)}, u32[]{:S(2)}, u32[]{:S(2)}) async-start(f32[16,16,128]{2,1,0:T(8,128)} %filter_kernel.1), calls=%async_computation.2 | async-start | bytes 262144 | tf_op jit(solution)/shard_map/all_to_all | solution.py:469
  55.3 0.0 collective-permute-done.2.y_even
  55.3 0.0 collective-permute-done.3.y_odd
  55.3 1.6 %edge_x_kernel.1 = (f32[48,48,128]{2,1,0:T(8,128)S(1)}, f32[144,128]{1,0:T(8,128)S(1)}, f32[144,128]{1,0:T(8,128)S(1)}) custom-call(f32[49152,128]{1,0:T(8,128)} %constant.2.clone.table, f32[32,32,128]{2,1,0:T(8,128)S(1)} %copy-done.1, f32[8,32,128]{2,1,0:T(8,128)S(1)} %collective-permute-done.z_even, f32[8,32,128]{2,1,0:T(8,128)S(1)} %collective-permute-done.1.z_odd, ...), custom_call_target="tpu_custom_call" | custom-call | flops 10000000000 | bytes 30000000 | tf_op jit(solution)/shard_map/edge_x_kernel/pallas_call | solution.py:470
  56.9 3.3 %collective-permute-start.4 = (f32[144,128]{1,0:T(8,128)S(1)}, f32[144,128]{1,0:T(8,128)S(1)}, u32[]{:S(2)}, u32[]{:S(2)}) collective-permute-start(f32[144,128]{1,0:T(8,128)S(1)} %get-tuple-element.25), channel_id=1, source_target_pairs={{0,64},{64,0},{128,192},{192,128},{256,320},{320,256},{384,448},{4... | collective-permute-start | bytes 221192 | tf_op jit(solution)/shard_map/ppermute | solution.py:449
  60.2 4.4 %collective-permute-start.5 = (f32[144,128]{1,0:T(8,128)S(1)}, f32[144,128]{1,0:T(8,128)S(1)}, u32[]{:S(2)}, u32[]{:S(2)}) collective-permute-start(f32[144,128]{1,0:T(8,128)S(1)} %get-tuple-element.26), channel_id=1, source_target_pairs={{0,448},{64,128},{128,64},{192,256},{256,192},{320,384},{384,320},... | collective-permute-start | bytes 221192 | tf_op jit(solution)/shard_map/ppermute | solution.py:448
  64.6 0.0 all-to-all-done.2.spectrum
  64.6 1.5 %far_kernel.1.far = f32[32,32,128]{2,1,0:T(8,128)S(1)} custom-call(f32[49152,128]{1,0:T(8,128)} %constant.2.clone.table, f32[16,16,128]{2,1,0:T(8,128)S(1)} %all-to-all-done.2.spectrum), custom_call_target="tpu_custom_call" | custom-call | flops 5000000000 | bytes 15000000 | tf_op jit(solution)/shard_map/far_kernel/pallas_call | solution.py:479
  66.1 0.0 collective-permute-done.4.x_even
  66.2 0.4 collective-permute-done.5.x_odd
  66.5 7.0 %near_kernel.1 = f32[32,32,128]{2,1,0:T(8,128)} custom-call(f32[49152,128]{1,0:T(8,128)} %constant.2.clone.table, f32[48,48,128]{2,1,0:T(8,128)S(1)} %get-tuple-element.24.waves, f32[144,128]{1,0:T(8,128)S(1)} %collective-permute-done.4.x_even, f32[144,128]{1,0:T(8,128)S(1)} %collective-permute-done.5.x_odd, f32[32,32,128]{2,1,0:T(8,128)S(1)} %far_kernel.1.far), custom_call_target="tpu_custom_call" | custom-call | flops 100000000 | bytes 300000 | tf_op jit(solution)/shard_map/near_kernel/pallas_call | solution.py:480
Async XLA Ops:
  0.0 1.0 %copy-start = (f32[32,32,128]{2,1,0:T(8,128)S(1)}, f32[32,32,128]{2,1,0:T(8,128)}, u32[]{:S(2)}) copy-start(f32[32,32,128]{2,1,0:T(8,128)} %density.5) | copy-start | bytes 1572868
  1.0 33.8 %copy-start.1 = (f32[32,32,128]{2,1,0:T(8,128)S(1)}, f32[32,32,128]{2,1,0:T(8,128)}, u32[]{:S(2)}) copy-start(f32[32,32,128]{2,1,0:T(8,128)} %density.5) | copy-start | bytes 1572868
  2.2 21.6 %all-to-all-start = ((f32[16,16,128]{2,1,0:T(8,128)}), f32[16,16,128]{2,1,0:T(8,128)S(1)}, u32[]{:S(2)}, u32[]{:S(2)}) async-start(f32[16,16,128]{2,1,0:T(8,128)} %get-tuple-element.20), calls=%async_computation | async-start | bytes 262144 | tf_op jit(solution)/shard_map/all_to_all | solution.py:457
  14.0 20.9 %collective-permute-start = (f32[8,32,128]{2,1,0:T(8,128)S(1)}, f32[8,32,128]{2,1,0:T(8,128)S(1)}, u32[]{:S(2)}, u32[]{:S(2)}) collective-permute-start(f32[8,32,128]{2,1,0:T(8,128)S(1)} %get-tuple-element.16), channel_id=1, source_target_pairs={{0,1},{1,0},{2,3},{3,2},{4,5},{5,4},{6,7},{7,6},{8,9},{9,8},{10,11... | collective-permute-start | bytes 393224 | tf_op jit(solution)/shard_map/ppermute | solution.py:449
  16.0 18.9 %collective-permute-start.1 = (f32[8,32,128]{2,1,0:T(8,128)S(1)}, f32[8,32,128]{2,1,0:T(8,128)S(1)}, u32[]{:S(2)}, u32[]{:S(2)}) collective-permute-start(f32[8,32,128]{2,1,0:T(8,128)S(1)} %get-tuple-element.17), channel_id=1, source_target_pairs={{0,3},{1,2},{2,1},{3,0},{4,7},{5,6},{6,5},{7,4},{8,11},{9,10},{10,... | collective-permute-start | bytes 393224 | tf_op jit(solution)/shard_map/ppermute | solution.py:448
  25.8 20.9 %all-to-all-start.1 = ((f32[32,2,8,128]{3,2,1,0:T(8,128)}), f32[32,2,8,128]{3,2,1,0:T(8,128)S(1)}, u32[]{:S(2)}, u32[]{:S(2)}) async-start(f32[32,2,8,128]{3,2,1,0:T(8,128)} %first_kernel.1), calls=%async_computation.1 | async-start | bytes 524288 | tf_op jit(solution)/shard_map/all_to_all | solution.py:460
  35.0 20.3 %collective-permute-start.2 = (f32[48,8,128]{2,1,0:T(8,128)S(1)}, f32[48,8,128]{2,1,0:T(8,128)S(1)}, u32[]{:S(2)}, u32[]{:S(2)}) collective-permute-start(f32[48,8,128]{2,1,0:T(8,128)S(1)} %get-tuple-element.18), channel_id=1, source_target_pairs={{0,4},{4,0},{8,12},{12,8},{16,20},{20,16},{24,28},{28,24},{32,36},... | collective-permute-start | bytes 589832 | tf_op jit(solution)/shard_map/ppermute | solution.py:449
  38.1 17.2 %collective-permute-start.3 = (f32[48,8,128]{2,1,0:T(8,128)S(1)}, f32[48,8,128]{2,1,0:T(8,128)S(1)}, u32[]{:S(2)}, u32[]{:S(2)}) collective-permute-start(f32[48,8,128]{2,1,0:T(8,128)S(1)} %get-tuple-element.19), channel_id=1, source_target_pairs={{0,60},{4,8},{8,4},{12,16},{16,12},{20,24},{24,20},{28,32},{32,28}... | collective-permute-start | bytes 589832 | tf_op jit(solution)/shard_map/ppermute | solution.py:448
  50.1 14.5 %all-to-all-start.2 = ((f32[16,16,128]{2,1,0:T(8,128)}), f32[16,16,128]{2,1,0:T(8,128)S(1)}, u32[]{:S(2)}, u32[]{:S(2)}) async-start(f32[16,16,128]{2,1,0:T(8,128)} %filter_kernel.1), calls=%async_computation.2 | async-start | bytes 262144 | tf_op jit(solution)/shard_map/all_to_all | solution.py:469
  56.9 9.2 %collective-permute-start.4 = (f32[144,128]{1,0:T(8,128)S(1)}, f32[144,128]{1,0:T(8,128)S(1)}, u32[]{:S(2)}, u32[]{:S(2)}) collective-permute-start(f32[144,128]{1,0:T(8,128)S(1)} %get-tuple-element.25), channel_id=1, source_target_pairs={{0,64},{64,0},{128,192},{192,128},{256,320},{320,256},{384,448},{4... | collective-permute-start | bytes 221192 | tf_op jit(solution)/shard_map/ppermute | solution.py:449
  60.2 6.3 %collective-permute-start.5 = (f32[144,128]{1,0:T(8,128)S(1)}, f32[144,128]{1,0:T(8,128)S(1)}, u32[]{:S(2)}, u32[]{:S(2)}) collective-permute-start(f32[144,128]{1,0:T(8,128)S(1)} %get-tuple-element.26), channel_id=1, source_target_pairs={{0,448},{64,128},{128,64},{192,256},{256,192},{320,384},{384,320},... | collective-permute-start | bytes 221192 | tf_op jit(solution)/shard_map/ppermute | solution.py:448

commit v6 on v5

--- a/solution.py
+++ b/solution.py
@@ -21,7 +21,6 @@
 BZ, BY, BX = MZ // GZ, MY // GY, MX // GX
 PZ, PY, PX = CZ + 2 * HALO, CY + 2 * HALO, CX + 2 * HALO
 LANES = 256
-GROUP = 3 * PY
 BORDER = BY + 2
 SHARE = 2 * GX
 KX = MX // SHARE
@@ -197,6 +196,11 @@
 def halves(x):
     high = x.astype(bf16)
     return high, (x - high.astype(f32)).astype(bf16)
+
+
+def close_dot(a, b):
+    (a, a_low), (b, b_low) = halves(a), halves(b)
+    return dot(a, b) + (dot(a, b_low) + dot(a_low, b))
 
 
 def lane(shape):
@@ -279,9 +283,9 @@
     rows = jnp.concatenate([rows[:, half].reshape(MZ * 8, MY) for half in range(2)], axis=1)
     rows = exact_dot(wait("into_z"), rows)
     rows = rows * wait("gain")
-    rows = exact_dot(wait("out_z"), rows)
+    rows = close_dot(wait("out_z"), rows)
     rows = jnp.concatenate([rows[:, :MY], rows[:, MY:]], axis=0)
-    rows = exact_dot(rows, wait("out_y"))
+    rows = close_dot(rows, wait("out_y"))
     for core in range(2):
         sides = []
         for half in range(2):
@@ -300,8 +304,10 @@
     held = {"last_x": held_x, "last_y": held_y}
     wait = TABLES.copies(table, held, sems, {"last_x": lax.axis_index("gx")})
     rows = spectrum[...].reshape(MX, 128)
-    field = transposed_dot(rows, wait("last_x"))
-    field = exact_dot(wait("last_y"), field)
+    field = close_dot(rows.T, wait("last_x"))
+    high, low = halves(field)
+    refine = wait("last_y").astype(bf16)
+    field = dot(refine, high) + dot(refine, low)
 
     def plane(z):
         return field[z * CY : (z + 1) * CY]
@@ -340,22 +346,17 @@
     padded[:, HALO + CY : PY] = jnp.where(lower, one, two)
 
     into_y = wait("into_y")[:, : 3 * PY].astype(bf16)
-    place = lane((GROUP, 128)) // HALO
-    left = right = jnp.zeros((GROUP, 128), f32)
-    for j in range(8):
-        rows = []
-        for pair in range(3):
-            z = 6 * j + 2 * pair
-            high, low = halves(jnp.concatenate([padded[z], padded[z + 1]], axis=1))
-            wave = dot(into_y, jnp.concatenate([high, high, low], axis=0))
-            waves[z], waves[z + 1] = wave[:, :128], wave[:, 128:]
-            rows += [wave[:, :128], wave[:, 128:]]
-        for i in range(2):
-            group = jnp.concatenate(rows[3 * i : 3 * i + 3], axis=0)
-            shift = (2 * j + i) * HALO
-            left = jnp.where(place == 2 * j + i, pltpu.roll(group, shift, 1) if shift else group, left)
-            shift = (shift - (CX - HALO)) % 128
-            right = jnp.where(place == 2 * j + i, pltpu.roll(group, shift, 1) if shift else group, right)
+    for z in range(0, PZ, 2):
+        high, low = halves(jnp.concatenate([padded[z], padded[z + 1]], axis=1))
+        wave = dot(into_y, jnp.concatenate([high, high, low], axis=0))
+        waves[z], waves[z + 1] = wave[:, :128], wave[:, 128:]
+    flat = waves.reshape(PZ * PY, 128)
+    left, right = [], []
+    for j in range(PZ * PY // 128):
+        turned = flat[j * 128 : (j + 1) * 128].T
+        left.append(turned[:HALO])
+        right.append(turned[128 - HALO :])
+    left, right = jnp.concatenate(left, axis=1), jnp.concatenate(right, axis=1)
     lower = is_even("gx")
     even[...] = jnp.where(lower, right, left)
     odd[...] = jnp.where(lower, left, right)
@@ -366,27 +367,18 @@
 ):
     held = {"into_x": held_ix, "gains": held_g, "into_y": held_y, "out_x": held_ox}
     wait = TABLES.copies(table, held, sems, {})
-    lanes = lane((GROUP, 128))
     lower = is_even("gx")
     one, two = x_even[...], x_odd[...]
-    left, right = jnp.where(lower, two, one), jnp.where(lower, one, two)
-    into_x = wait("into_x").astype(bf16)
-    for j in range(16):
-        rows = waves[3 * j : 3 * j + 3].reshape(GROUP, 128)
-        to_left, to_right = (-HALO * j) % 128, (HALO - HALO * j) % 128
-        ends = jnp.where(
-            lanes < HALO,
-            pltpu.roll(left, to_left, 1) if to_left else left,
-            pltpu.roll(right, to_right, 1) if to_right else right,
-        )
-        ends = jnp.where(lanes < 2 * HALO, ends, 0.0)
-        high = ends.astype(bf16).astype(f32)
-        low = ends - high
-        ends = (high + pltpu.roll(high, 2 * HALO, 1) + pltpu.roll(low, 4 * HALO, 1)).astype(bf16)
-        high, low = halves(rows)
-        wave = dot(jnp.concatenate([high, high, low, ends], axis=1), into_x)
-        for i in range(3):
-            wave_x[3 * j + i] = wave[i * PY : (i + 1) * PY]
+    ends = jnp.concatenate([jnp.where(lower, two, one), jnp.where(lower, one, two)], axis=0)
+    high = ends.astype(bf16).astype(f32)
+    ends = jnp.concatenate([high, high, ends - high], axis=0)
+    into_x = wait("into_x")[:432].astype(bf16)
+    flat = waves.reshape(PZ * PY, 128)
+    flat_x = wave_x.reshape(PZ * PY, LANES)
+    for j in range(18):
+        part = slice(j * 128, (j + 1) * 128)
+        high, low = halves(flat[part])
+        flat_x[part] = dot(jnp.concatenate([high, high, low, ends[:, part].T.astype(bf16)], axis=1), into_x)
 
     wait("gains")
 
@@ -408,16 +400,15 @@
 
     out_y = wait("into_y")[HALO : HALO + CY, : 3 * PY].astype(bf16)
     out_x = wait("out_x").astype(bf16)
-
-    for step in range(CZ // 4):
-        rows = []
-        for i in range(4):
-            high, low = halves(wave_z[step * 4 + i])
-            rows.append(dot(out_y, jnp.concatenate([high, high, low], axis=0)))
-        high, low = halves(jnp.concatenate(rows, axis=0))
-        field = dot(jnp.concatenate([high, high, low], axis=1), out_x)
-        for i in range(4):
-            out[step * 4 + i] = far[step * 4 + i] + field[i * CY : (i + 1) * CY]
+    high, low = halves(wave_z[...].reshape(CZ * PY, LANES))
+    both = dot(high, jnp.concatenate([out_x[:256], out_x[256:512]], axis=1))
+    rows = both[:, :128] + both[:, 128:] + dot(low, out_x[:256])
+    for z in range(0, CZ, 2):
+        pair = jnp.concatenate([rows[z * PY : (z + 1) * PY], rows[(z + 1) * PY : (z + 2) * PY]], axis=1)
+        high, low = halves(pair)
+        field = dot(out_y, jnp.concatenate([high, high, low], axis=0))
+        out[z] = far[z] + field[:, :128]
+        out[z + 1] = far[z + 1] + field[:, 128:]
 
 
 def call(kernel, outs, arrays=0, tables=(), scratch=(), us=1.0):
@@ -469,7 +460,7 @@
     spectrum = lax.all_to_all(spectrum, ("gx", "core"), 0, 0, tiled=True)
     waves, even, odd = call(
         edge_x_kernel,
-        [(PZ, PY, CX), (GROUP, 128), (GROUP, 128)],
+        [(PZ, PY, CX), (HALO, PZ * PY), (HALO, PZ * PY)],
         5,
         ["into_y"],
         [pltpu.VMEM((PZ, PY, CX), f32)],

time: 74.2 us -> 71.4 us (0.962)
  Pallas kernels: 16.7 us -> 13.7 us
    pallas_call x1, Pallas kernels: 6.97 us -> 4.76 us  [body(): call(near_kernel, (CZ, CY, CX), 4, ['gains', 'into_x', 'into_y', 'out_x']...]
  transfers between devices with their start and end apart: 9 -> 9, of which waited for: 2 -> 4; matrix products, arithmetic and copies ran while one was open for 0% -> 0% of each run, Pallas kernels for 12% -> 11%
where the time goes in v6:
time: 71.4 us; the launch traced here: 70.7 us
  starting transfers between devices  52.7 us (74%)
  Pallas kernels  13.7 us (19%)
  waiting for transfers between devices  3.07 us (4%)
  local copies, waits for them, and re-layouts  1.04 us (1%)
    ppermute x3, starting transfers between devices, exchange(): odd = lax.ppermute(odd, axis, high_first)  18.3 us
    all_to_all x1, starting transfers between devices, body(): charges = lax.all_to_all(charges, ('gx', 'core'), 0, 0, tiled=True)  11.8 us
    all_to_all x1, starting transfers between devices, body(): spectrum = lax.all_to_all(spectrum, ('gy', 'yh'), 0, 0, tiled=True)  9.08 us
    ppermute x3, starting transfers between devices, exchange(): return (lax.ppermute(even, axis, low_first), odd)  8.34 us
    all_to_all x1, starting transfers between devices, body(): spectrum = lax.all_to_all(spectrum, ('gx', 'core'), 0, 0, tiled=True)  5.22 us
    pallas_call x1, Pallas kernels, body(): call(near_kernel, (CZ, CY, CX), 4, ['gains', 'into_x', 'into_y', 'out_x']...  4.76 us
    pallas_call x1, Pallas kernels, body(): call(filter_kernel, (SHARE, KX, 128), 1, ['full_y', 'into_z', 'gain', 'ou...  3.1 us
    all_to_all x1, waiting for transfers between devices, body(): spectrum = lax.all_to_all(spectrum, ('gy', 'yh'), 0, 0, tiled=True)  2.39 us
  transfers between devices with their start and end apart: 9, of which 4 were waited for; matrix products, arithmetic and copies ran while one was open for 0% of the time, Pallas kernels for 11%

profile of v6, /device:TPU:1, one launch (start us, length us, event | category | flops | bytes accessed | tf_op | source)
XLA Modules:
  0.0 70.7 jit_solution(7166583739431223888)
XLA Ops:
  0.0 0.0 copy-start
  0.0 1.0 %copy-done = f32[32,32,128]{2,1,0:T(8,128)S(1)} copy-done((f32[32,32,128]{2,1,0:T(8,128)S(1)}, f32[32,32,128]{2,1,0:T(8,128)}, u32[]{:S(2)}) %copy-start) | copy-done | bytes 524312
  1.0 0.0 copy-start.1
  1.0 1.1 %charge_kernel.1 = (f32[16,16,128]{2,1,0:T(8,128)}, f32[8,32,128]{2,1,0:T(8,128)S(1)}, f32[8,32,128]{2,1,0:T(8,128)S(1)}) custom-call(f32[32,32,128]{2,1,0:T(8,128)S(1)} %copy-done), custom_call_target="tpu_custom_call" | custom-call | flops 1000000000 | bytes 3000000 | tf_op jit(solution)/shard_map/charge_kernel/pallas_call | solution.py:445
  2.2 11.8 %all-to-all-start = ((f32[16,16,128]{2,1,0:T(8,128)}), f32[16,16,128]{2,1,0:T(8,128)S(1)}, u32[]{:S(2)}, u32[]{:S(2)}) async-start(f32[16,16,128]{2,1,0:T(8,128)} %get-tuple-element.20), calls=%async_computation | async-start | bytes 262144 | tf_op jit(solution)/shard_map/all_to_all | solution.py:448
  14.0 2.0 %collective-permute-start = (f32[8,32,128]{2,1,0:T(8,128)S(1)}, f32[8,32,128]{2,1,0:T(8,128)S(1)}, u32[]{:S(2)}, u32[]{:S(2)}) collective-permute-start(f32[8,32,128]{2,1,0:T(8,128)S(1)} %get-tuple-element.16), channel_id=1, source_target_pairs={{0,1},{1,0},{2,3},{3,2},{4,5},{5,4},{6,7},{7,6},{8,9},{9,8},{10,11... | collective-permute-start | bytes 393224 | tf_op jit(solution)/shard_map/ppermute | solution.py:440
  16.0 7.7 %collective-permute-start.1 = (f32[8,32,128]{2,1,0:T(8,128)S(1)}, f32[8,32,128]{2,1,0:T(8,128)S(1)}, u32[]{:S(2)}, u32[]{:S(2)}) collective-permute-start(f32[8,32,128]{2,1,0:T(8,128)S(1)} %get-tuple-element.17), channel_id=1, source_target_pairs={{0,3},{1,2},{2,1},{3,0},{4,7},{5,6},{6,5},{7,4},{8,11},{9,10},{10,... | collective-permute-start | bytes 393224 | tf_op jit(solution)/shard_map/ppermute | solution.py:439
  23.8 0.0 all-to-all-done.charges
  23.8 2.0 %first_kernel.1 = f32[32,2,8,128]{3,2,1,0:T(8,128)} custom-call(f32[49152,128]{1,0:T(8,128)} %constant.2.clone.table, f32[16,16,128]{2,1,0:T(8,128)S(1)} %all-to-all-done.charges), custom_call_target="tpu_custom_call" | custom-call | flops 1300000000 | bytes 3900000 | tf_op jit(solution)/shard_map/first_kernel/pallas_call | solution.py:450
  25.8 9.1 %all-to-all-start.1 = ((f32[32,2,8,128]{3,2,1,0:T(8,128)}), f32[32,2,8,128]{3,2,1,0:T(8,128)S(1)}, u32[]{:S(2)}, u32[]{:S(2)}) async-start(f32[32,2,8,128]{3,2,1,0:T(8,128)} %first_kernel.1), calls=%async_computation.1 | async-start | bytes 524288 | tf_op jit(solution)/shard_map/all_to_all | solution.py:451
  34.9 0.0 collective-permute-done.z_even
  34.9 0.0 collective-permute-done.1.z_odd
  34.9 0.0 copy-done.1
  34.9 0.1 edge_y_kernel.1
  35.0 3.1 %collective-permute-start.2 = (f32[48,8,128]{2,1,0:T(8,128)S(1)}, f32[48,8,128]{2,1,0:T(8,128)S(1)}, u32[]{:S(2)}, u32[]{:S(2)}) collective-permute-start(f32[48,8,128]{2,1,0:T(8,128)S(1)} %get-tuple-element.18), channel_id=1, source_target_pairs={{0,4},{4,0},{8,12},{12,8},{16,20},{20,16},{24,28},{28,24},{32,36},... | collective-permute-start | bytes 589832 | tf_op jit(solution)/shard_map/ppermute | solution.py:440
  38.1 6.2 %collective-permute-start.3 = (f32[48,8,128]{2,1,0:T(8,128)S(1)}, f32[48,8,128]{2,1,0:T(8,128)S(1)}, u32[]{:S(2)}, u32[]{:S(2)}) collective-permute-start(f32[48,8,128]{2,1,0:T(8,128)S(1)} %get-tuple-element.19), channel_id=1, source_target_pairs={{0,60},{4,8},{8,4},{12,16},{16,12},{20,24},{24,20},{28,32},{32,28}... | collective-permute-start | bytes 589832 | tf_op jit(solution)/shard_map/ppermute | solution.py:439
  44.3 2.4 %all-to-all-done.1.spectrum = f32[32,2,8,128]{3,2,1,0:T(8,128)S(1)} async-done(((f32[32,2,8,128]{3,2,1,0:T(8,128)}), f32[32,2,8,128]{3,2,1,0:T(8,128)S(1)}, u32[]{:S(2)}, u32[]{:S(2)}) %all-to-all-start.1) | async-done | bytes 262176 | tf_op jit(solution)/shard_map/all_to_all | solution.py:451
  46.7 3.1 %filter_kernel.1 = f32[16,16,128]{2,1,0:T(8,128)} custom-call(f32[49152,128]{1,0:T(8,128)} %constant.2.clone.table, f32[32,2,8,128]{3,2,1,0:T(8,128)S(1)} %all-to-all-done.1.spectrum), custom_call_target="tpu_custom_call" | custom-call | flops 3000000000 | bytes 9000000 | tf_op jit(solution)/shard_map/filter_kernel/pallas_call | solution.py:456
  49.8 5.2 %all-to-all-start.2 = ((f32[16,16,128]{2,1,0:T(8,128)}), f32[16,16,128]{2,1,0:T(8,128)S(1)}, u32[]{:S(2)}, u32[]{:S(2)}) async-start(f32[16,16,128]{2,1,0:T(8,128)} %filter_kernel.1), calls=%async_computation.2 | async-start | bytes 262144 | tf_op jit(solution)/shard_map/all_to_all | solution.py:460
  55.0 0.0 collective-permute-done.2.y_even
  55.0 0.1 collective-permute-done.3.y_odd
  55.1 1.3 %edge_x_kernel.1 = (f32[48,48,128]{2,1,0:T(8,128)S(1)}, f32[8,2304]{1,0:T(8,128)S(1)}, f32[8,2304]{1,0:T(8,128)S(1)}) custom-call(f32[49152,128]{1,0:T(8,128)} %constant.2.clone.table, f32[32,32,128]{2,1,0:T(8,128)S(1)} %copy-done.1, f32[8,32,128]{2,1,0:T(8,128)S(1)} %collective-permute-done.z_even, f32[8,32,128]{2,1,0:T(8,128)S(1)} %collective-permute-done.1.z_odd, ...), custom_call_target="tpu_custom_call" | custom-call | flops 10000000000 | bytes 30000000 | tf_op jit(solution)/shard_map/edge_x_kernel/pallas_call | solution.py:461
  56.4 3.2 %collective-permute-start.4 = (f32[8,2304]{1,0:T(8,128)S(1)}, f32[8,2304]{1,0:T(8,128)S(1)}, u32[]{:S(2)}, u32[]{:S(2)}) collective-permute-start(f32[8,2304]{1,0:T(8,128)S(1)} %get-tuple-element.25), channel_id=1, source_target_pairs={{0,64},{64,0},{128,192},{192,128},{256,320},{320,256},{384,448},{4... | collective-permute-start | bytes 221192 | tf_op jit(solution)/shard_map/ppermute | solution.py:440
  59.6 4.4 %collective-permute-start.5 = (f32[8,2304]{1,0:T(8,128)S(1)}, f32[8,2304]{1,0:T(8,128)S(1)}, u32[]{:S(2)}, u32[]{:S(2)}) collective-permute-start(f32[8,2304]{1,0:T(8,128)S(1)} %get-tuple-element.26), channel_id=1, source_target_pairs={{0,448},{64,128},{128,64},{192,256},{256,192},{320,384},{384,320},... | collective-permute-start | bytes 221192 | tf_op jit(solution)/shard_map/ppermute | solution.py:439
  64.0 0.2 all-to-all-done.2.spectrum
  64.2 1.4 %far_kernel.1.far = f32[32,32,128]{2,1,0:T(8,128)S(1)} custom-call(f32[49152,128]{1,0:T(8,128)} %constant.2.clone.table, f32[16,16,128]{2,1,0:T(8,128)S(1)} %all-to-all-done.2.spectrum), custom_call_target="tpu_custom_call" | custom-call | flops 5000000000 | bytes 15000000 | tf_op jit(solution)/shard_map/far_kernel/pallas_call | solution.py:470
  65.6 0.0 collective-permute-done.4.x_even
  65.6 0.3 collective-permute-done.5.x_odd
  65.9 4.8 %near_kernel.1 = f32[32,32,128]{2,1,0:T(8,128)} custom-call(f32[49152,128]{1,0:T(8,128)} %constant.2.clone.table, f32[48,48,128]{2,1,0:T(8,128)S(1)} %get-tuple-element.24.waves, f32[8,2304]{1,0:T(8,128)S(1)} %collective-permute-done.4.x_even, f32[8,2304]{1,0:T(8,128)S(1)} %collective-permute-done.5.x_odd, f32[32,32,128]{2,1,0:T(8,128)S(1)} %far_kernel.1.far), custom_call_target="tpu_custom_call" | custom-call | flops 100000000 | bytes 300000 | tf_op jit(solution)/shard_map/near_kernel/pallas_call | solution.py:471
Async XLA Ops:
  0.0 1.0 %copy-start = (f32[32,32,128]{2,1,0:T(8,128)S(1)}, f32[32,32,128]{2,1,0:T(8,128)}, u32[]{:S(2)}) copy-start(f32[32,32,128]{2,1,0:T(8,128)} %density.5) | copy-start | bytes 1572868
  1.0 33.8 %copy-start.1 = (f32[32,32,128]{2,1,0:T(8,128)S(1)}, f32[32,32,128]{2,1,0:T(8,128)}, u32[]{:S(2)}) copy-start(f32[32,32,128]{2,1,0:T(8,128)} %density.5) | copy-start | bytes 1572868
  2.2 21.6 %all-to-all-start = ((f32[16,16,128]{2,1,0:T(8,128)}), f32[16,16,128]{2,1,0:T(8,128)S(1)}, u32[]{:S(2)}, u32[]{:S(2)}) async-start(f32[16,16,128]{2,1,0:T(8,128)} %get-tuple-element.20), calls=%async_computation | async-start | bytes 262144 | tf_op jit(solution)/shard_map/all_to_all | solution.py:448
  14.0 20.9 %collective-permute-start = (f32[8,32,128]{2,1,0:T(8,128)S(1)}, f32[8,32,128]{2,1,0:T(8,128)S(1)}, u32[]{:S(2)}, u32[]{:S(2)}) collective-permute-start(f32[8,32,128]{2,1,0:T(8,128)S(1)} %get-tuple-element.16), channel_id=1, source_target_pairs={{0,1},{1,0},{2,3},{3,2},{4,5},{5,4},{6,7},{7,6},{8,9},{9,8},{10,11... | collective-permute-start | bytes 393224 | tf_op jit(solution)/shard_map/ppermute | solution.py:440
  16.0 18.9 %collective-permute-start.1 = (f32[8,32,128]{2,1,0:T(8,128)S(1)}, f32[8,32,128]{2,1,0:T(8,128)S(1)}, u32[]{:S(2)}, u32[]{:S(2)}) collective-permute-start(f32[8,32,128]{2,1,0:T(8,128)S(1)} %get-tuple-element.17), channel_id=1, source_target_pairs={{0,3},{1,2},{2,1},{3,0},{4,7},{5,6},{6,5},{7,4},{8,11},{9,10},{10,... | collective-permute-start | bytes 393224 | tf_op jit(solution)/shard_map/ppermute | solution.py:439
  25.8 20.9 %all-to-all-start.1 = ((f32[32,2,8,128]{3,2,1,0:T(8,128)}), f32[32,2,8,128]{3,2,1,0:T(8,128)S(1)}, u32[]{:S(2)}, u32[]{:S(2)}) async-start(f32[32,2,8,128]{3,2,1,0:T(8,128)} %first_kernel.1), calls=%async_computation.1 | async-start | bytes 524288 | tf_op jit(solution)/shard_map/all_to_all | solution.py:451
  35.0 20.0 %collective-permute-start.2 = (f32[48,8,128]{2,1,0:T(8,128)S(1)}, f32[48,8,128]{2,1,0:T(8,128)S(1)}, u32[]{:S(2)}, u32[]{:S(2)}) collective-permute-start(f32[48,8,128]{2,1,0:T(8,128)S(1)} %get-tuple-element.18), channel_id=1, source_target_pairs={{0,4},{4,0},{8,12},{12,8},{16,20},{20,16},{24,28},{28,24},{32,36},... | collective-permute-start | bytes 589832 | tf_op jit(solution)/shard_map/ppermute | solution.py:440
  38.1 17.0 %collective-permute-start.3 = (f32[48,8,128]{2,1,0:T(8,128)S(1)}, f32[48,8,128]{2,1,0:T(8,128)S(1)}, u32[]{:S(2)}, u32[]{:S(2)}) collective-permute-start(f32[48,8,128]{2,1,0:T(8,128)S(1)} %get-tuple-element.19), channel_id=1, source_target_pairs={{0,60},{4,8},{8,4},{12,16},{16,12},{20,24},{24,20},{28,32},{32,28}... | collective-permute-start | bytes 589832 | tf_op jit(solution)/shard_map/ppermute | solution.py:439
  49.8 14.4 %all-to-all-start.2 = ((f32[16,16,128]{2,1,0:T(8,128)}), f32[16,16,128]{2,1,0:T(8,128)S(1)}, u32[]{:S(2)}, u32[]{:S(2)}) async-start(f32[16,16,128]{2,1,0:T(8,128)} %filter_kernel.1), calls=%async_computation.2 | async-start | bytes 262144 | tf_op jit(solution)/shard_map/all_to_all | solution.py:460
  56.4 9.2 %collective-permute-start.4 = (f32[8,2304]{1,0:T(8,128)S(1)}, f32[8,2304]{1,0:T(8,128)S(1)}, u32[]{:S(2)}, u32[]{:S(2)}) collective-permute-start(f32[8,2304]{1,0:T(8,128)S(1)} %get-tuple-element.25), channel_id=1, source_target_pairs={{0,64},{64,0},{128,192},{192,128},{256,320},{320,256},{384,448},{4... | collective-permute-start | bytes 221192 | tf_op jit(solution)/shard_map/ppermute | solution.py:440
  59.6 6.3 %collective-permute-start.5 = (f32[8,2304]{1,0:T(8,128)S(1)}, f32[8,2304]{1,0:T(8,128)S(1)}, u32[]{:S(2)}, u32[]{:S(2)}) collective-permute-start(f32[8,2304]{1,0:T(8,128)S(1)} %get-tuple-element.26), channel_id=1, source_target_pairs={{0,448},{64,128},{128,64},{192,256},{256,192},{320,384},{384,320},... | collective-permute-start | bytes 221192 | tf_op jit(solution)/shard_map/ppermute | solution.py:439

commit v7 on v6

--- a/solution.py
+++ b/solution.py
@@ -21,9 +21,11 @@
 BZ, BY, BX = MZ // GZ, MY // GY, MX // GX
 PZ, PY, PX = CZ + 2 * HALO, CY + 2 * HALO, CX + 2 * HALO
 LANES = 256
+OWN_US = 1.0
 BORDER = BY + 2
 SHARE = 2 * GX
 KX = MX // SHARE
+TAIL = PX - CX
 VMEM_MIB = 44
 TABLE_ROWS = 24 * 2048
 
@@ -54,13 +56,15 @@
     cos_y = np.cos(2.0 * np.pi / PY * np.outer(np.arange(PY), both))
     cos_x = np.cos(2.0 * np.pi / PX * np.outer(np.arange(PX), both))
     spectral = np.einsum("dab,ka,lb->dkl", kernel, cos_y, cos_x) / (PY * PX)
-    gains = np.zeros(((HALO + 1) * PY, LANES))
-    gains[:, :PX] = spectral.reshape(-1, PX)
+    gains = spectral[:, :, :CX].reshape(-1, CX)
+    tail_gains = np.zeros((HALO + 1, 8, 128))
+    tails = spectral[:, :, CX:].reshape(HALO + 1, PY // 8, 8, TAIL).swapaxes(1, 2)
+    tail_gains[:, :, : PY // 8 * TAIL] = tails.reshape(HALO + 1, 8, PY // 8 * TAIL)
+    tail_gains = tail_gains.reshape(-1, 128)
 
     every_x, every_y = np.arange(PX), np.arange(PY)
-    forward_x = np.zeros((PX, LANES))
-    forward_x[:, :PX] = cas(every_x, every_x, PX)
-    high, low = split(forward_x)
+    spread = np.r_[0:CX, np.tile(np.arange(CX, PX), 8)]
+    high, low = split(cas(every_x, spread, PX))
     own = slice(HALO, HALO + CX)
     ends = np.r_[0:HALO, HALO + CX : PX]
     into_x = np.zeros((512, LANES))
@@ -68,14 +72,20 @@
     into_x[384:400], into_x[400:416], into_x[416:432] = high[ends], low[ends], high[ends]
 
     high, low = split(cas(every_y, every_y, PY))
+    inner = slice(HALO, HALO + CY)
     into_y = np.zeros((PY, LANES))
     into_y[:, : 3 * PY] = np.concatenate([high, low, high], axis=1)
 
-    back_x = np.zeros((LANES, CX))
-    back_x[:PX] = cas(every_x, every_x[own], PX)
-    high, low = split(back_x)
-    out_x = np.concatenate([high, low, high], axis=0)
-    return {"gains": gains, "into_x": into_x, "into_y": into_y, "out_x": out_x}
+    high, low = split(cas(spread, every_x[own], PX))
+    back_x = np.concatenate([high, low], axis=1)
+    return {
+        "gains": gains,
+        "tail_gains": tail_gains,
+        "into_x": into_x,
+        "into_y": into_y,
+        "back_y": into_y[inner],
+        "back_x": back_x,
+    }
 
 
 def far_tables():
@@ -150,38 +160,48 @@
 
     def shape(self, name):
         _, count, halves = self.place[name]
-        return pltpu.VMEM((halves, count, 128), f32)
-
-    def copies(self, ref, held, sems, index):
-        made = []
-        for i, (name, target) in enumerate(held.items()):
-            first, count, halves = self.place[name]
-            rows = halves * count
-            start = first + index.get(name, 0) * rows
-            if name in index:
-                start = pl.multiple_of(start, 8)
-            for half in range(halves):
-                source = ref.at[pl.ds(start + half * count, count)]
-                made.append(pltpu.make_async_copy(source, target.at[half], sems.at[i]))
-        for copy in made:
+        return halves * count, 128
+
+    def copy(self, ref, name, held, sem, part=None):
+        first, count, halves = self.place[name]
+        rows = halves * count
+        start = first if part is None else pl.multiple_of(first + part * rows, 8)
+        return pltpu.make_async_copy(ref.at[pl.ds(start, rows)], held, sem)
+
+    def height(self, names):
+        return sum(self.shape(name)[0] for name in names)
+
+    def rows(self, held, names, name):
+        return held.at[pl.ds(self.height(names[: names.index(name)]), self.shape(name)[0])]
+
+    def reader(self, held, names):
+        def get(name):
+            _, count, halves = self.place[name]
+            rows = self.rows(held, names, name)
+            if halves == 1:
+                return rows[...]
+            return jnp.concatenate([rows[0:count], rows[count : 2 * count]], axis=1)
+
+        return get
+
+    def fetch(self, ref, held, names, sems, part={}):
+        copies = {
+            name: self.copy(ref, name, self.rows(held, names, name), sems.at[i], part.get(name))
+            for i, name in enumerate(names)
+        }
+        for copy in copies.values():
             copy.start()
-        pairs, at = {}, 0
-        for name in held:
-            halves = self.place[name][2]
-            pairs[name] = made[at : at + halves]
-            at += halves
+        get = self.reader(held, names)
 
         def wait(name):
-            for copy in pairs[name]:
-                copy.wait()
-            target = held[name]
-            if len(pairs[name]) == 1:
-                return target[0]
-            return jnp.concatenate([target[0], target[1]], axis=1)
+            copies[name].wait()
+            return get(name)
 
         return wait
 
 
+FILTER = ["full_y", "into_z", "gain", "out_z", "out_y"]
+NEAR = ["gains", "tail_gains", "into_x", "back_y", "back_x"]
 TABLES = Tables()
 
 
@@ -219,7 +239,23 @@
     return lax.rem(lax.axis_index(axis), 2) == 0
 
 
-def charge_kernel(density, out, even, odd):
+def send(held, out, sems):
+    count = held.shape[0]
+    copies = [
+        pltpu.make_async_copy(held, out.at[pl.ds(i * count, count)], sems.at[i])
+        for i in range(out.shape[0] // count)
+    ]
+    for copy in copies:
+        copy.start()
+
+    def wait():
+        for copy in copies:
+            copy.wait()
+
+    return wait
+
+
+def charge_kernel(density, out, even, odd, message, sems):
     parts = []
     for high in range(2):
         planes = []
@@ -236,15 +272,18 @@
 
     rows = exact_dot(rows, pool((4 * CX, 128), 0, 1))
     rows = exact_dot(pool((2 * BY, 2 * CY), 1, 0), rows)
-    for peer in range(SHARE):
-        out[peer] = rows
+    for copy in range(4):
+        message[copy] = rows
+    wait = send(message, out, sems)
     start = jnp.where(is_even("core"), CZ - HALO, 0)
     even[...] = density[pl.ds(start, HALO)]
     odd[...] = density[pl.ds(CZ - HALO - start, HALO)]
-
-
-def first_kernel(table, charges, out, held, sems):
-    wait = TABLES.copies(table, {"first_x": held}, sems, {"first_x": share()})
+    wait()
+
+
+def first_kernel(table, charges, out, held, message, sem, sems):
+    copy = TABLES.copy(table, "first_x", held, sem, share())
+    copy.start()
     peers = charges[...].reshape(GX, 32, 128)
     place = lane((32, 128)) // BX
     blocks = []
@@ -260,7 +299,8 @@
             sides.append(total)
         blocks.append(jnp.concatenate(sides, axis=1))
     rows = jnp.concatenate(blocks, axis=0)
-    rows = exact_dot(rows, wait("first_x"))
+    copy.wait()
+    rows = exact_dot(rows, held[...])
     place = lane((BY, 128)) // KX
     for core in range(2):
         total = None
@@ -268,24 +308,23 @@
             start = (z % 4) * 32 + core * 16 + (z // 4) * 8
             piece = rows[start : start + 8]
             total = piece if z == 0 else jnp.where(place == z, piece, total)
-        for peer in range(2 * GY):
-            out[peer, core] = total
-
-
-def filter_kernel(table, spectrum, out, held_y, held_z, held_g, held_iz, held_iy, sems):
-    held = {"full_y": held_y, "into_z": held_z, "gain": held_g, "out_z": held_iz, "out_y": held_iy}
-    index = {"gain": share(), "out_z": lax.axis_index("yh"), "out_y": lax.axis_index("gy")}
-    wait = TABLES.copies(table, held, sems, index)
+        for copy in range(8):
+            message[copy, core] = total
+    send(message, out, sems)()
+
+
+def filter_kernel(held, spectrum, out, message, sems):
     blocks = spectrum[...].reshape(GY, 4, BY, 128)
-    full_y = wait("full_y")
+    get = TABLES.reader(held, FILTER)
+    full_y = get("full_y")
     waves = [transposed_dot(blocks[:, b].reshape(MY, 128), full_y) for b in range(4)]
     rows = jnp.concatenate(waves, axis=0).reshape(MZ, 2, 8, MY)
     rows = jnp.concatenate([rows[:, half].reshape(MZ * 8, MY) for half in range(2)], axis=1)
-    rows = exact_dot(wait("into_z"), rows)
-    rows = rows * wait("gain")
-    rows = close_dot(wait("out_z"), rows)
+    rows = exact_dot(get("into_z"), rows)
+    rows = rows * get("gain")
+    rows = close_dot(get("out_z"), rows)
     rows = jnp.concatenate([rows[:, :MY], rows[:, MY:]], axis=0)
-    rows = close_dot(rows, wait("out_y"))
+    rows = close_dot(rows, get("out_y"))
     for core in range(2):
         sides = []
         for half in range(2):
@@ -295,14 +334,15 @@
                 piece = rows[start : start + 8]
                 total = piece if z == 0 else total + pltpu.roll(piece, z * BORDER, 1)
             sides.append(total)
-        message = jnp.concatenate(sides, axis=0)
-        for peer in range(GX):
-            out[peer * 2 + core] = message
-
-
-def far_kernel(table, spectrum, out, held_x, held_y, sems):
-    held = {"last_x": held_x, "last_y": held_y}
-    wait = TABLES.copies(table, held, sems, {"last_x": lax.axis_index("gx")})
+        rows_out = jnp.concatenate(sides, axis=0)
+        for copy in range(2):
+            message[copy * 2 + core] = rows_out
+    send(message, out, sems)()
+
+
+def far_kernel(table, spectrum, out, for_near, held, sems, more):
+    wait = TABLES.fetch(table, held, ["last_x", "last_y"], sems, {"last_x": lax.axis_index("gx")})
+    wait_near = TABLES.fetch(table, for_near, NEAR, more)
     rows = spectrum[...].reshape(MX, 128)
     field = close_dot(rows.T, wait("last_x"))
     high, low = halves(field)
@@ -319,27 +359,28 @@
             value = (1.0 - abs(t)) * here + abs(t) * (before if t < 0 else after)
             z = block * COARSEN + residue
             out[z] = value
-
-
-def edge_y_kernel(density, z_even, z_odd, even, odd):
-    lower = is_even("core")
-    start = jnp.where(is_even("gy"), CY - HALO, 0)
-    for target, first in ((even, start), (odd, CY - HALO - start)):
-        rows = pl.ds(pl.multiple_of(first, 8), HALO)
-        one, two = z_even[:, rows], z_odd[:, rows]
-        target[0:HALO] = jnp.where(lower, two, one)
-        target[HALO : HALO + CZ] = density[:, rows]
-        target[HALO + CZ : PZ] = jnp.where(lower, one, two)
-
-
-def edge_x_kernel(table, density, z_even, z_odd, y_even, y_odd, waves, even, odd, padded, held, sems):
-    wait = TABLES.copies(table, {"into_y": held}, sems, {})
+    for name in NEAR:
+        wait_near(name)
+
+
+def edge_y_kernel(table, density, z_even, z_odd, even, odd, planes, for_filter, sems):
+    part = {"gain": share(), "out_z": lax.axis_index("yh"), "out_y": lax.axis_index("gy")}
+    wait = TABLES.fetch(table, for_filter, FILTER, sems, part)
     lower = is_even("core")
     one, two = z_even[...], z_odd[...]
-    middle = slice(HALO, HALO + CY)
-    padded[0:HALO, middle] = jnp.where(lower, two, one)
-    padded[HALO : HALO + CZ, middle] = density[...]
-    padded[HALO + CZ : PZ, middle] = jnp.where(lower, one, two)
+    planes[0:HALO] = jnp.where(lower, two, one)
+    planes[HALO : HALO + CZ] = density[...]
+    planes[HALO + CZ : PZ] = jnp.where(lower, one, two)
+    start = jnp.where(is_even("gy"), CY - HALO, 0)
+    even[...] = planes[:, pl.ds(pl.multiple_of(start, 8), HALO)]
+    odd[...] = planes[:, pl.ds(pl.multiple_of(CY - HALO - start, 8), HALO)]
+    for name in FILTER:
+        wait(name)
+
+
+def edge_x_kernel(table, planes, y_even, y_odd, waves, even, odd, padded, held, sems):
+    wait = TABLES.fetch(table, held, ["into_y"], sems)
+    padded[:, HALO : HALO + CY] = planes[...]
     lower = is_even("gy")
     one, two = y_even[...], y_odd[...]
     padded[:, 0:HALO] = jnp.where(lower, two, one)
@@ -362,70 +403,96 @@
     odd[...] = jnp.where(lower, left, right)
 
 
+def sum_planes(gain, load, store):
+    window = [load(z) for z in range(2 * HALO)]
+    for z in range(CZ):
+        window.append(load(z + 2 * HALO))
+        total = gain[0] * window[HALO]
+        for d in range(1, HALO + 1):
+            total = total + gain[d] * (window[HALO - d] + window[HALO + d])
+        store(z, total)
+        window.pop(0)
+
+
 def near_kernel(
-    table, waves, x_even, x_odd, far, out, wave_x, wave_z, held_g, held_ix, held_y, held_ox, sems
+    held, waves, x_even, x_odd, far, out, wave_x, tails, sums, tail_sums, field, sems
 ):
-    held = {"into_x": held_ix, "gains": held_g, "into_y": held_y, "out_x": held_ox}
-    wait = TABLES.copies(table, held, sems, {})
+    get = TABLES.reader(held, NEAR)
     lower = is_even("gx")
     one, two = x_even[...], x_odd[...]
     ends = jnp.concatenate([jnp.where(lower, two, one), jnp.where(lower, one, two)], axis=0)
     high = ends.astype(bf16).astype(f32)
     ends = jnp.concatenate([high, high, ends - high], axis=0)
-    into_x = wait("into_x")[:432].astype(bf16)
-    flat = waves.reshape(PZ * PY, 128)
-    flat_x = wave_x.reshape(PZ * PY, LANES)
+    weights = get("into_x")[:432].astype(bf16)
+    flat, flat_x = waves.reshape(PZ * PY, 128), wave_x.reshape(PZ * PY, 128)
+    tile = lane((8, 128)) // TAIL
+    planes = {}
     for j in range(18):
         part = slice(j * 128, (j + 1) * 128)
         high, low = halves(flat[part])
-        flat_x[part] = dot(jnp.concatenate([high, high, low, ends[:, part].T.astype(bf16)], axis=1), into_x)
-
-    wait("gains")
+        wave = dot(jnp.concatenate([high, high, low, ends[:, part].T.astype(bf16)], axis=1), weights)
+        flat_x[part] = wave[:, :128]
+        for i in range(16):
+            z, t = divmod(16 * j + i, PY // 8)
+            piece = wave[8 * i : 8 * i + 8, 128:]
+            planes[z] = piece if t == 0 else jnp.where(tile == t, piece, planes[z])
+            if t == PY // 8 - 1:
+                tails[z] = planes.pop(z)
+
+    def store_tail(z, value):
+        tail_sums[z] = value
+
+    gains, tail_gains = (TABLES.rows(held, NEAR, name) for name in ("gains", "tail_gains"))
+    sum_planes([tail_gains[d * 8 : d * 8 + 8] for d in range(HALO + 1)], lambda z: tails[z], store_tail)
 
     @pl.loop(0, PY // 8)
     def _(c):
-        for side in range(LANES // 128):
-            gain = [
-                held_g[side, pl.ds(pl.multiple_of(d * PY + c * 8, 8), 8)] for d in range(HALO + 1)
-            ]
-            row, column = pl.ds(pl.multiple_of(c * 8, 8), 8), pl.ds(side * 128, 128)
-            window = [wave_x[z, row, column] for z in range(2 * HALO)]
-            for z in range(CZ):
-                window.append(wave_x[z + 2 * HALO, row, column])
-                total = gain[0] * window[HALO]
-                for d in range(1, HALO + 1):
-                    total = total + gain[d] * (window[HALO - d] + window[HALO + d])
-                wave_z[z, row, column] = total
-                window.pop(0)
-
-    out_y = wait("into_y")[HALO : HALO + CY, : 3 * PY].astype(bf16)
-    out_x = wait("out_x").astype(bf16)
-    high, low = halves(wave_z[...].reshape(CZ * PY, LANES))
-    both = dot(high, jnp.concatenate([out_x[:256], out_x[256:512]], axis=1))
-    rows = both[:, :128] + both[:, 128:] + dot(low, out_x[:256])
+        row = pl.ds(pl.multiple_of(c * 8, 8), 8)
+
+        def store(z, value):
+            sums[z, row] = value
+
+        sum_planes(
+            [gains[pl.ds(pl.multiple_of(d * PY + c * 8, 8), 8)] for d in range(HALO + 1)],
+            lambda z: wave_x[z, row],
+            store,
+        )
+
+    to_y = get("back_y")[:, : 3 * PY].astype(bf16)
+    to_x = get("back_x").astype(bf16)
+    rows = []
+    for z in range(CZ):
+        tail = tail_sums[z]
+        tail = jnp.concatenate([jnp.where(tile == t, tail, 0.0) for t in range(PY // 8)], axis=0)
+        rows.append(jnp.concatenate([sums[z], tail], axis=1))
+    high, low = halves(jnp.concatenate(rows, axis=0))
+    both = dot(high, to_x)
+    rows = both[:, :128] + both[:, 128:] + dot(low, to_x[:, :128])
+    copies = []
     for z in range(0, CZ, 2):
         pair = jnp.concatenate([rows[z * PY : (z + 1) * PY], rows[(z + 1) * PY : (z + 2) * PY]], axis=1)
         high, low = halves(pair)
-        field = dot(out_y, jnp.concatenate([high, high, low], axis=0))
-        out[z] = far[z] + field[:, :128]
-        out[z + 1] = far[z + 1] + field[:, 128:]
-
-
-def call(kernel, outs, arrays=0, tables=(), scratch=(), us=1.0):
-    vmem = pl.BlockSpec(memory_space=pltpu.VMEM)
+        cells = dot(to_y, jnp.concatenate([high, high, low], axis=0))
+        field[z] = far[z] + cells[:, :128]
+        field[z + 1] = far[z + 1] + cells[:, 128:]
+        if z % 8 == 6:
+            part = pl.ds(z - 6, 8)
+            copies.append(pltpu.make_async_copy(field.at[part], out.at[part], sems.at[z // 8]))
+            copies[-1].start()
+    for copy in copies:
+        copy.wait()
+
+
+def call(kernel, outs, arrays=0, table=False, sent=0, scratch=(), us=1.0):
+    vmem, hbm = pl.BlockSpec(memory_space=pltpu.VMEM), pl.BlockSpec(memory_space=pltpu.HBM)
     many = isinstance(outs, list)
-    specs = [vmem] * arrays
-    scratch = list(scratch)
-    if tables:
-        specs = [pl.BlockSpec(memory_space=pltpu.HBM)] + specs
-        scratch += [TABLES.shape(name) for name in tables]
-        scratch.append(pltpu.SemaphoreType.DMA((len(tables),)))
+    specs = [hbm] * table + [vmem] * arrays
     return pl.pallas_call(
         kernel,
         out_shape=[jax.ShapeDtypeStruct(s, f32) for s in outs] if many else jax.ShapeDtypeStruct(outs, f32),
         in_specs=specs,
-        out_specs=[vmem] * len(outs) if many else vmem,
-        scratch_shapes=scratch,
+        out_specs=[hbm] * sent + [vmem] * (len(outs) - sent) if many else hbm if sent else vmem,
+        scratch_shapes=list(scratch),
         compiler_params=pltpu.CompilerParams(vmem_limit_bytes=VMEM_MIB * 1024 * 1024),
         cost_estimate=pl.CostEstimate(flops=int(us * 1e9), bytes_accessed=int(us * 3e6), transcendentals=0),
         name=kernel.__name__,
@@ -441,41 +508,75 @@
 
 
 def body(density):
+    dma, vmem = pltpu.SemaphoreType.DMA, pltpu.VMEM
     table = jnp.asarray(TABLES.array)
     charges, *z_ends = call(
-        charge_kernel, [(SHARE, 16, 128), (HALO, CY, CX), (HALO, CY, CX)], 1, us=1.0
+        charge_kernel,
+        [(SHARE, 16, 128), (HALO, CY, CX), (HALO, CY, CX)],
+        1,
+        sent=1,
+        scratch=[vmem((4, 16, 128), f32), dma((4,))],
     )(density)
     charges = lax.all_to_all(charges, ("gx", "core"), 0, 0, tiled=True)
     z_ends = exchange(*z_ends, ("yh", "core"))
-    spectrum = call(first_kernel, (2 * GY, 2, 8, 128), 1, ["first_x"], us=1.3)(table, charges)
+    spectrum = call(
+        first_kernel,
+        (2 * GY, 2, 8, 128),
+        1,
+        table=True,
+        sent=1,
+        scratch=[vmem((MX, 128), f32), vmem((8, 2, 8, 128), f32), dma, dma((4,))],
+        us=1.3,
+    )(table, charges)
     spectrum = lax.all_to_all(spectrum, ("gy", "yh"), 0, 0, tiled=True)
 
-    y_ends = call(edge_y_kernel, [(PZ, HALO, CX)] * 2, 3, us=10.0)(density, *z_ends)
+    *y_ends, planes, for_filter = call(
+        edge_y_kernel,
+        [(PZ, HALO, CX), (PZ, HALO, CX), (PZ, CY, CX), (TABLES.height(FILTER), 128)],
+        3,
+        table=True,
+        scratch=[dma((len(FILTER),))],
+        us=10.0,
+    )(table, density, *z_ends)
     spectrum, _ = lax.optimization_barrier((spectrum, y_ends))
     y_ends = exchange(*y_ends, "gy")
-    spectrum = call(filter_kernel, (SHARE, KX, 128), 1, ["full_y", "into_z", "gain", "out_z", "out_y"], us=3.0)(
-        table, spectrum
-    )
+    spectrum = call(
+        filter_kernel, (SHARE, KX, 128), 2, sent=1, scratch=[vmem((4, KX, 128), f32), dma((4,))], us=3.0
+    )(for_filter, spectrum)
     y_ends, _ = lax.optimization_barrier((y_ends, spectrum))
     spectrum = lax.all_to_all(spectrum, ("gx", "core"), 0, 0, tiled=True)
     waves, even, odd = call(
         edge_x_kernel,
         [(PZ, PY, CX), (HALO, PZ * PY), (HALO, PZ * PY)],
-        5,
-        ["into_y"],
-        [pltpu.VMEM((PZ, PY, CX), f32)],
+        3,
+        table=True,
+        scratch=[vmem((PZ, PY, CX), f32), vmem(TABLES.shape("into_y"), f32), dma((1,))],
         us=10.0,
-    )(table, density, *z_ends, *y_ends)
+    )(table, planes, *y_ends)
     x_ends = exchange(even, odd, "gx")
-    far = call(far_kernel, (CZ, CY, CX), 1, ["last_x", "last_y"], us=5.0)(table, spectrum)
+    far, for_near = call(
+        far_kernel,
+        [(CZ, CY, CX), (TABLES.height(NEAR), 128)],
+        1,
+        table=True,
+        scratch=[vmem((TABLES.height(["last_x", "last_y"]), 128), f32), dma((2,)), dma((len(NEAR),))],
+        us=5.0,
+    )(table, spectrum)
     return call(
         near_kernel,
         (CZ, CY, CX),
-        4,
-        ["gains", "into_x", "into_y", "out_x"],
-        [pltpu.VMEM((PZ, PY, LANES), f32), pltpu.VMEM((CZ, PY, LANES), f32)],
+        5,
+        sent=1,
+        scratch=[
+            vmem((PZ, PY, 128), f32),
+            vmem((PZ, 8, 128), f32),
+            vmem((CZ, PY, 128), f32),
+            vmem((CZ, 8, 128), f32),
+            vmem((CZ, CY, CX), f32),
+            dma((4,)),
+        ],
         us=0.1,
-    )(table, waves, *x_ends, far)
+    )(for_near, waves, *x_ends, far)
 
 
 def solution(mesh):

time: 71.4 us -> 68.8 us (0.964)
  Pallas kernels: 13.7 us -> 12.4 us
  starting transfers between devices: 52.7 us -> 51.8 us
    pallas_call x6, Pallas kernels: 12.6 us -> 11.3 us  [the longest x1 2.96 us: body(): call(near_kernel, (CZ, CY, CX), 5, sent=1, scratch=[vmem((PZ, PY, 128), f...]
    all_to_all x1, waiting for transfers between devices: 2.39 us -> 1.25 us  [body(): spectrum = lax.all_to_all(spectrum, ('gy', 'yh'), 0, 0, tiled=True)]
    ppermute x3, starting transfers between devices: 8.34 us -> 7.24 us  [exchange(): return (lax.ppermute(even, axis, low_first), odd)]
    ppermute x3, waiting for transfers between devices: 0.47 us -> 1.32 us  [exchange(): odd = lax.ppermute(odd, axis, high_first)]
  transfers between devices with their start and end apart: 9 -> 9, of which waited for: 4 -> 4; matrix products, arithmetic and copies ran while one was open for 0% -> 0% of each run, Pallas kernels for 11% -> 12%
where the time goes in v7:
time: 68.8 us; the launch traced here: 68.2 us
  starting transfers between devices  51.8 us (75%)
  Pallas kernels  12.4 us (18%)
  waiting for transfers between devices  2.76 us (4%)
  local copies, waits for them, and re-layouts  1.05 us (2%)
    ppermute x3, starting transfers between devices, exchange(): odd = lax.ppermute(odd, axis, high_first)  18.3 us
    all_to_all x1, starting transfers between devices, body(): charges = lax.all_to_all(charges, ('gx', 'core'), 0, 0, tiled=True)  11.8 us
    all_to_all x1, starting transfers between devices, body(): spectrum = lax.all_to_all(spectrum, ('gy', 'yh'), 0, 0, tiled=True)  8.93 us
    ppermute x3, starting transfers between devices, exchange(): return (lax.ppermute(even, axis, low_first), odd)  7.24 us
    all_to_all x1, starting transfers between devices, body(): spectrum = lax.all_to_all(spectrum, ('gx', 'core'), 0, 0, tiled=True)  5.41 us
    pallas_call x1, Pallas kernels, body(): call(near_kernel, (CZ, CY, CX), 5, sent=1, scratch=[vmem((PZ, PY, 128), f...  2.96 us
    pallas_call x1, Pallas kernels, body(): call(filter_kernel, (SHARE, KX, 128), 2, sent=1, scratch=[vmem((4, KX, 12...  2.12 us
    pallas_call x1, Pallas kernels, body(): call(first_kernel, (2 * GY, 2, 8, 128), 1, table=True, sent=1, scratch=[v...  2.01 us
  transfers between devices with their start and end apart: 9, of which 4 were waited for; matrix products, arithmetic and copies ran while one was open for 0% of the time, Pallas kernels for 12%

profile of v7, /device:TPU:1, one launch (start us, length us, event | category | flops | bytes accessed | tf_op | source)
XLA Modules:
  0.0 68.2 jit_solution(15085057014921525744)
XLA Ops:
  0.0 0.0 copy-start
  0.0 1.0 %copy-done = f32[32,32,128]{2,1,0:T(8,128)S(1)} copy-done((f32[32,32,128]{2,1,0:T(8,128)S(1)}, f32[32,32,128]{2,1,0:T(8,128)}, u32[]{:S(2)}) %copy-start) | copy-done | bytes 524312
  1.0 1.1 %charge_kernel.1 = (f32[16,16,128]{2,1,0:T(8,128)}, f32[8,32,128]{2,1,0:T(8,128)S(1)}, f32[8,32,128]{2,1,0:T(8,128)S(1)}) custom-call(f32[32,32,128]{2,1,0:T(8,128)S(1)} %copy-done), custom_call_target="tpu_custom_call" | custom-call | flops 1000000000 | bytes 3000000 | tf_op jit(solution)/shard_map/charge_kernel/pallas_call | solution.py:513
  2.2 11.8 %all-to-all-start = ((f32[16,16,128]{2,1,0:T(8,128)}), f32[16,16,128]{2,1,0:T(8,128)S(1)}, u32[]{:S(2)}, u32[]{:S(2)}) async-start(f32[16,16,128]{2,1,0:T(8,128)} %get-tuple-element.23), calls=%async_computation | async-start | bytes 262144 | tf_op jit(solution)/shard_map/all_to_all | solution.py:520
  14.0 2.0 %collective-permute-start = (f32[8,32,128]{2,1,0:T(8,128)S(1)}, f32[8,32,128]{2,1,0:T(8,128)S(1)}, u32[]{:S(2)}, u32[]{:S(2)}) collective-permute-start(f32[8,32,128]{2,1,0:T(8,128)S(1)} %get-tuple-element.20), channel_id=1, source_target_pairs={{0,1},{1,0},{2,3},{3,2},{4,5},{5,4},{6,7},{7,6},{8,9},{9,8},{10,11... | collective-permute-start | bytes 393224 | tf_op jit(solution)/shard_map/ppermute | solution.py:507
  16.0 0.0 copy-start.1
  16.1 7.9 %collective-permute-start.1 = (f32[8,32,128]{2,1,0:T(8,128)S(1)}, f32[8,32,128]{2,1,0:T(8,128)S(1)}, u32[]{:S(2)}, u32[]{:S(2)}) collective-permute-start(f32[8,32,128]{2,1,0:T(8,128)S(1)} %get-tuple-element.21), channel_id=1, source_target_pairs={{0,3},{1,2},{2,1},{3,0},{4,7},{5,6},{6,5},{7,4},{8,11},{9,10},{10,... | collective-permute-start | bytes 393224 | tf_op jit(solution)/shard_map/ppermute | solution.py:506
  23.9 0.0 all-to-all-done.charges
  23.9 2.0 %first_kernel.1 = f32[32,2,8,128]{3,2,1,0:T(8,128)} custom-call(f32[49152,128]{1,0:T(8,128)} %constant.2.clone.table, f32[16,16,128]{2,1,0:T(8,128)S(1)} %all-to-all-done.charges), custom_call_target="tpu_custom_call" | custom-call | flops 1300000000 | bytes 3900000 | tf_op jit(solution)/shard_map/first_kernel/pallas_call | solution.py:522
  26.0 8.9 %all-to-all-start.1 = ((f32[32,2,8,128]{3,2,1,0:T(8,128)}), f32[32,2,8,128]{3,2,1,0:T(8,128)S(1)}, u32[]{:S(2)}, u32[]{:S(2)}) async-start(f32[32,2,8,128]{3,2,1,0:T(8,128)} %first_kernel.1), calls=%async_computation.1 | async-start | bytes 524288 | tf_op jit(solution)/shard_map/all_to_all | solution.py:531
  34.9 0.0 collective-permute-done.z_even
  34.9 0.0 collective-permute-done.1.z_odd
  34.9 0.0 copy-done.1
  34.9 1.2 %edge_y_kernel.1 = (f32[48,8,128]{2,1,0:T(8,128)S(1)}, f32[48,8,128]{2,1,0:T(8,128)S(1)}, f32[48,32,128]{2,1,0:T(8,128)S(1)}, f32[1600,128]{1,0:T(8,128)S(1)}) custom-call(f32[49152,128]{1,0:T(8,128)} %constant.2.clone.table, f32[32,32,128]{2,1,0:T(8,128)S(1)} %copy-done.1, f32[8,32,128]{2,1,0:T(8,128)S(1)} %collective-permute-done.z_even, ...), custom_call_target="tpu_custom_call" | custom-call | flops 10000000000 | bytes 30000000 | tf_op jit(solution)/shard_map/edge_y_kernel/pallas_call | solution.py:533
  36.1 3.1 %collective-permute-start.2 = (f32[48,8,128]{2,1,0:T(8,128)S(1)}, f32[48,8,128]{2,1,0:T(8,128)S(1)}, u32[]{:S(2)}, u32[]{:S(2)}) collective-permute-start(f32[48,8,128]{2,1,0:T(8,128)S(1)} %get-tuple-element.24), channel_id=1, source_target_pairs={{0,4},{4,0},{8,12},{12,8},{16,20},{20,16},{24,28},{28,24},{32,36},... | collective-permute-start | bytes 589832 | tf_op jit(solution)/shard_map/ppermute | solution.py:507
  39.2 6.2 %collective-permute-start.3 = (f32[48,8,128]{2,1,0:T(8,128)S(1)}, f32[48,8,128]{2,1,0:T(8,128)S(1)}, u32[]{:S(2)}, u32[]{:S(2)}) collective-permute-start(f32[48,8,128]{2,1,0:T(8,128)S(1)} %get-tuple-element.25), channel_id=1, source_target_pairs={{0,60},{4,8},{8,4},{12,16},{16,12},{20,24},{24,20},{28,32},{32,28}... | collective-permute-start | bytes 589832 | tf_op jit(solution)/shard_map/ppermute | solution.py:506
  45.4 1.2 %all-to-all-done.1.spectrum = f32[32,2,8,128]{3,2,1,0:T(8,128)S(1)} async-done(((f32[32,2,8,128]{3,2,1,0:T(8,128)}), f32[32,2,8,128]{3,2,1,0:T(8,128)S(1)}, u32[]{:S(2)}, u32[]{:S(2)}) %all-to-all-start.1) | async-done | bytes 262176 | tf_op jit(solution)/shard_map/all_to_all | solution.py:531
  46.7 2.1 %filter_kernel.1 = f32[16,16,128]{2,1,0:T(8,128)} custom-call(f32[1600,128]{1,0:T(8,128)S(1)} %get-tuple-element.22.held, f32[32,2,8,128]{3,2,1,0:T(8,128)S(1)} %all-to-all-done.1.spectrum), custom_call_target="tpu_custom_call" | custom-call | flops 3000000000 | bytes 9000000 | tf_op jit(solution)/shard_map/filter_kernel/pallas_call | solution.py:543
  48.8 5.4 %all-to-all-start.2 = ((f32[16,16,128]{2,1,0:T(8,128)}), f32[16,16,128]{2,1,0:T(8,128)S(1)}, u32[]{:S(2)}, u32[]{:S(2)}) async-start(f32[16,16,128]{2,1,0:T(8,128)} %filter_kernel.1), calls=%async_computation.2 | async-start | bytes 262144 | tf_op jit(solution)/shard_map/all_to_all | solution.py:547
  54.2 0.0 collective-permute-done.2.y_even
  54.2 1.2 %collective-permute-done.3.y_odd = f32[48,8,128]{2,1,0:T(8,128)S(1)} collective-permute-done((f32[48,8,128]{2,1,0:T(8,128)S(1)}, f32[48,8,128]{2,1,0:T(8,128)S(1)}, u32[]{:S(2)}, u32[]{:S(2)}) %collective-permute-start.3) | collective-permute-done | bytes 196640 | tf_op jit(solution)/shard_map/ppermute | solution.py:506
  55.4 1.3 %edge_x_kernel.1 = (f32[48,48,128]{2,1,0:T(8,128)S(1)}, f32[8,2304]{1,0:T(8,128)S(1)}, f32[8,2304]{1,0:T(8,128)S(1)}) custom-call(f32[49152,128]{1,0:T(8,128)} %constant.2.clone.table, f32[48,32,128]{2,1,0:T(8,128)S(1)} %get-tuple-element.28.planes, f32[48,8,128]{2,1,0:T(8,128)S(1)} %collective-permute-done.2.y_even, ...), custom_call_target="tpu_custom_call" | custom-call | flops 10000000000 | bytes 30000000 | tf_op jit(solution)/shard_map/edge_x_kernel/pallas_call | solution.py:548
  56.8 2.1 %collective-permute-start.4 = (f32[8,2304]{1,0:T(8,128)S(1)}, f32[8,2304]{1,0:T(8,128)S(1)}, u32[]{:S(2)}, u32[]{:S(2)}) collective-permute-start(f32[8,2304]{1,0:T(8,128)S(1)} %get-tuple-element.32), channel_id=1, source_target_pairs={{0,64},{64,0},{128,192},{192,128},{256,320},{320,256},{384,448},{4... | collective-permute-start | bytes 221192 | tf_op jit(solution)/shard_map/ppermute | solution.py:507
  58.9 4.3 %collective-permute-start.5 = (f32[8,2304]{1,0:T(8,128)S(1)}, f32[8,2304]{1,0:T(8,128)S(1)}, u32[]{:S(2)}, u32[]{:S(2)}) collective-permute-start(f32[8,2304]{1,0:T(8,128)S(1)} %get-tuple-element.33), channel_id=1, source_target_pairs={{0,448},{64,128},{128,64},{192,256},{256,192},{320,384},{384,320},... | collective-permute-start | bytes 221192 | tf_op jit(solution)/shard_map/ppermute | solution.py:506
  63.2 0.2 all-to-all-done.2.spectrum
  63.4 1.7 %far_kernel.1 = (f32[32,32,128]{2,1,0:T(8,128)S(1)}, f32[2104,128]{1,0:T(8,128)S(1)}) custom-call(f32[49152,128]{1,0:T(8,128)} %constant.2.clone.table, f32[16,16,128]{2,1,0:T(8,128)S(1)} %all-to-all-done.2.spectrum), custom_call_target="tpu_custom_call" | custom-call | flops 5000000000 | bytes 15000000 | tf_op jit(solution)/shard_map/far_kernel/pallas_call | solution.py:557
  65.1 0.0 collective-permute-done.4.x_even
  65.1 0.1 collective-permute-done.5.x_odd
  65.2 3.0 %near_kernel.1 = f32[32,32,128]{2,1,0:T(8,128)} custom-call(f32[2104,128]{1,0:T(8,128)S(1)} %get-tuple-element.27.held, f32[48,48,128]{2,1,0:T(8,128)S(1)} %get-tuple-element.31.waves, f32[8,2304]{1,0:T(8,128)S(1)} %collective-permute-done.4.x_even, f32[8,2304]{1,0:T(8,128)S(1)} %collective-permute-done.5.x_odd, f32[32,32,128]{2,1,0:T(8,128)S(1)} %get-tuple-element.34.far), custom_call_target="tpu_custom_call" | custom-call | flops 100000000 | bytes 300000 | tf_op jit(solution)/shard_map/near_kernel/pallas_call | solution.py:565
Async XLA Ops:
  0.0 1.0 %copy-start = (f32[32,32,128]{2,1,0:T(8,128)S(1)}, f32[32,32,128]{2,1,0:T(8,128)}, u32[]{:S(2)}) copy-start(f32[32,32,128]{2,1,0:T(8,128)} %density.3) | copy-start | bytes 1572868
  2.2 21.8 %all-to-all-start = ((f32[16,16,128]{2,1,0:T(8,128)}), f32[16,16,128]{2,1,0:T(8,128)S(1)}, u32[]{:S(2)}, u32[]{:S(2)}) async-start(f32[16,16,128]{2,1,0:T(8,128)} %get-tuple-element.23), calls=%async_computation | async-start | bytes 262144 | tf_op jit(solution)/shard_map/all_to_all | solution.py:520
  14.0 20.9 %collective-permute-start = (f32[8,32,128]{2,1,0:T(8,128)S(1)}, f32[8,32,128]{2,1,0:T(8,128)S(1)}, u32[]{:S(2)}, u32[]{:S(2)}) collective-permute-start(f32[8,32,128]{2,1,0:T(8,128)S(1)} %get-tuple-element.20), channel_id=1, source_target_pairs={{0,1},{1,0},{2,3},{3,2},{4,5},{5,4},{6,7},{7,6},{8,9},{9,8},{10,11... | collective-permute-start | bytes 393224 | tf_op jit(solution)/shard_map/ppermute | solution.py:507
  16.0 18.9 %copy-start.1 = (f32[32,32,128]{2,1,0:T(8,128)S(1)}, f32[32,32,128]{2,1,0:T(8,128)}, u32[]{:S(2)}) copy-start(f32[32,32,128]{2,1,0:T(8,128)} %density.3) | copy-start | bytes 1572868
  16.1 18.9 %collective-permute-start.1 = (f32[8,32,128]{2,1,0:T(8,128)S(1)}, f32[8,32,128]{2,1,0:T(8,128)S(1)}, u32[]{:S(2)}, u32[]{:S(2)}) collective-permute-start(f32[8,32,128]{2,1,0:T(8,128)S(1)} %get-tuple-element.21), channel_id=1, source_target_pairs={{0,3},{1,2},{2,1},{3,0},{4,7},{5,6},{6,5},{7,4},{8,11},{9,10},{10,... | collective-permute-start | bytes 393224 | tf_op jit(solution)/shard_map/ppermute | solution.py:506
  26.0 20.7 %all-to-all-start.1 = ((f32[32,2,8,128]{3,2,1,0:T(8,128)}), f32[32,2,8,128]{3,2,1,0:T(8,128)S(1)}, u32[]{:S(2)}, u32[]{:S(2)}) async-start(f32[32,2,8,128]{3,2,1,0:T(8,128)} %first_kernel.1), calls=%async_computation.1 | async-start | bytes 524288 | tf_op jit(solution)/shard_map/all_to_all | solution.py:531
  36.1 18.1 %collective-permute-start.2 = (f32[48,8,128]{2,1,0:T(8,128)S(1)}, f32[48,8,128]{2,1,0:T(8,128)S(1)}, u32[]{:S(2)}, u32[]{:S(2)}) collective-permute-start(f32[48,8,128]{2,1,0:T(8,128)S(1)} %get-tuple-element.24), channel_id=1, source_target_pairs={{0,4},{4,0},{8,12},{12,8},{16,20},{20,16},{24,28},{28,24},{32,36},... | collective-permute-start | bytes 589832 | tf_op jit(solution)/shard_map/ppermute | solution.py:507
  39.2 16.2 %collective-permute-start.3 = (f32[48,8,128]{2,1,0:T(8,128)S(1)}, f32[48,8,128]{2,1,0:T(8,128)S(1)}, u32[]{:S(2)}, u32[]{:S(2)}) collective-permute-start(f32[48,8,128]{2,1,0:T(8,128)S(1)} %get-tuple-element.25), channel_id=1, source_target_pairs={{0,60},{4,8},{8,4},{12,16},{16,12},{20,24},{24,20},{28,32},{32,28}... | collective-permute-start | bytes 589832 | tf_op jit(solution)/shard_map/ppermute | solution.py:506
  48.8 14.6 %all-to-all-start.2 = ((f32[16,16,128]{2,1,0:T(8,128)}), f32[16,16,128]{2,1,0:T(8,128)S(1)}, u32[]{:S(2)}, u32[]{:S(2)}) async-start(f32[16,16,128]{2,1,0:T(8,128)} %filter_kernel.1), calls=%async_computation.2 | async-start | bytes 262144 | tf_op jit(solution)/shard_map/all_to_all | solution.py:547
  56.8 8.3 %collective-permute-start.4 = (f32[8,2304]{1,0:T(8,128)S(1)}, f32[8,2304]{1,0:T(8,128)S(1)}, u32[]{:S(2)}, u32[]{:S(2)}) collective-permute-start(f32[8,2304]{1,0:T(8,128)S(1)} %get-tuple-element.32), channel_id=1, source_target_pairs={{0,64},{64,0},{128,192},{192,128},{256,320},{320,256},{384,448},{4... | collective-permute-start | bytes 221192 | tf_op jit(solution)/shard_map/ppermute | solution.py:507
  58.9 6.3 %collective-permute-start.5 = (f32[8,2304]{1,0:T(8,128)S(1)}, f32[8,2304]{1,0:T(8,128)S(1)}, u32[]{:S(2)}, u32[]{:S(2)}) collective-permute-start(f32[8,2304]{1,0:T(8,128)S(1)} %get-tuple-element.33), channel_id=1, source_target_pairs={{0,448},{64,128},{128,64},{192,256},{256,192},{320,384},{384,320},... | collective-permute-start | bytes 221192 | tf_op jit(solution)/shard_map/ppermute | solution.py:506

commit v8 on v7

--- a/solution.py
+++ b/solution.py
@@ -255,7 +255,8 @@
     return wait
 
 
-def charge_kernel(density, out, even, odd, message, sems):
+def charge_kernel(table, density, out, even, odd, first_x, message, sems, more):
+    wait_first = TABLES.fetch(table, first_x, ["first_x"], more, {"first_x": share()})
     parts = []
     for high in range(2):
         planes = []
@@ -278,12 +279,11 @@
     start = jnp.where(is_even("core"), CZ - HALO, 0)
     even[...] = density[pl.ds(start, HALO)]
     odd[...] = density[pl.ds(CZ - HALO - start, HALO)]
+    wait_first("first_x")
     wait()
 
 
-def first_kernel(table, charges, out, held, message, sem, sems):
-    copy = TABLES.copy(table, "first_x", held, sem, share())
-    copy.start()
+def first_kernel(first_x, charges, out, message, sems):
     peers = charges[...].reshape(GX, 32, 128)
     place = lane((32, 128)) // BX
     blocks = []
@@ -299,8 +299,7 @@
             sides.append(total)
         blocks.append(jnp.concatenate(sides, axis=1))
     rows = jnp.concatenate(blocks, axis=0)
-    copy.wait()
-    rows = exact_dot(rows, held[...])
+    rows = exact_dot(rows, first_x[...])
     place = lane((BY, 128)) // KX
     for core in range(2):
         total = None
@@ -510,24 +509,19 @@
 def body(density):
     dma, vmem = pltpu.SemaphoreType.DMA, pltpu.VMEM
     table = jnp.asarray(TABLES.array)
-    charges, *z_ends = call(
+    charges, *z_ends, first_x = call(
         charge_kernel,
-        [(SHARE, 16, 128), (HALO, CY, CX), (HALO, CY, CX)],
+        [(SHARE, 16, 128), (HALO, CY, CX), (HALO, CY, CX), (MX, 128)],
         1,
+        table=True,
         sent=1,
-        scratch=[vmem((4, 16, 128), f32), dma((4,))],
-    )(density)
+        scratch=[vmem((4, 16, 128), f32), dma((4,)), dma((1,))],
+    )(table, density)
     charges = lax.all_to_all(charges, ("gx", "core"), 0, 0, tiled=True)
     z_ends = exchange(*z_ends, ("yh", "core"))
     spectrum = call(
-        first_kernel,
-        (2 * GY, 2, 8, 128),
-        1,
-        table=True,
-        sent=1,
-        scratch=[vmem((MX, 128), f32), vmem((8, 2, 8, 128), f32), dma, dma((4,))],
-        us=1.3,
-    )(table, charges)
+        first_kernel, (2 * GY, 2, 8, 128), 2, sent=1, scratch=[vmem((8, 2, 8, 128), f32), dma((4,))], us=1.3
+    )(first_x, charges)
     spectrum = lax.all_to_all(spectrum, ("gy", "yh"), 0, 0, tiled=True)
 
     *y_ends, planes, for_filter = call(

time: 68.8 us -> 67.8 us (0.985)
  Pallas kernels: 12.4 us -> 11.5 us
    pallas_call x2, Pallas kernels: 3.15 us -> 2.25 us  [the longest x1 1.15 us: body(): call(charge_kernel, [(SHARE, 16, 128), (HALO, CY, CX), (HALO, CY, CX), (M...]
  transfers between devices with their start and end apart: 9 -> 9, of which waited for: 4 -> 4; matrix products, arithmetic and copies ran while one was open for 0% -> 0% of each run, Pallas kernels for 12% -> 11%
where the time goes in v8:
time: 67.8 us; the launch traced here: 67.1 us
  starting transfers between devices  51.6 us (76%)
  Pallas kernels  11.5 us (17%)
  waiting for transfers between devices  2.82 us (4%)
  local copies, waits for them, and re-layouts  1.05 us (2%)
    ppermute x3, starting transfers between devices, exchange(): odd = lax.ppermute(odd, axis, high_first)  18.3 us
    all_to_all x1, starting transfers between devices, body(): charges = lax.all_to_all(charges, ('gx', 'core'), 0, 0, tiled=True)  11.8 us
    all_to_all x1, starting transfers between devices, body(): spectrum = lax.all_to_all(spectrum, ('gy', 'yh'), 0, 0, tiled=True)  9.07 us
    ppermute x3, starting transfers between devices, exchange(): return (lax.ppermute(even, axis, low_first), odd)  7.11 us
    all_to_all x1, starting transfers between devices, body(): spectrum = lax.all_to_all(spectrum, ('gx', 'core'), 0, 0, tiled=True)  5.28 us
    pallas_call x1, Pallas kernels, body(): call(near_kernel, (CZ, CY, CX), 5, sent=1, scratch=[vmem((PZ, PY, 128), f...  2.96 us
    pallas_call x1, Pallas kernels, body(): call(filter_kernel, (SHARE, KX, 128), 2, sent=1, scratch=[vmem((4, KX, 12...  2.12 us
    pallas_call x1, Pallas kernels, body(): call(far_kernel, [(CZ, CY, CX), (TABLES.height(NEAR), 128)], 1, table=Tru...  1.7 us
  transfers between devices with their start and end apart: 9, of which 4 were waited for; matrix products, arithmetic and copies ran while one was open for 0% of the time, Pallas kernels for 11%

profile of v8, /device:TPU:1, one launch (start us, length us, event | category | flops | bytes accessed | tf_op | source)
XLA Modules:
  0.0 67.1 jit_solution(13077439338524247828)
XLA Ops:
  0.0 0.0 copy-start
  0.0 1.0 %copy-done = f32[32,32,128]{2,1,0:T(8,128)S(1)} copy-done((f32[32,32,128]{2,1,0:T(8,128)S(1)}, f32[32,32,128]{2,1,0:T(8,128)}, u32[]{:S(2)}) %copy-start) | copy-done | bytes 524312
  1.0 1.1 %charge_kernel.1 = (f32[16,16,128]{2,1,0:T(8,128)}, f32[8,32,128]{2,1,0:T(8,128)S(1)}, f32[8,32,128]{2,1,0:T(8,128)S(1)}, f32[256,128]{1,0:T(8,128)S(1)}) custom-call(f32[49152,128]{1,0:T(8,128)} %constant.2.clone.table, f32[32,32,128]{2,1,0:T(8,128)S(1)} %copy-done), custom_call_target="tpu_custom_call" | custom-call | flops 1000000000 | bytes 3000000 | tf_op jit(solution)/shard_map/charge_kernel/pallas_call | solution.py:512
  2.2 11.8 %all-to-all-start = ((f32[16,16,128]{2,1,0:T(8,128)}), f32[16,16,128]{2,1,0:T(8,128)S(1)}, u32[]{:S(2)}, u32[]{:S(2)}) async-start(f32[16,16,128]{2,1,0:T(8,128)} %get-tuple-element.25), calls=%async_computation | async-start | bytes 262144 | tf_op jit(solution)/shard_map/all_to_all | solution.py:520
  14.0 2.0 %collective-permute-start = (f32[8,32,128]{2,1,0:T(8,128)S(1)}, f32[8,32,128]{2,1,0:T(8,128)S(1)}, u32[]{:S(2)}, u32[]{:S(2)}) collective-permute-start(f32[8,32,128]{2,1,0:T(8,128)S(1)} %get-tuple-element.21), channel_id=1, source_target_pairs={{0,1},{1,0},{2,3},{3,2},{4,5},{5,4},{6,7},{7,6},{8,9},{9,8},{10,11... | collective-permute-start | bytes 393224 | tf_op jit(solution)/shard_map/ppermute | solution.py:506
  16.1 7.7 %collective-permute-start.1 = (f32[8,32,128]{2,1,0:T(8,128)S(1)}, f32[8,32,128]{2,1,0:T(8,128)S(1)}, u32[]{:S(2)}, u32[]{:S(2)}) collective-permute-start(f32[8,32,128]{2,1,0:T(8,128)S(1)} %get-tuple-element.22), channel_id=1, source_target_pairs={{0,3},{1,2},{2,1},{3,0},{4,7},{5,6},{6,5},{7,4},{8,11},{9,10},{10,... | collective-permute-start | bytes 393224 | tf_op jit(solution)/shard_map/ppermute | solution.py:505
  23.8 0.0 all-to-all-done.charges
  23.8 0.0 copy-start.1
  23.8 1.1 %first_kernel.1 = f32[32,2,8,128]{3,2,1,0:T(8,128)} custom-call(f32[256,128]{1,0:T(8,128)S(1)} %get-tuple-element.24.first_x, f32[16,16,128]{2,1,0:T(8,128)S(1)} %all-to-all-done.charges), custom_call_target="tpu_custom_call" | custom-call | flops 1300000000 | bytes 3900000 | tf_op jit(solution)/shard_map/first_kernel/pallas_call | solution.py:522
  24.9 9.1 %all-to-all-start.1 = ((f32[32,2,8,128]{3,2,1,0:T(8,128)}), f32[32,2,8,128]{3,2,1,0:T(8,128)S(1)}, u32[]{:S(2)}, u32[]{:S(2)}) async-start(f32[32,2,8,128]{3,2,1,0:T(8,128)} %first_kernel.1), calls=%async_computation.1 | async-start | bytes 524288 | tf_op jit(solution)/shard_map/all_to_all | solution.py:525
  34.0 0.0 collective-permute-done.z_even
  34.0 0.0 collective-permute-done.1.z_odd
  34.0 0.0 copy-done.1
  34.0 1.2 %edge_y_kernel.1 = (f32[48,8,128]{2,1,0:T(8,128)S(1)}, f32[48,8,128]{2,1,0:T(8,128)S(1)}, f32[48,32,128]{2,1,0:T(8,128)S(1)}, f32[1600,128]{1,0:T(8,128)S(1)}) custom-call(f32[49152,128]{1,0:T(8,128)} %constant.2.clone.table, f32[32,32,128]{2,1,0:T(8,128)S(1)} %copy-done.1, f32[8,32,128]{2,1,0:T(8,128)S(1)} %collective-permute-done.z_even, ...), custom_call_target="tpu_custom_call" | custom-call | flops 10000000000 | bytes 30000000 | tf_op jit(solution)/shard_map/edge_y_kernel/pallas_call | solution.py:527
  35.2 3.1 %collective-permute-start.2 = (f32[48,8,128]{2,1,0:T(8,128)S(1)}, f32[48,8,128]{2,1,0:T(8,128)S(1)}, u32[]{:S(2)}, u32[]{:S(2)}) collective-permute-start(f32[48,8,128]{2,1,0:T(8,128)S(1)} %get-tuple-element.26), channel_id=1, source_target_pairs={{0,4},{4,0},{8,12},{12,8},{16,20},{20,16},{24,28},{28,24},{32,36},... | collective-permute-start | bytes 589832 | tf_op jit(solution)/shard_map/ppermute | solution.py:506
  38.4 6.2 %collective-permute-start.3 = (f32[48,8,128]{2,1,0:T(8,128)S(1)}, f32[48,8,128]{2,1,0:T(8,128)S(1)}, u32[]{:S(2)}, u32[]{:S(2)}) collective-permute-start(f32[48,8,128]{2,1,0:T(8,128)S(1)} %get-tuple-element.27), channel_id=1, source_target_pairs={{0,60},{4,8},{8,4},{12,16},{16,12},{20,24},{24,20},{28,32},{32,28}... | collective-permute-start | bytes 589832 | tf_op jit(solution)/shard_map/ppermute | solution.py:505
  44.5 1.2 %all-to-all-done.1.spectrum = f32[32,2,8,128]{3,2,1,0:T(8,128)S(1)} async-done(((f32[32,2,8,128]{3,2,1,0:T(8,128)}), f32[32,2,8,128]{3,2,1,0:T(8,128)S(1)}, u32[]{:S(2)}, u32[]{:S(2)}) %all-to-all-start.1) | async-done | bytes 262176 | tf_op jit(solution)/shard_map/all_to_all | solution.py:525
  45.8 2.1 %filter_kernel.1 = f32[16,16,128]{2,1,0:T(8,128)} custom-call(f32[1600,128]{1,0:T(8,128)S(1)} %get-tuple-element.23.held, f32[32,2,8,128]{3,2,1,0:T(8,128)S(1)} %all-to-all-done.1.spectrum), custom_call_target="tpu_custom_call" | custom-call | flops 3000000000 | bytes 9000000 | tf_op jit(solution)/shard_map/filter_kernel/pallas_call | solution.py:537
  47.9 5.3 %all-to-all-start.2 = ((f32[16,16,128]{2,1,0:T(8,128)}), f32[16,16,128]{2,1,0:T(8,128)S(1)}, u32[]{:S(2)}, u32[]{:S(2)}) async-start(f32[16,16,128]{2,1,0:T(8,128)} %filter_kernel.1), calls=%async_computation.2 | async-start | bytes 262144 | tf_op jit(solution)/shard_map/all_to_all | solution.py:541
  53.2 0.0 collective-permute-done.2.y_even
  53.2 1.3 %collective-permute-done.3.y_odd = f32[48,8,128]{2,1,0:T(8,128)S(1)} collective-permute-done((f32[48,8,128]{2,1,0:T(8,128)S(1)}, f32[48,8,128]{2,1,0:T(8,128)S(1)}, u32[]{:S(2)}, u32[]{:S(2)}) %collective-permute-start.3) | collective-permute-done | bytes 196640 | tf_op jit(solution)/shard_map/ppermute | solution.py:505
  54.6 1.3 %edge_x_kernel.1 = (f32[48,48,128]{2,1,0:T(8,128)S(1)}, f32[8,2304]{1,0:T(8,128)S(1)}, f32[8,2304]{1,0:T(8,128)S(1)}) custom-call(f32[49152,128]{1,0:T(8,128)} %constant.2.clone.table, f32[48,32,128]{2,1,0:T(8,128)S(1)} %get-tuple-element.30.planes, f32[48,8,128]{2,1,0:T(8,128)S(1)} %collective-permute-done.2.y_even, ...), custom_call_target="tpu_custom_call" | custom-call | flops 10000000000 | bytes 30000000 | tf_op jit(solution)/shard_map/edge_x_kernel/pallas_call | solution.py:542
  55.9 2.0 %collective-permute-start.4 = (f32[8,2304]{1,0:T(8,128)S(1)}, f32[8,2304]{1,0:T(8,128)S(1)}, u32[]{:S(2)}, u32[]{:S(2)}) collective-permute-start(f32[8,2304]{1,0:T(8,128)S(1)} %get-tuple-element.34), channel_id=1, source_target_pairs={{0,64},{64,0},{128,192},{192,128},{256,320},{320,256},{384,448},{4... | collective-permute-start | bytes 221192 | tf_op jit(solution)/shard_map/ppermute | solution.py:506
  57.9 4.4 %collective-permute-start.5 = (f32[8,2304]{1,0:T(8,128)S(1)}, f32[8,2304]{1,0:T(8,128)S(1)}, u32[]{:S(2)}, u32[]{:S(2)}) collective-permute-start(f32[8,2304]{1,0:T(8,128)S(1)} %get-tuple-element.35), channel_id=1, source_target_pairs={{0,448},{64,128},{128,64},{192,256},{256,192},{320,384},{384,320},... | collective-permute-start | bytes 221192 | tf_op jit(solution)/shard_map/ppermute | solution.py:505
  62.3 0.2 all-to-all-done.2.spectrum
  62.4 1.7 %far_kernel.1 = (f32[32,32,128]{2,1,0:T(8,128)S(1)}, f32[2104,128]{1,0:T(8,128)S(1)}) custom-call(f32[49152,128]{1,0:T(8,128)} %constant.2.clone.table, f32[16,16,128]{2,1,0:T(8,128)S(1)} %all-to-all-done.2.spectrum), custom_call_target="tpu_custom_call" | custom-call | flops 5000000000 | bytes 15000000 | tf_op jit(solution)/shard_map/far_kernel/pallas_call | solution.py:551
  64.1 0.0 collective-permute-done.4.x_even
  64.1 0.1 collective-permute-done.5.x_odd
  64.2 3.0 %near_kernel.1 = f32[32,32,128]{2,1,0:T(8,128)} custom-call(f32[2104,128]{1,0:T(8,128)S(1)} %get-tuple-element.29.held, f32[48,48,128]{2,1,0:T(8,128)S(1)} %get-tuple-element.33.waves, f32[8,2304]{1,0:T(8,128)S(1)} %collective-permute-done.4.x_even, f32[8,2304]{1,0:T(8,128)S(1)} %collective-permute-done.5.x_odd, f32[32,32,128]{2,1,0:T(8,128)S(1)} %get-tuple-element.36.far), custom_call_target="tpu_custom_call" | custom-call | flops 100000000 | bytes 300000 | tf_op jit(solution)/shard_map/near_kernel/pallas_call | solution.py:559
Async XLA Ops:
  0.0 1.0 %copy-start = (f32[32,32,128]{2,1,0:T(8,128)S(1)}, f32[32,32,128]{2,1,0:T(8,128)}, u32[]{:S(2)}) copy-start(f32[32,32,128]{2,1,0:T(8,128)} %density.3) | copy-start | bytes 1572868
  2.2 21.6 %all-to-all-start = ((f32[16,16,128]{2,1,0:T(8,128)}), f32[16,16,128]{2,1,0:T(8,128)S(1)}, u32[]{:S(2)}, u32[]{:S(2)}) async-start(f32[16,16,128]{2,1,0:T(8,128)} %get-tuple-element.25), calls=%async_computation | async-start | bytes 262144 | tf_op jit(solution)/shard_map/all_to_all | solution.py:520
  14.0 20.0 %collective-permute-start = (f32[8,32,128]{2,1,0:T(8,128)S(1)}, f32[8,32,128]{2,1,0:T(8,128)S(1)}, u32[]{:S(2)}, u32[]{:S(2)}) collective-permute-start(f32[8,32,128]{2,1,0:T(8,128)S(1)} %get-tuple-element.21), channel_id=1, source_target_pairs={{0,1},{1,0},{2,3},{3,2},{4,5},{5,4},{6,7},{7,6},{8,9},{9,8},{10,11... | collective-permute-start | bytes 393224 | tf_op jit(solution)/shard_map/ppermute | solution.py:506
  16.1 18.0 %collective-permute-start.1 = (f32[8,32,128]{2,1,0:T(8,128)S(1)}, f32[8,32,128]{2,1,0:T(8,128)S(1)}, u32[]{:S(2)}, u32[]{:S(2)}) collective-permute-start(f32[8,32,128]{2,1,0:T(8,128)S(1)} %get-tuple-element.22), channel_id=1, source_target_pairs={{0,3},{1,2},{2,1},{3,0},{4,7},{5,6},{6,5},{7,4},{8,11},{9,10},{10,... | collective-permute-start | bytes 393224 | tf_op jit(solution)/shard_map/ppermute | solution.py:505
  23.8 10.2 %copy-start.1 = (f32[32,32,128]{2,1,0:T(8,128)S(1)}, f32[32,32,128]{2,1,0:T(8,128)}, u32[]{:S(2)}) copy-start(f32[32,32,128]{2,1,0:T(8,128)} %density.3) | copy-start | bytes 1572868
  24.9 20.9 %all-to-all-start.1 = ((f32[32,2,8,128]{3,2,1,0:T(8,128)}), f32[32,2,8,128]{3,2,1,0:T(8,128)S(1)}, u32[]{:S(2)}, u32[]{:S(2)}) async-start(f32[32,2,8,128]{3,2,1,0:T(8,128)} %first_kernel.1), calls=%async_computation.1 | async-start | bytes 524288 | tf_op jit(solution)/shard_map/all_to_all | solution.py:525
  35.2 18.0 %collective-permute-start.2 = (f32[48,8,128]{2,1,0:T(8,128)S(1)}, f32[48,8,128]{2,1,0:T(8,128)S(1)}, u32[]{:S(2)}, u32[]{:S(2)}) collective-permute-start(f32[48,8,128]{2,1,0:T(8,128)S(1)} %get-tuple-element.26), channel_id=1, source_target_pairs={{0,4},{4,0},{8,12},{12,8},{16,20},{20,16},{24,28},{28,24},{32,36},... | collective-permute-start | bytes 589832 | tf_op jit(solution)/shard_map/ppermute | solution.py:506
  38.4 16.2 %collective-permute-start.3 = (f32[48,8,128]{2,1,0:T(8,128)S(1)}, f32[48,8,128]{2,1,0:T(8,128)S(1)}, u32[]{:S(2)}, u32[]{:S(2)}) collective-permute-start(f32[48,8,128]{2,1,0:T(8,128)S(1)} %get-tuple-element.27), channel_id=1, source_target_pairs={{0,60},{4,8},{8,4},{12,16},{16,12},{20,24},{24,20},{28,32},{32,28}... | collective-permute-start | bytes 589832 | tf_op jit(solution)/shard_map/ppermute | solution.py:505
  47.9 14.5 %all-to-all-start.2 = ((f32[16,16,128]{2,1,0:T(8,128)}), f32[16,16,128]{2,1,0:T(8,128)S(1)}, u32[]{:S(2)}, u32[]{:S(2)}) async-start(f32[16,16,128]{2,1,0:T(8,128)} %filter_kernel.1), calls=%async_computation.2 | async-start | bytes 262144 | tf_op jit(solution)/shard_map/all_to_all | solution.py:541
  55.9 8.2 %collective-permute-start.4 = (f32[8,2304]{1,0:T(8,128)S(1)}, f32[8,2304]{1,0:T(8,128)S(1)}, u32[]{:S(2)}, u32[]{:S(2)}) collective-permute-start(f32[8,2304]{1,0:T(8,128)S(1)} %get-tuple-element.34), channel_id=1, source_target_pairs={{0,64},{64,0},{128,192},{192,128},{256,320},{320,256},{384,448},{4... | collective-permute-start | bytes 221192 | tf_op jit(solution)/shard_map/ppermute | solution.py:506
  57.9 6.3 %collective-permute-start.5 = (f32[8,2304]{1,0:T(8,128)S(1)}, f32[8,2304]{1,0:T(8,128)S(1)}, u32[]{:S(2)}, u32[]{:S(2)}) collective-permute-start(f32[8,2304]{1,0:T(8,128)S(1)} %get-tuple-element.35), channel_id=1, source_target_pairs={{0,448},{64,128},{128,64},{192,256},{256,192},{320,384},{384,320},... | collective-permute-start | bytes 221192 | tf_op jit(solution)/shard_map/ppermute | solution.py:505

commit v9 on v8

--- a/solution.py
+++ b/solution.py
@@ -21,7 +21,6 @@
 BZ, BY, BX = MZ // GZ, MY // GY, MX // GX
 PZ, PY, PX = CZ + 2 * HALO, CY + 2 * HALO, CX + 2 * HALO
 LANES = 256
-OWN_US = 1.0
 BORDER = BY + 2
 SHARE = 2 * GX
 KX = MX // SHARE
@@ -200,6 +199,7 @@
         return wait
 
 
+LAST = ["last_x", "last_y"]
 FILTER = ["full_y", "into_z", "gain", "out_z", "out_y"]
 NEAR = ["gains", "tail_gains", "into_x", "back_y", "back_x"]
 TABLES = Tables()
@@ -312,7 +312,8 @@
     send(message, out, sems)()
 
 
-def filter_kernel(held, spectrum, out, message, sems):
+def filter_kernel(table, held, spectrum, out, for_far, message, sems, sems_far):
+    wait_far = TABLES.fetch(table, for_far, LAST, sems_far, {"last_x": lax.axis_index("gx")})
     blocks = spectrum[...].reshape(GY, 4, BY, 128)
     get = TABLES.reader(held, FILTER)
     full_y = get("full_y")
@@ -336,16 +337,19 @@
         rows_out = jnp.concatenate(sides, axis=0)
         for copy in range(2):
             message[copy * 2 + core] = rows_out
-    send(message, out, sems)()
-
-
-def far_kernel(table, spectrum, out, for_near, held, sems, more):
-    wait = TABLES.fetch(table, held, ["last_x", "last_y"], sems, {"last_x": lax.axis_index("gx")})
+    wait_out = send(message, out, sems)
+    for name in LAST:
+        wait_far(name)
+    wait_out()
+
+
+def far_kernel(table, held, spectrum, out, for_near, more):
+    get = TABLES.reader(held, LAST)
     wait_near = TABLES.fetch(table, for_near, NEAR, more)
     rows = spectrum[...].reshape(MX, 128)
-    field = close_dot(rows.T, wait("last_x"))
+    field = close_dot(rows.T, get("last_x"))
     high, low = halves(field)
-    refine = wait("last_y").astype(bf16)
+    refine = get("last_y").astype(bf16)
     field = dot(refine, high) + dot(refine, low)
 
     def plane(z):
@@ -534,9 +538,15 @@
     )(table, density, *z_ends)
     spectrum, _ = lax.optimization_barrier((spectrum, y_ends))
     y_ends = exchange(*y_ends, "gy")
-    spectrum = call(
-        filter_kernel, (SHARE, KX, 128), 2, sent=1, scratch=[vmem((4, KX, 128), f32), dma((4,))], us=3.0
-    )(for_filter, spectrum)
+    spectrum, for_far = call(
+        filter_kernel,
+        [(SHARE, KX, 128), (TABLES.height(LAST), 128)],
+        2,
+        table=True,
+        sent=1,
+        scratch=[vmem((4, KX, 128), f32), dma((4,)), dma((len(LAST),))],
+        us=3.0,
+    )(table, for_filter, spectrum)
     y_ends, _ = lax.optimization_barrier((y_ends, spectrum))
     spectrum = lax.all_to_all(spectrum, ("gx", "core"), 0, 0, tiled=True)
     waves, even, odd = call(
@@ -551,11 +561,11 @@
     far, for_near = call(
         far_kernel,
         [(CZ, CY, CX), (TABLES.height(NEAR), 128)],
-        1,
+        2,
         table=True,
-        scratch=[vmem((TABLES.height(["last_x", "last_y"]), 128), f32), dma((2,)), dma((len(NEAR),))],
+        scratch=[dma((len(NEAR),))],
         us=5.0,
-    )(table, spectrum)
+    )(table, for_far, spectrum)
     return call(
         near_kernel,
         (CZ, CY, CX),

time: 67.8 us -> 68.2 us (level)
  no operation moved by 1% of the time
where the time goes in v9:
time: 68.2 us; the launch traced here: 67.5 us
  starting transfers between devices  51.9 us (76%)
  Pallas kernels  11.6 us (17%)
  waiting for transfers between devices  2.81 us (4%)
  local copies, waits for them, and re-layouts  1.05 us (2%)
    ppermute x3, starting transfers between devices, exchange(): odd = lax.ppermute(odd, axis, high_first)  18.3 us
    all_to_all x1, starting transfers between devices, body(): charges = lax.all_to_all(charges, ('gx', 'core'), 0, 0, tiled=True)  11.8 us
    all_to_all x1, starting transfers between devices, body(): spectrum = lax.all_to_all(spectrum, ('gy', 'yh'), 0, 0, tiled=True)  9.07 us
    ppermute x3, starting transfers between devices, exchange(): return (lax.ppermute(even, axis, low_first), odd)  7.44 us
    all_to_all x1, starting transfers between devices, body(): spectrum = lax.all_to_all(spectrum, ('gx', 'core'), 0, 0, tiled=True)  5.28 us
    pallas_call x1, Pallas kernels, body(): call(near_kernel, (CZ, CY, CX), 5, sent=1, scratch=[vmem((PZ, PY, 128), f...  2.96 us
    pallas_call x1, Pallas kernels, body(): call(filter_kernel, [(SHARE, KX, 128), (TABLES.height(LAST), 128)], 2, ta...  2.45 us
    ppermute x3, waiting for transfers between devices, exchange(): odd = lax.ppermute(odd, axis, high_first)  1.4 us
  transfers between devices with their start and end apart: 9, of which 4 were waited for; matrix products, arithmetic and copies ran while one was open for 0% of the time, Pallas kernels for 11%

profile of v9, /device:TPU:1, one launch (start us, length us, event | category | flops | bytes accessed | tf_op | source)
XLA Modules:
  0.0 67.5 jit_solution(8883473584595354932)
XLA Ops:
  0.0 0.0 copy-start
  0.0 1.0 %copy-done = f32[32,32,128]{2,1,0:T(8,128)S(1)} copy-done((f32[32,32,128]{2,1,0:T(8,128)S(1)}, f32[32,32,128]{2,1,0:T(8,128)}, u32[]{:S(2)}) %copy-start) | copy-done | bytes 524312
  1.0 1.1 %charge_kernel.1 = (f32[16,16,128]{2,1,0:T(8,128)}, f32[8,32,128]{2,1,0:T(8,128)S(1)}, f32[8,32,128]{2,1,0:T(8,128)S(1)}, f32[256,128]{1,0:T(8,128)S(1)}) custom-call(f32[49152,128]{1,0:T(8,128)} %constant.2.clone.table, f32[32,32,128]{2,1,0:T(8,128)S(1)} %copy-done), custom_call_target="tpu_custom_call" | custom-call | flops 1000000000 | bytes 3000000 | tf_op jit(solution)/shard_map/charge_kernel/pallas_call | solution.py:516
  2.2 11.8 %all-to-all-start = ((f32[16,16,128]{2,1,0:T(8,128)}), f32[16,16,128]{2,1,0:T(8,128)S(1)}, u32[]{:S(2)}, u32[]{:S(2)}) async-start(f32[16,16,128]{2,1,0:T(8,128)} %get-tuple-element.27), calls=%async_computation | async-start | bytes 262144 | tf_op jit(solution)/shard_map/all_to_all | solution.py:524
  14.0 2.0 %collective-permute-start = (f32[8,32,128]{2,1,0:T(8,128)S(1)}, f32[8,32,128]{2,1,0:T(8,128)S(1)}, u32[]{:S(2)}, u32[]{:S(2)}) collective-permute-start(f32[8,32,128]{2,1,0:T(8,128)S(1)} %get-tuple-element.23), channel_id=1, source_target_pairs={{0,1},{1,0},{2,3},{3,2},{4,5},{5,4},{6,7},{7,6},{8,9},{9,8},{10,11... | collective-permute-start | bytes 393224 | tf_op jit(solution)/shard_map/ppermute | solution.py:510
  16.1 7.7 %collective-permute-start.1 = (f32[8,32,128]{2,1,0:T(8,128)S(1)}, f32[8,32,128]{2,1,0:T(8,128)S(1)}, u32[]{:S(2)}, u32[]{:S(2)}) collective-permute-start(f32[8,32,128]{2,1,0:T(8,128)S(1)} %get-tuple-element.24), channel_id=1, source_target_pairs={{0,3},{1,2},{2,1},{3,0},{4,7},{5,6},{6,5},{7,4},{8,11},{9,10},{10,... | collective-permute-start | bytes 393224 | tf_op jit(solution)/shard_map/ppermute | solution.py:509
  23.8 0.0 all-to-all-done.charges
  23.8 0.0 copy-start.1
  23.8 1.1 %first_kernel.1 = f32[32,2,8,128]{3,2,1,0:T(8,128)} custom-call(f32[256,128]{1,0:T(8,128)S(1)} %get-tuple-element.26.first_x, f32[16,16,128]{2,1,0:T(8,128)S(1)} %all-to-all-done.charges), custom_call_target="tpu_custom_call" | custom-call | flops 1300000000 | bytes 3900000 | tf_op jit(solution)/shard_map/first_kernel/pallas_call | solution.py:526
  24.9 9.1 %all-to-all-start.1 = ((f32[32,2,8,128]{3,2,1,0:T(8,128)}), f32[32,2,8,128]{3,2,1,0:T(8,128)S(1)}, u32[]{:S(2)}, u32[]{:S(2)}) async-start(f32[32,2,8,128]{3,2,1,0:T(8,128)} %first_kernel.1), calls=%async_computation.1 | async-start | bytes 524288 | tf_op jit(solution)/shard_map/all_to_all | solution.py:529
  34.0 0.0 collective-permute-done.z_even
  34.0 0.0 collective-permute-done.1.z_odd
  34.0 0.0 copy-done.1
  34.0 1.2 %edge_y_kernel.1 = (f32[48,8,128]{2,1,0:T(8,128)S(1)}, f32[48,8,128]{2,1,0:T(8,128)S(1)}, f32[48,32,128]{2,1,0:T(8,128)S(1)}, f32[1600,128]{1,0:T(8,128)S(1)}) custom-call(f32[49152,128]{1,0:T(8,128)} %constant.2.clone.table, f32[32,32,128]{2,1,0:T(8,128)S(1)} %copy-done.1, f32[8,32,128]{2,1,0:T(8,128)S(1)} %collective-permute-done.z_even, ...), custom_call_target="tpu_custom_call" | custom-call | flops 10000000000 | bytes 30000000 | tf_op jit(solution)/shard_map/edge_y_kernel/pallas_call | solution.py:531
  35.2 3.1 %collective-permute-start.2 = (f32[48,8,128]{2,1,0:T(8,128)S(1)}, f32[48,8,128]{2,1,0:T(8,128)S(1)}, u32[]{:S(2)}, u32[]{:S(2)}) collective-permute-start(f32[48,8,128]{2,1,0:T(8,128)S(1)} %get-tuple-element.28), channel_id=1, source_target_pairs={{0,4},{4,0},{8,12},{12,8},{16,20},{20,16},{24,28},{28,24},{32,36},... | collective-permute-start | bytes 589832 | tf_op jit(solution)/shard_map/ppermute | solution.py:510
  38.4 6.2 %collective-permute-start.3 = (f32[48,8,128]{2,1,0:T(8,128)S(1)}, f32[48,8,128]{2,1,0:T(8,128)S(1)}, u32[]{:S(2)}, u32[]{:S(2)}) collective-permute-start(f32[48,8,128]{2,1,0:T(8,128)S(1)} %get-tuple-element.29), channel_id=1, source_target_pairs={{0,60},{4,8},{8,4},{12,16},{16,12},{20,24},{24,20},{28,32},{32,28}... | collective-permute-start | bytes 589832 | tf_op jit(solution)/shard_map/ppermute | solution.py:509
  44.5 1.2 %all-to-all-done.1.spectrum = f32[32,2,8,128]{3,2,1,0:T(8,128)S(1)} async-done(((f32[32,2,8,128]{3,2,1,0:T(8,128)}), f32[32,2,8,128]{3,2,1,0:T(8,128)S(1)}, u32[]{:S(2)}, u32[]{:S(2)}) %all-to-all-start.1) | async-done | bytes 262176 | tf_op jit(solution)/shard_map/all_to_all | solution.py:529
  45.8 2.5 %filter_kernel.1 = (f32[16,16,128]{2,1,0:T(8,128)}, f32[576,128]{1,0:T(8,128)S(1)}) custom-call(f32[49152,128]{1,0:T(8,128)} %constant.2.clone.table, f32[1600,128]{1,0:T(8,128)S(1)} %get-tuple-element.25.held, f32[32,2,8,128]{3,2,1,0:T(8,128)S(1)} %all-to-all-done.1.spectrum), custom_call_target="tpu_custom_call" | custom-call | flops 3000000000 | bytes 9000000 | tf_op jit(solution)/shard_map/filter_kernel/pallas_call | solution.py:541
  48.2 5.3 %all-to-all-start.2 = ((f32[16,16,128]{2,1,0:T(8,128)}), f32[16,16,128]{2,1,0:T(8,128)S(1)}, u32[]{:S(2)}, u32[]{:S(2)}) async-start(f32[16,16,128]{2,1,0:T(8,128)} %get-tuple-element.32), calls=%async_computation.2 | async-start | bytes 262144 | tf_op jit(solution)/shard_map/all_to_all | solution.py:551
  53.5 0.0 collective-permute-done.2.y_even
  53.5 1.0 %collective-permute-done.3.y_odd = f32[48,8,128]{2,1,0:T(8,128)S(1)} collective-permute-done((f32[48,8,128]{2,1,0:T(8,128)S(1)}, f32[48,8,128]{2,1,0:T(8,128)S(1)}, u32[]{:S(2)}, u32[]{:S(2)}) %collective-permute-start.3) | collective-permute-done | bytes 196640 | tf_op jit(solution)/shard_map/ppermute | solution.py:509
  54.6 1.3 %edge_x_kernel.1 = (f32[48,48,128]{2,1,0:T(8,128)S(1)}, f32[8,2304]{1,0:T(8,128)S(1)}, f32[8,2304]{1,0:T(8,128)S(1)}) custom-call(f32[49152,128]{1,0:T(8,128)} %constant.2.clone.table, f32[48,32,128]{2,1,0:T(8,128)S(1)} %get-tuple-element.34.planes, f32[48,8,128]{2,1,0:T(8,128)S(1)} %collective-permute-done.2.y_even, ...), custom_call_target="tpu_custom_call" | custom-call | flops 10000000000 | bytes 30000000 | tf_op jit(solution)/shard_map/edge_x_kernel/pallas_call | solution.py:552
  55.9 2.3 %collective-permute-start.4 = (f32[8,2304]{1,0:T(8,128)S(1)}, f32[8,2304]{1,0:T(8,128)S(1)}, u32[]{:S(2)}, u32[]{:S(2)}) collective-permute-start(f32[8,2304]{1,0:T(8,128)S(1)} %get-tuple-element.38), channel_id=1, source_target_pairs={{0,64},{64,0},{128,192},{192,128},{256,320},{320,256},{384,448},{4... | collective-permute-start | bytes 221192 | tf_op jit(solution)/shard_map/ppermute | solution.py:510
  58.2 4.4 %collective-permute-start.5 = (f32[8,2304]{1,0:T(8,128)S(1)}, f32[8,2304]{1,0:T(8,128)S(1)}, u32[]{:S(2)}, u32[]{:S(2)}) collective-permute-start(f32[8,2304]{1,0:T(8,128)S(1)} %get-tuple-element.39), channel_id=1, source_target_pairs={{0,448},{64,128},{128,64},{192,256},{256,192},{320,384},{384,320},... | collective-permute-start | bytes 221192 | tf_op jit(solution)/shard_map/ppermute | solution.py:509
  62.6 0.2 all-to-all-done.2.spectrum
  62.7 1.4 %far_kernel.1 = (f32[32,32,128]{2,1,0:T(8,128)S(1)}, f32[2104,128]{1,0:T(8,128)S(1)}) custom-call(f32[49152,128]{1,0:T(8,128)} %constant.2.clone.table, f32[576,128]{1,0:T(8,128)S(1)} %get-tuple-element.31.held, f32[16,16,128]{2,1,0:T(8,128)S(1)} %all-to-all-done.2.spectrum), custom_call_target="tpu_custom_call" | custom-call | flops 5000000000 | bytes 15000000 | tf_op jit(solution)/shard_map/far_kernel/pallas_call | solution.py:561
  64.1 0.0 collective-permute-done.4.x_even
  64.1 0.4 collective-permute-done.5.x_odd
  64.5 3.0 %near_kernel.1 = f32[32,32,128]{2,1,0:T(8,128)} custom-call(f32[2104,128]{1,0:T(8,128)S(1)} %get-tuple-element.33.held, f32[48,48,128]{2,1,0:T(8,128)S(1)} %get-tuple-element.37.waves, f32[8,2304]{1,0:T(8,128)S(1)} %collective-permute-done.4.x_even, f32[8,2304]{1,0:T(8,128)S(1)} %collective-permute-done.5.x_odd, f32[32,32,128]{2,1,0:T(8,128)S(1)} %get-tuple-element.40.far), custom_call_target="tpu_custom_call" | custom-call | flops 100000000 | bytes 300000 | tf_op jit(solution)/shard_map/near_kernel/pallas_call | solution.py:569
Async XLA Ops:
  0.0 1.0 %copy-start = (f32[32,32,128]{2,1,0:T(8,128)S(1)}, f32[32,32,128]{2,1,0:T(8,128)}, u32[]{:S(2)}) copy-start(f32[32,32,128]{2,1,0:T(8,128)} %density.3) | copy-start | bytes 1572868
  2.2 21.6 %all-to-all-start = ((f32[16,16,128]{2,1,0:T(8,128)}), f32[16,16,128]{2,1,0:T(8,128)S(1)}, u32[]{:S(2)}, u32[]{:S(2)}) async-start(f32[16,16,128]{2,1,0:T(8,128)} %get-tuple-element.27), calls=%async_computation | async-start | bytes 262144 | tf_op jit(solution)/shard_map/all_to_all | solution.py:524
  14.0 20.0 %collective-permute-start = (f32[8,32,128]{2,1,0:T(8,128)S(1)}, f32[8,32,128]{2,1,0:T(8,128)S(1)}, u32[]{:S(2)}, u32[]{:S(2)}) collective-permute-start(f32[8,32,128]{2,1,0:T(8,128)S(1)} %get-tuple-element.23), channel_id=1, source_target_pairs={{0,1},{1,0},{2,3},{3,2},{4,5},{5,4},{6,7},{7,6},{8,9},{9,8},{10,11... | collective-permute-start | bytes 393224 | tf_op jit(solution)/shard_map/ppermute | solution.py:510
  16.1 18.0 %collective-permute-start.1 = (f32[8,32,128]{2,1,0:T(8,128)S(1)}, f32[8,32,128]{2,1,0:T(8,128)S(1)}, u32[]{:S(2)}, u32[]{:S(2)}) collective-permute-start(f32[8,32,128]{2,1,0:T(8,128)S(1)} %get-tuple-element.24), channel_id=1, source_target_pairs={{0,3},{1,2},{2,1},{3,0},{4,7},{5,6},{6,5},{7,4},{8,11},{9,10},{10,... | collective-permute-start | bytes 393224 | tf_op jit(solution)/shard_map/ppermute | solution.py:509
  23.8 10.2 %copy-start.1 = (f32[32,32,128]{2,1,0:T(8,128)S(1)}, f32[32,32,128]{2,1,0:T(8,128)}, u32[]{:S(2)}) copy-start(f32[32,32,128]{2,1,0:T(8,128)} %density.3) | copy-start | bytes 1572868
  24.9 20.9 %all-to-all-start.1 = ((f32[32,2,8,128]{3,2,1,0:T(8,128)}), f32[32,2,8,128]{3,2,1,0:T(8,128)S(1)}, u32[]{:S(2)}, u32[]{:S(2)}) async-start(f32[32,2,8,128]{3,2,1,0:T(8,128)} %first_kernel.1), calls=%async_computation.1 | async-start | bytes 524288 | tf_op jit(solution)/shard_map/all_to_all | solution.py:529
  35.2 18.3 %collective-permute-start.2 = (f32[48,8,128]{2,1,0:T(8,128)S(1)}, f32[48,8,128]{2,1,0:T(8,128)S(1)}, u32[]{:S(2)}, u32[]{:S(2)}) collective-permute-start(f32[48,8,128]{2,1,0:T(8,128)S(1)} %get-tuple-element.28), channel_id=1, source_target_pairs={{0,4},{4,0},{8,12},{12,8},{16,20},{20,16},{24,28},{28,24},{32,36},... | collective-permute-start | bytes 589832 | tf_op jit(solution)/shard_map/ppermute | solution.py:510
  38.4 16.2 %collective-permute-start.3 = (f32[48,8,128]{2,1,0:T(8,128)S(1)}, f32[48,8,128]{2,1,0:T(8,128)S(1)}, u32[]{:S(2)}, u32[]{:S(2)}) collective-permute-start(f32[48,8,128]{2,1,0:T(8,128)S(1)} %get-tuple-element.29), channel_id=1, source_target_pairs={{0,60},{4,8},{8,4},{12,16},{16,12},{20,24},{24,20},{28,32},{32,28}... | collective-permute-start | bytes 589832 | tf_op jit(solution)/shard_map/ppermute | solution.py:509
  48.2 14.5 %all-to-all-start.2 = ((f32[16,16,128]{2,1,0:T(8,128)}), f32[16,16,128]{2,1,0:T(8,128)S(1)}, u32[]{:S(2)}, u32[]{:S(2)}) async-start(f32[16,16,128]{2,1,0:T(8,128)} %get-tuple-element.32), calls=%async_computation.2 | async-start | bytes 262144 | tf_op jit(solution)/shard_map/all_to_all | solution.py:551
  55.9 8.2 %collective-permute-start.4 = (f32[8,2304]{1,0:T(8,128)S(1)}, f32[8,2304]{1,0:T(8,128)S(1)}, u32[]{:S(2)}, u32[]{:S(2)}) collective-permute-start(f32[8,2304]{1,0:T(8,128)S(1)} %get-tuple-element.38), channel_id=1, source_target_pairs={{0,64},{64,0},{128,192},{192,128},{256,320},{320,256},{384,448},{4... | collective-permute-start | bytes 221192 | tf_op jit(solution)/shard_map/ppermute | solution.py:510
  58.2 6.3 %collective-permute-start.5 = (f32[8,2304]{1,0:T(8,128)S(1)}, f32[8,2304]{1,0:T(8,128)S(1)}, u32[]{:S(2)}, u32[]{:S(2)}) collective-permute-start(f32[8,2304]{1,0:T(8,128)S(1)} %get-tuple-element.39), channel_id=1, source_target_pairs={{0,448},{64,128},{128,64},{192,256},{256,192},{320,384},{384,320},... | collective-permute-start | bytes 221192 | tf_op jit(solution)/shard_map/ppermute | solution.py:509
